TPU v7x, 512 devices: a whole 4x4x16 slice. The times are simulated.
512 devices in a mesh: sec: 32 (over y, x, core), cross: 16 (over z).
Axes of the slice: x: 4, y: 4, z: 16, core: 2. Of those that a mesh axis runs over, the one named last changes fastest.
Arguments:
- state: float32 [5, 1024, 4, 4096], P(None, 'sec', None, 'cross'), may hold values from -1.1 to 5, as said below
- time_step: float32 [1024, 4, 4096], P('sec', None, 'cross'), may hold values from 0.001 to 0.01
- to_char: float32 [5, 5], replicated, may hold values from -2.5 to 2.5
- to_cons: float32 [5, 5], replicated, may hold values from -2.5 to 2.5
- lower_bands: float32 [3, 3, 1024], P(None, None, 'sec'), may hold values from -1.9 to 1.25, as said below
- upper_bands: float32 [3, 2, 1024], P(None, None, 'sec'), may hold values from -1.5 to 0.5, as said below
Outputs:
- update: float32 [5, 1024, 4, 4096], P(None, 'sec', None, 'cross')
Inputs may be any that keep to these rules, and one draw needn't show every extreme that they name: `state`: density lies in 0.7 to 1.3, velocities within 0.8 in magnitude and pressure in 0.6 to 1.4; the energy follows from an ideal gas with ratio of heats 1.4. `lower_bands`: each lower factor has diagonal 0.8 to 1.25 and equals the diagonal times (1 - a S)(1 - b S) for a shift S, with 0 < a < 1 and 0.1 <= b <= 0.5 per cell. `upper_bands`: each upper factor equals (1 - a S')(1 - b S') for the backward shift S', with 0 < a < 1 and 0.1 <= b <= 0.5 per cell.
All inputs are finite; a program needn't handle non-finite values.
Results may differ from a plain program's by a relative error of at most 0.0003.
Values sent between devices are 32-bit elements; how exact they have to be, the bound alone decides.
No kernel may reach another device: no remote copies, remote signals or barrier semaphores. Data moves between devices by JAX's collectives and lax.ppermute only.
A program may use at most 64 MiB of HBM per device.

v0:
```python
import jax
import jax.numpy as jnp
from jax import lax
from jax.sharding import PartitionSpec as P

DISSIPATION = 0.0625
UPPER_LIMIT = lax.Precision.HIGHEST


def entering(part, axis, combine, identity, reverse):
    count = lax.axis_size(axis)
    place = lax.axis_index(axis)
    ahead = count - 1 - place if reverse else place
    gathered = jax.tree.map(lambda a: lax.all_gather(a, axis), part)
    state = jax.tree.map(lambda a, e: jnp.zeros_like(a) + jnp.asarray(e, a.dtype), part, identity)

    def one(step, state):
        source = count - 1 - step if reverse else step
        return combine(
            state, jax.tree.map(lambda a: lax.dynamic_index_in_dim(a, source, 0, False), gathered)
        )

    return lax.fori_loop(0, ahead, one, state)


def extended(array, sides, width):
    for axis, dim in sides:
        count, length = (lax.axis_size(axis), array.shape[dim])
        up = [(i, (i + 1) % count) for i in range(count - 1)]
        down = [(j, i) for i, j in up]
        last = lax.slice_in_dim(array, length - width, length, axis=dim)
        initial = lax.slice_in_dim(array, 0, width, axis=dim)
        before = lax.ppermute(last, axis, up)
        after = lax.ppermute(initial, axis, down)
        array = jnp.concatenate([before, array, after], axis=dim)
    return array


def euler_flux(state, direction_axis):
    density = state[0]
    velocity = state[1 + direction_axis] / density
    kinetic = 0.5 * (state[1] * state[1] + state[2] * state[2] + state[3] * state[3]) / density
    pressure = 0.4 * (state[4] - kinetic)
    parts = [
        state[1 + direction_axis],
        state[1] * velocity,
        state[2] * velocity,
        state[3] * velocity,
        (state[4] + pressure) * velocity,
    ]
    parts[1 + direction_axis] = parts[1 + direction_axis] + pressure
    return jnp.stack(parts)


def by_variable(table):
    return jnp.stack([table[0], table[0], table[0], table[1], table[2]])


def lower_inverse(band_diag, band_one, band_two):
    length = band_diag.shape[1]
    square = jnp.eye(length, dtype=jnp.float32)

    def lower_turn(carry, items):
        prior_one, prior_two = carry
        unit_row, diag_now, one_now, two_now = items
        row = (
            unit_row[None] - one_now[:, None] * prior_one - two_now[:, None] * prior_two
        ) / diag_now[:, None]
        return ((row, prior_one), row)

    empty = jnp.zeros((3, length), jnp.float32)
    _, rows = lax.scan(lower_turn, (empty, empty), (square, band_diag.T, band_one.T, band_two.T))
    return rows.transpose(1, 0, 2)


def upper_inverse(upper_one, upper_two):
    length = upper_one.shape[1]
    square = jnp.eye(length, dtype=jnp.float32)

    def upper_turn(carry, items):
        next_one, next_two = carry
        unit_row, one_now, two_now = items
        row = unit_row[None] - one_now[:, None] * next_one - two_now[:, None] * next_two
        return ((row, next_one), row)

    empty = jnp.zeros((3, length), jnp.float32)
    _, rows = lax.scan(upper_turn, (empty, empty), (square, upper_one.T, upper_two.T), reverse=True)
    return rows.transpose(1, 0, 2)


def compose(preceding, later):
    leading_map, leading_shift = preceding
    trailing_map, trailing_shift = later
    merged_map = jnp.einsum("igd,idq->igq", trailing_map, leading_map, precision=UPPER_LIMIT)
    merged_shift = (
        jnp.einsum("igd,idq->igq", trailing_map, leading_shift, precision=UPPER_LIMIT)
        + trailing_shift
    )
    return (merged_map, merged_shift)


def identity_of(shifts):
    return (jnp.broadcast_to(jnp.eye(2, dtype=jnp.float32), (5, 2, 2)), jnp.zeros_like(shifts))


def apply_pair(matrix, values):
    return jnp.einsum("vik,vkc->vic", matrix, values, precision=UPPER_LIMIT)


def resolve(couple, base, back_couple, upper_sel):
    length = base.shape[1]
    maps = couple[:, length - 2 :, :]
    shifts = base[:, length - 2 :, :]
    incoming = entering((maps, shifts), "sec", compose, identity_of(shifts), False)[1]
    forward = base + apply_pair(couple, incoming)
    back_base = apply_pair(upper_sel, forward)
    back_shifts = back_base[:, :2, :]
    arriving = entering(
        (back_couple[:, :2, :], back_shifts), "sec", compose, identity_of(back_shifts), True
    )[1]
    return back_base + apply_pair(back_couple, arriving)


def on_device(state, time_step, to_char, to_cons, lower_bands, upper_bands):
    length = state.shape[1]
    numerical_transport_row = euler_flux(state, 0)
    line_pad = extended(jnp.concatenate([numerical_transport_row, state], axis=0), (("sec", 1),), 2)
    flux_pad = line_pad[:5, 1:-1]
    diff_line = 0.5 * (flux_pad[:, 2:] - flux_pad[:, :-2])
    state_pad = line_pad[5:]
    fourth = (
        state_pad[:, 4:]
        - 4.0 * state_pad[:, 3:-1]
        + 6.0 * state_pad[:, 2:-2]
        - 4.0 * state_pad[:, 1:-3]
        + state_pad[:, :-4]
    )
    flux_side = euler_flux(state, 1)
    side_pad = extended(flux_side, (("cross", 3),), 1)
    diff_side = 0.5 * (side_pad[..., 2:] - side_pad[..., :-2])
    flux_third = euler_flux(state, 2)
    diff_third = 0.5 * (jnp.roll(flux_third, -1, axis=2) - jnp.roll(flux_third, 1, axis=2))
    residual = -(diff_line + diff_side + diff_third) - DISSIPATION * fourth
    right = time_step[None] * residual
    char = jnp.einsum("uv,vlzy->ulzy", to_char, right, precision=UPPER_LIMIT)
    values = char.reshape(5, length, -1)
    band_two = lower_bands[:, 0]
    band_one = lower_bands[:, 1]
    band_diag = lower_bands[:, 2]
    lower_inv = lower_inverse(band_diag, band_one, band_two)
    first_col = -lower_inv[:, :, 0] * band_two[:, 0:1]
    second_col = -lower_inv[:, :, 0] * band_one[:, 0:1] - lower_inv[:, :, 1] * band_two[:, 1:2]
    couple = by_variable(jnp.stack([first_col, second_col], axis=-1))
    base = jnp.einsum("vij,vjc->vic", by_variable(lower_inv), values, precision=UPPER_LIMIT)
    upper_one = upper_bands[:, 0]
    upper_two = upper_bands[:, 1]
    upper_inv = upper_inverse(upper_one, upper_two)
    near_col = (
        -upper_inv[:, :, length - 2] * upper_two[:, length - 2 : length - 1]
        - upper_inv[:, :, length - 1] * upper_one[:, length - 1 : length]
    )
    far_col = -upper_inv[:, :, length - 1] * upper_two[:, length - 1 : length]
    back_couple = by_variable(jnp.stack([near_col, far_col], axis=-1))
    upper_sel = by_variable(upper_inv)
    backward = resolve(couple, base, back_couple, upper_sel)
    result = jnp.einsum("uv,vic->uic", to_cons, backward, precision=UPPER_LIMIT)
    return result.reshape(state.shape)


def solution(mesh):
    in_specs = (
        P(None, "sec", None, "cross"),
        P("sec", None, "cross"),
        P(),
        P(),
        P(None, None, "sec"),
        P(None, None, "sec"),
    )
    out_specs = P(None, "sec", None, "cross")
    return jax.shard_map(
        on_device, mesh=mesh, in_specs=in_specs, out_specs=out_specs, check_vma=False
    )
```

profile of v0, /device:TPU:1, one launch (start us, length us, event | category | flops | bytes accessed | tf_op | source)
XLA Modules:
  0.0 267.9 jit_solution(3283019490305282089)
XLA Ops:
  7.5 1.1 multiply_dynamic-update-slice_fusion.5
  10.2 8.8 %collective-permute-start = (f32[10,2,4,256]{3,2,1,0:T(4,128)}, f32[10,2,4,256]{3,2,1,0:T(4,128)}, u32[]{:S(2)}, u32[]{:S(2)}) collective-permute-start(f32[10,2,4,256]{3,2,1,0:T(4,128)} %get-tuple-element.543), channel_id=1, source_target_pairs={{16,0},{32,16},{48,32},{64,48},{80,64},{96,80},{112,96},{128,112},... | collective-permute-start | bytes 245768 | tf_op jit(solution)/shard_map/ppermute | solution.py:34
  19.0 1.9 collective-permute-start.1
  20.9 1.1 fusion.49
  22.0 1.3 collective-permute-start.2
  23.3 4.7 %collective-permute-start.3 = (f32[5,32,4,1]{3,2,1,0:T(4,128)}, f32[5,32,4,1]{3,2,1,0:T(4,128)}, u32[]{:S(2)}, u32[]{:S(2)}) collective-permute-start(f32[5,32,4,1]{3,2,1,0:T(4,128)} %get-tuple-element.550), channel_id=1, source_target_pairs={{0,1},{1,2},{2,3},{3,4},{4,5},{5,6},{6,7},{7,8},{8,9},{9,10},{10,1... | collective-permute-start | bytes 7688 | tf_op jit(solution)/shard_map/ppermute | solution.py:33
  30.0 25.6 %while.63 = (s32[]{:T(128)}, f32[3,32]{1,0:T(4,128)S(1)}, f32[3,32]{1,0:T(4,128)S(1)}, f32[32,3,32]{2,1,0:T(4,128)S(1)}, f32[32,32]{1,0:T(8,128)}, /*index=5*/f3...) while((s32[]{:T(128)}, f32[3,32]{1,0:T(4,128)S(1)}, ...), condition=%wide.region_3.4_spmd.clone, body=%wide.region_2.3_spmd.clone.sunk | while | flops 579 | bytes 12743 | solution.py:72
  56.7 4.6 %fusion.27 = f32[5,32,4,256]{3,2,1,0:T(4,128)S(1)} fusion(f32[10,32,4,256]{3,2,1,0:T(4,128)} %copy-done.2, f32[10,2,4,256]{3,2,1,0:T(4,128)} %collective-permute-done.1, f32[5,32,4,256]{3,2,1,0:T(4,128)S(1)} %copy-done.1, f32[10,2,4,256]{3,2,1,0:T(4,128)} %collective-permute-done, f32[5,32,3,256]{3,2,1,0:T(4,128)S(1)} %get-tuple-element.553, ...), kind=kLoop, calls=%fused_computation.61 | loop fusion | flops 4423680 | bytes 4887552 | tf_op jit(solution)/shard_map/mul | solution.py:144
  61.3 1.4 convolution_bitcast_fusion.1
  64.8 24.9 %while.62 = (s32[]{:T(128)}, f32[3,32]{1,0:T(4,128)S(1)}, f32[3,32]{1,0:T(4,128)S(1)}, f32[32,3,32]{2,1,0:T(4,128)S(1)}, f32[32,32]{1,0:T(8,128)}, /*index=5*/f3...) while((s32[]{:T(128)}, f32[3,32]{1,0:T(4,128)S(1)}, ...), condition=%wide.region_1.2_spmd.clone, body=%wide.region_0.1_spmd.clone.sunk | while | flops 484 | bytes 12215 | solution.py:87
  90.3 23.2 %all-gather = f32[160,2,2]{2,1,0:T(2,128)S(1)} all-gather(f32[5,2,2]{2,1,0:T(2,128)S(1)} %copy.85), channel_id=2, replica_groups=mesh['sec'=32,'cross'=16] {'sec'}, dimensions={0}, use_global_device_ids=true | all-gather | bytes 2640 | tf_op jit(solution)/shard_map/all_gather | solution.py:14
  114.0 10.4 %all-gather.7.cloned.1.call-done = f32[160,2,1024]{2,1,0:T(2,128)} async-done(((f32[5,2,1024]{2,1,0:T(2,128)}), f32[160,2,1024]{2,1,0:T(2,128)}) %all-gather.7.cloned.1.call-update) | async-done | bytes 1310736 | tf_op jit(solution)/shard_map/all_gather | solution.py:14
  124.5 1.2 while.60
  124.6 1.1 convolution_add_fusion.6
  128.5 58.1 %all-gather.2 = f32[160,2,2]{2,1,0:T(2,128)S(1)} all-gather(f32[5,2,2]{2,1,0:T(2,128)S(1)} %copy.86), channel_id=4, replica_groups=mesh['sec'=32,'cross'=16] {'sec'}, dimensions={0}, use_global_device_ids=true | all-gather | bytes 2640 | tf_op jit(solution)/shard_map/all_gather | solution.py:14
  187.1 33.9 %all-gather.9.cloned.1.call-done = f32[160,2,1024]{2,1,0:T(2,128)} async-done(((f32[5,2,1024]{2,1,0:T(2,128)}), f32[160,2,1024]{2,1,0:T(2,128)}) %all-gather.9.cloned.1.call-update) | async-done | bytes 1310736 | tf_op jit(solution)/shard_map/all_gather | solution.py:14
  221.1 36.5 %while.61 = (s32[]{:T(128)}, f32[5,2,1024]{2,1,0:T(2,128)S(1)}, s32[]{:T(128)}, f32[32,5,2,2]{1,3,2,0:T(2,128)S(1)}, f32[32,5,2,1024]{3,2,1,0:T(2,128)}, /*index=5*/s32[]{:T(128)}, s32[]{:T(128)}, s32[]{:T(128)}, s32[]{:T(128)}) while((s32[]{:T(128)}, f32[5,2,1024]{2,1,0:T(2,128)S(1)}, s32[]{:T(128)}, f32[32,5,2,2]{1,3,2,0:T(2,128)S(1)}, ...), condition=%wide.region_7.8_spmd, body=%wide.region_6.7_spmd.sunk | while | flops 256006 | bytes 205347 | solution.py:23
  221.4 1.1 convolution_add_fusion.7
  222.6 1.1 convolution_add_fusion.7
  223.8 1.1 convolution_add_fusion.7
  225.1 1.1 convolution_add_fusion.7
  226.3 1.1 convolution_add_fusion.7
  227.5 1.1 convolution_add_fusion.7
  228.7 1.1 convolution_add_fusion.7
  229.9 1.1 convolution_add_fusion.7
  231.1 1.1 convolution_add_fusion.7
  232.3 1.1 convolution_add_fusion.7
  233.5 1.1 convolution_add_fusion.7
  234.7 1.1 convolution_add_fusion.7
  235.9 1.1 convolution_add_fusion.7
  237.1 1.1 convolution_add_fusion.7
  238.4 1.1 convolution_add_fusion.7
  239.6 1.1 convolution_add_fusion.7
  240.8 1.1 convolution_add_fusion.7
  242.0 1.1 convolution_add_fusion.7
  243.2 1.1 convolution_add_fusion.7
  244.4 1.1 convolution_add_fusion.7
  245.6 1.1 convolution_add_fusion.7
  246.8 1.1 convolution_add_fusion.7
  248.0 1.1 convolution_add_fusion.7
  249.2 1.1 convolution_add_fusion.7
  250.4 1.1 convolution_add_fusion.7
  251.7 1.1 convolution_add_fusion.7
  252.9 1.1 convolution_add_fusion.7
  254.1 1.1 convolution_add_fusion.7
  255.3 1.1 convolution_add_fusion.7
  256.5 1.1 convolution_add_fusion.7
  258.3 1.4 convolution_bitcast_fusion
  (399 shorter events, 67.6 us)
Async XLA Ops:
  6.5 54.8 %copy-start = (f32[5,5]{1,0:T(8,128)S(1)}, f32[5,5]{1,0:T(8,128)}, u32[]{:S(2)}) copy-start(f32[5,5]{1,0:T(8,128)} %param.16) | copy-start | bytes 304
  6.5 2.1 copy-start.1
  6.5 117.9 %all-gather.7.cloned.1.call-start = ((), (), s32[]{:S(2)}) async-start(), calls=%async_computation | async-start | bytes 1351680 | tf_op jit(solution)/shard_map/all_gather | solution.py:14
  9.5 18.5 %copy-start.2 = (f32[10,32,4,256]{3,2,1,0:T(4,128)}, f32[10,32,4,256]{3,2,1,0:T(4,128)S(1)}, u32[]{:S(2)}) copy-start(f32[10,32,4,256]{3,2,1,0:T(4,128)S(1)} %constant_dynamic-update-slice_fusion) | copy-start | bytes 3932164
  10.2 46.5 %collective-permute-start = (f32[10,2,4,256]{3,2,1,0:T(4,128)}, f32[10,2,4,256]{3,2,1,0:T(4,128)}, u32[]{:S(2)}, u32[]{:S(2)}) collective-permute-start(f32[10,2,4,256]{3,2,1,0:T(4,128)} %get-tuple-element.543), channel_id=1, source_target_pairs={{16,0},{32,16},{48,32},{64,48},{80,64},{96,80},{112,96},{128,112},... | collective-permute-start | bytes 245768 | tf_op jit(solution)/shard_map/ppermute | solution.py:34
  19.0 37.7 %collective-permute-start.1 = (f32[10,2,4,256]{3,2,1,0:T(4,128)}, f32[10,2,4,256]{3,2,1,0:T(4,128)}, u32[]{:S(2)}, u32[]{:S(2)}) collective-permute-start(f32[10,2,4,256]{3,2,1,0:T(4,128)} %get-tuple-element.544), channel_id=1, source_target_pairs={{0,16},{16,32},{32,48},{48,64},{64,80},{80,96},{96,112},{112,128},... | collective-permute-start | bytes 245768 | tf_op jit(solution)/shard_map/ppermute | solution.py:33
  22.0 34.7 %collective-permute-start.2 = (f32[5,32,4,1]{3,2,1,0:T(4,128)}, f32[5,32,4,1]{3,2,1,0:T(4,128)S(1)}, u32[]{:S(2)}, u32[]{:S(2)}) collective-permute-start(f32[5,32,4,1]{3,2,1,0:T(4,128)} %get-tuple-element.549), channel_id=1, source_target_pairs={{1,0},{2,1},{3,2},{4,3},{5,4},{6,5},{7,6},{8,7},{9,8},{10,9},{11,1... | collective-permute-start | bytes 7688 | tf_op jit(solution)/shard_map/ppermute | solution.py:34
  23.3 33.4 %collective-permute-start.3 = (f32[5,32,4,1]{3,2,1,0:T(4,128)}, f32[5,32,4,1]{3,2,1,0:T(4,128)}, u32[]{:S(2)}, u32[]{:S(2)}) collective-permute-start(f32[5,32,4,1]{3,2,1,0:T(4,128)} %get-tuple-element.550), channel_id=1, source_target_pairs={{0,1},{1,2},{2,3},{3,4},{4,5},{5,6},{6,7},{7,8},{8,9},{9,10},{10,1... | collective-permute-start | bytes 7688 | tf_op jit(solution)/shard_map/ppermute | solution.py:33
  28.0 1.1 copy-start.6
  28.3 28.4 %copy-start.3 = (f32[32,4,256]{2,1,0:T(4,128)S(1)}, f32[32,4,256]{2,1,0:T(4,128)}, u32[]{:S(2)}) copy-start(f32[32,4,256]{2,1,0:T(4,128)} %param.15) | copy-start | bytes 393220
  62.9 26.7 %copy-start.4 = (f32[3,32]{1,0:T(4,128)S(1)}, f32[3,32]{1,0:T(4,128)}, u32[]{:S(2)}) copy-start(f32[3,32]{1,0:T(4,128)} %get-tuple-element.577) | copy-start | bytes 1156
  64.7 156.4 %all-gather.9.cloned.1.call-start = ((), (), s32[]{:S(2)}) async-start(), calls=%async_computation.1 | async-start | bytes 1351680 | tf_op jit(solution)/shard_map/all_gather | solution.py:14
  221.1 37.2 %copy-start.5 = (f32[5,5]{1,0:T(8,128)S(1)}, f32[5,5]{1,0:T(8,128)}, u32[]{:S(2)}) copy-start(f32[5,5]{1,0:T(8,128)} %param.17) | copy-start | bytes 304
Sparse Core Ops, SparseCore 0:
  64.8 59.6 all-gather.6
  128.0 93.0 all-gather.8
where the time goes:
time: 272 us; the launch traced here: 268 us
  blocking collectives  81.3 us (30%)
  local copies, waits for them, and re-layouts  59 us (22%)
  waiting for transfers between devices  44.4 us (16%)
  matrix products  38.4 us (14%)
  starting transfers between devices  16.7 us (6%)
  between operations  13.7 us (5%)
  other arithmetic  12.4 us (5%)
    all_gather x2, blocking collectives, entering(): gathered = jax.tree.map(lambda a: lax.all_gather(a, axis), part)  81.3 us
    all_gather x2, waiting for transfers between devices, entering(): gathered = jax.tree.map(lambda a: lax.all_gather(a, axis), part)  44.4 us
    dot_general x31, matrix products, compose(): jnp.einsum('igd,idq->igq', trailing_map, leading_shift, precision=UPPER_L...  32.8 us
    sub x32, local copies, waits for them, and re-layouts, lower_turn(): unit_row[None] - one_now[:, None] * prior_one - two_now[:, None] * prior_two  22.2 us
    sub x32, local copies, waits for them, and re-layouts, upper_turn(): unit_row[None] - one_now[:, None] * next_one - two_now[:, None] * next_two  22 us
    ppermute x2, starting transfers between devices, extended(): after = lax.ppermute(initial, axis, down)  10.1 us
    ppermute x2, starting transfers between devices, extended(): before = lax.ppermute(last, axis, up)  6.65 us
  transfers between devices with their start and end apart: 6, of which 2 were waited for; matrix products, arithmetic and copies ran while one was open for 21% of the time, Pallas kernels for 0%

commit v1 on v0

v1 whole, which is shorter than its diff:
```python
import jax
import jax.numpy as jnp
from jax import lax
from jax.experimental import pallas as pl
from jax.experimental.pallas import tpu as pltpu
from jax.sharding import PartitionSpec as P

SYSTEM = (0, 0, 0, 1, 2)
F32 = jnp.float32
TILE = (8, 128)


def iotas():
    sub = lax.broadcasted_iota(jnp.int32, TILE, 0)
    lane = lax.broadcasted_iota(jnp.int32, TILE, 1)
    return sub, lane


def roll(x, shift, axis):
    size = x.shape[axis]
    return pltpu.roll(x, shift % size if isinstance(shift, int) else shift, axis)


def primitives(q):
    inv = 1.0 / jnp.where(q[0] == 0.0, 1.0, q[0])
    kinetic = 0.5 * (q[1] * q[1] + q[2] * q[2] + q[3] * q[3]) * inv
    return inv, 0.4 * (q[4] - kinetic)


def flux(q, inv, pressure, k):
    velocity = q[1 + k] * inv
    parts = [q[1 + k], q[1] * velocity, q[2] * velocity, q[3] * velocity, (q[4] + pressure) * velocity]
    parts[1 + k] = parts[1 + k] + pressure
    return parts


def quarter_move(x, a, b):
    return x if a == b else roll(x, 32 * (b - a), 1)


def by_quarter(lane, xs):
    return jnp.where(
        lane < 64, jnp.where(lane < 32, xs[0], xs[1]), jnp.where(lane < 96, xs[2], xs[3])
    )


def edges_kernel(cells, x_ref, lower_ref, upper_ref, edge_ref, last_ref, first_ref, coef_ref):
    sub, lane = iotas()
    left = sub < 4
    packed = []
    for v in range(5):
        total = jnp.zeros(TILE, F32)
        for i in range(cells):
            moved = roll(x_ref[pl.ds((v * cells + i) * 8, 8), :], i, 1)
            total = jnp.where(lane == jnp.where(left, i, (i - 1) % 128), moved, total)
        total = roll(total, 4, 0)
        packed.append(jnp.where(left, roll(total, 1, 1), roll(total, 127, 1)))
        for n in range(2):
            last_ref[pl.ds((v * 2 + n) * 8, 8), :] = x_ref[pl.ds((v * cells + cells - 2 + n) * 8, 8), :]
            first_ref[pl.ds((v * 2 + n) * 8, 8), :] = x_ref[pl.ds((v * cells + n) * 8, 8), :]
    inv, pressure = primitives(packed)
    for v, part in enumerate(flux(packed, inv, pressure, 1)):
        edge_ref[pl.ds(v * 8, 8), :] = part
    coef_ref[...] = jnp.zeros(coef_ref.shape, F32)
    for s in range(3):
        inverse = 1.0 / lower_ref[s, 2:3, :]
        coef_ref[s * 5 : s * 5 + 1, 0:cells] = lower_ref[s, 1:2, :] * inverse
        coef_ref[s * 5 + 1 : s * 5 + 2, 0:cells] = lower_ref[s, 0:1, :] * inverse
        coef_ref[s * 5 + 2 : s * 5 + 3, 0:cells] = inverse
        coef_ref[s * 5 + 3 : s * 5 + 5, 0:cells] = upper_ref[s]


def local_kernel(
    cells, x_ref, dt_ref, before_ref, after_ref, west_ref, east_ref, coef_ref, char_mat, char_ref, out_ref, q_ref, f_ref
):
    sub, lane = iotas()
    third = sub % 4
    west = sub < 4
    for v in range(5):
        q_ref[v, 0:16] = before_ref[pl.ds(v * 16, 16), :]
        q_ref[v, pl.ds(16, cells * 8)] = x_ref[pl.ds(v * cells * 8, cells * 8), :]
        q_ref[v, pl.ds(16 + cells * 8, 16)] = after_ref[pl.ds(v * 16, 16), :]
    beside = [
        jnp.where(west, west_ref[pl.ds(v * 8, 8), :], east_ref[pl.ds(v * 8, 8), :]) for v in range(5)
    ]
    outside = (west & (lane == 0)) | (~west & (lane == 127))
    unit = [jnp.where((lane == n) & (sub >= 0), 1.0, 0.0).astype(F32) for n in range(4)]
    zero = jnp.where((lane < 0) & (sub < 0), 1.0, 0.0).astype(F32)
    rows = SYSTEM + (0, 1, 2)

    def layer(i):
        at = pl.ds(pl.multiple_of((i + 2) * 8, 8), 8)
        return [q_ref[v, at, :] for v in range(5)]

    def line(i):
        q = layer(i)
        inv, pressure = primitives(q)
        return flux(q, inv, pressure, 0), inv, pressure

    def forward(i, carry):
        flux_before, (flux_now, inv, pressure), prior_one, prior_two = carry
        q = layer(i)
        flux_after, inv_after, pressure_after = line(i + 1)
        side = flux(q, inv, pressure, 1)
        over = flux(q, inv, pressure, 2)
        two, one, next_one, next_two = (layer(i + n) for n in (-2, -1, 1, 2))
        scale = -0.5 * dt_ref[pl.ds(pl.multiple_of(i * 8, 8), 8), :]
        right = []
        for v in range(5):
            down, up = roll(side[v], 1, 1), roll(side[v], 127, 1)
            cut = roll(jnp.where(lane == 0, down, up), 4, 0)
            cut = jnp.where(outside, roll(beside[v], lax.rem(128 - i, 128), 1), cut)
            side_diff = jnp.where(lane == 127, cut, up) - jnp.where(lane == 0, cut, down)
            over_diff = jnp.where(third == 3, roll(over[v], 3, 0), roll(over[v], 7, 0)) - jnp.where(
                third == 0, roll(over[v], 5, 0), roll(over[v], 1, 0)
            )
            fourth = (two[v] + next_two[v]) - 4.0 * (one[v] + next_one[v]) + 6.0 * q[v]
            total = (flux_after[v] - flux_before[v]) + side_diff + over_diff + 0.125 * fourth
            right.append(scale * total)
        new = []
        for n, s in enumerate(rows):
            value = -(coef_ref[s * 5, i] * prior_one[n]) - coef_ref[s * 5 + 1, i] * prior_two[n]
            if n < 5:
                char = sum(char_mat[n, v] * right[v] for v in range(5))
                char_ref[pl.ds(pl.multiple_of((n * cells + i) * 8, 8), 8), :] = char
                value = value + coef_ref[s * 5 + 2, i] * char
            f_ref[n, pl.ds(pl.multiple_of(i * 8, 8), 8), :] = value
            new.append(value)
        return flux_now, (flux_after, inv_after, pressure_after), new, prior_one

    start = [zero] * 5
    _, _, last_one, last_two = lax.fori_loop(
        0,
        cells,
        forward,
        (line(-1)[0], line(0), start + [unit[0]] * 3, start + [unit[1]] * 3),
    )

    def backward(step, carry):
        i = cells - 1 - step
        next_one, next_two = carry
        new = []
        for n, s in enumerate(rows):
            value = f_ref[n, pl.ds(pl.multiple_of(i * 8, 8), 8), :]
            new.append(value - coef_ref[s * 5 + 3, i] * next_one[n] - coef_ref[s * 5 + 4, i] * next_two[n])
        return new, next_one

    first_one, first_two = lax.fori_loop(
        0, cells, backward, (start + [unit[2]] * 3, start + [unit[3]] * 3)
    )
    ends = (last_one, last_two, first_one, first_two)
    response = zero
    for s in range(3):
        for k in range(4):
            at = (s * 4 + k) * 4
            moved = ends[k][5 + s] if at == 0 else roll(ends[k][5 + s], at, 1)
            response = jnp.where((lane >= at) & (lane < at + 4), moved, response)
    for quarter in range(4):
        base = quarter * 64
        for k in range(4):
            out_ref[pl.ds(base + k, 8, stride=8), :] = by_quarter(
                lane, [quarter_move(ends[k][u], quarter, u) for u in range(4)]
            )
        out_ref[pl.ds(base + 4, 8, stride=8), :] = by_quarter(
            lane, [quarter_move(ends[k][4], quarter, k) for k in range(4)]
        )
        out_ref[pl.ds(base + 5, 8, stride=8), :] = jnp.broadcast_to(response[0:1, :], TILE)
        for k in (6, 7):
            out_ref[pl.ds(base + k, 8, stride=8), :] = zero


def reduced_kernel(count, in_ref, out_ref, part_ref, coef_ref, four_ref):
    lane = lax.broadcasted_iota(jnp.int32, (count, 128), 1)
    fifth = in_ref[pl.ds(4, count, stride=8), :]
    response = in_ref[pl.ds(5, count, stride=8), :]
    for k in range(4):
        part_ref[k, 0] = in_ref[pl.ds(k, count, stride=8), :]
        part_ref[k, 1] = quarter_move(fifth, k, 0)
        for c in range(4):
            if k < 2 and c >= 2:
                continue
            wide = [
                jnp.broadcast_to(response[:, (s * 4 + k) * 4 + c : (s * 4 + k) * 4 + c + 1], (count, 128))
                for s in range(3)
            ]
            coef_ref[k * 4 + c, 0] = jnp.where(lane < 96, wide[0], wide[1])
            coef_ref[k * 4 + c, 1] = wide[2]
    zero = jnp.zeros((1, 128), F32)

    def take(ref, n, tile, t):
        return ref[n, tile, t : t + 1, :]

    inflow = [(zero, zero), (zero, zero)]
    sums = []
    for t in range(count):
        row = []
        for tile in range(2):
            one, two = inflow[tile]
            for k, value in ((0, one), (1, two)):
                if tile == 0:
                    out_ref[t * 8 + k : t * 8 + k + 1, :] = value
                else:
                    four_ref[k, t : t + 1, :] = value
            made = [
                take(part_ref, k, tile, t)
                + take(coef_ref, k * 4, tile, t) * one
                + take(coef_ref, k * 4 + 1, tile, t) * two
                for k in range(4)
            ]
            inflow[tile] = (made[0], made[1])
            row.append((made[2], made[3]))
        sums.append(row)
    inflow = [(zero, zero), (zero, zero)]
    for t in reversed(range(count)):
        for tile in range(2):
            one, two = inflow[tile]
            for k, value in ((2, one), (3, two)):
                if tile == 0:
                    out_ref[t * 8 + k : t * 8 + k + 1, :] = value
                else:
                    four_ref[k, t : t + 1, :] = value
            inflow[tile] = tuple(
                sums[t][tile][k - 2]
                + take(coef_ref, k * 4 + 2, tile, t) * one
                + take(coef_ref, k * 4 + 3, tile, t) * two
                for k in (2, 3)
            )
    out_ref[pl.ds(4, count, stride=8), :] = by_quarter(
        lane, [quarter_move(four_ref[k], 0, k) for k in range(4)]
    )
    for k in (5, 6, 7):
        out_ref[pl.ds(k, count, stride=8), :] = jnp.zeros((count, 128), F32)


def final_kernel(cells, char_ref, in_ref, coef_ref, cons_mat, out_ref, f_ref):
    _, lane = iotas()
    inflow = []
    for k in range(4):
        parts = [in_ref[pl.ds(q * 64 + k, 8, stride=8), :] for q in range(4)]
        inflow.append(
            [by_quarter(lane, [quarter_move(parts[q], u, q) for q in range(4)]) for u in range(4)]
        )
    parts = [in_ref[pl.ds(q * 64 + 4, 8, stride=8), :] for q in range(4)]
    for k in range(4):
        inflow[k].append(by_quarter(lane, [quarter_move(parts[q], k, q) for q in range(4)]))

    def forward(i, carry):
        prior_one, prior_two = carry
        new = []
        for n, s in enumerate(SYSTEM):
            value = coef_ref[s * 5 + 2, i] * char_ref[pl.ds(pl.multiple_of((n * cells + i) * 8, 8), 8), :]
            value = value - coef_ref[s * 5 + 1, i] * prior_two[n] - coef_ref[s * 5, i] * prior_one[n]
            f_ref[n, pl.ds(pl.multiple_of(i * 8, 8), 8), :] = value
            new.append(value)
        return new, prior_one

    lax.fori_loop(0, cells, forward, (inflow[0], inflow[1]))

    def backward(step, carry):
        i = cells - 1 - step
        next_one, next_two = carry
        new = []
        for n, s in enumerate(SYSTEM):
            value = f_ref[n, pl.ds(pl.multiple_of(i * 8, 8), 8), :]
            new.append(value - coef_ref[s * 5 + 4, i] * next_two[n] - coef_ref[s * 5 + 3, i] * next_one[n])
        for n in range(5):
            out_ref[pl.ds(pl.multiple_of((n * cells + i) * 8, 8), 8), :] = sum(
                cons_mat[n, v] * new[v] for v in range(5)
            )
        return new, next_one

    lax.fori_loop(0, cells, backward, (inflow[2], inflow[3]))


def shaped(*shape):
    return jax.ShapeDtypeStruct(shape, F32)


VMEM = pl.BlockSpec(memory_space=pltpu.VMEM)
SMEM = pl.BlockSpec(memory_space=pltpu.SMEM)


def on_device(state, time_step, to_char, to_cons, lower_bands, upper_bands):
    cells = state.shape[1]
    count = lax.axis_size("sec")
    columns = lax.axis_size("cross")
    flat = state.reshape(5, cells, 4, 2, 128).transpose(0, 1, 3, 2, 4).reshape(5 * cells * 8, 128)
    steps = time_step.reshape(cells, 4, 2, 128).transpose(0, 2, 1, 3).reshape(cells * 8, 128)
    edge, last, first, coef = pl.pallas_call(
        lambda *refs: edges_kernel(cells, *refs),
        out_shape=(shaped(40, 128), shaped(80, 128), shaped(80, 128), shaped(16, 128)),
        in_specs=[VMEM] * 3,
        out_specs=(VMEM,) * 4,
        name="edges",
    )(flat, lower_bands, upper_bands)
    up = [(i, i + 1) for i in range(count - 1)]
    right = [(i, i + 1) for i in range(columns - 1)]
    before = lax.ppermute(last, "sec", up)
    after = lax.ppermute(first, "sec", [(j, i) for i, j in up])
    west = lax.ppermute(edge, "cross", right)
    east = lax.ppermute(edge, "cross", [(j, i) for i, j in right])
    char, ends = pl.pallas_call(
        lambda *refs: local_kernel(cells, *refs),
        out_shape=(shaped(5 * cells * 8, 128), shaped(256, 128)),
        in_specs=[VMEM] * 6 + [SMEM] * 2,
        out_specs=(VMEM, VMEM),
        scratch_shapes=[
            pltpu.VMEM((5, (cells + 4) * 8, 128), F32),
            pltpu.VMEM((8, cells * 8, 128), F32),
        ],
        name="local",
    )(flat, steps, before, after, west, east, coef, to_char)
    ends = lax.all_to_all(ends, "sec", 0, 0, tiled=True)
    inflow = pl.pallas_call(
        lambda *refs: reduced_kernel(count, *refs),
        out_shape=shaped(256, 128),
        in_specs=[VMEM],
        out_specs=VMEM,
        scratch_shapes=[
            pltpu.VMEM((4, 2, count, 128), F32),
            pltpu.VMEM((16, 2, count, 128), F32),
            pltpu.VMEM((4, count, 128), F32),
        ],
        name="reduced",
    )(ends)
    inflow = lax.all_to_all(inflow, "sec", 0, 0, tiled=True)
    result = pl.pallas_call(
        lambda *refs: final_kernel(cells, *refs),
        out_shape=shaped(5 * cells * 8, 128),
        in_specs=[VMEM, VMEM, SMEM, SMEM],
        out_specs=VMEM,
        scratch_shapes=[pltpu.VMEM((5, cells * 8, 128), F32)],
        name="final",
    )(char, inflow, coef, to_cons)
    return result.reshape(5, cells, 2, 4, 128).transpose(0, 1, 3, 2, 4).reshape(state.shape)


def solution(mesh):
    in_specs = (
        P(None, "sec", None, "cross"),
        P("sec", None, "cross"),
        P(),
        P(),
        P(None, None, "sec"),
        P(None, None, "sec"),
    )
    out_specs = P(None, "sec", None, "cross")
    return jax.shard_map(
        on_device, mesh=mesh, in_specs=in_specs, out_specs=out_specs, check_vma=False
    )
```

time: 272 us -> 59 us (0.22)
  the two profiles are of different devices: /device:TPU:1 before, /device:TPU:385 now
where the time goes in v1:
time: 59 us; the launch traced here: 58.6 us
  blocking collectives  29.2 us (49%)
  Pallas kernels  13.3 us (23%)
  starting transfers between devices  11.4 us (19%)
  waiting for transfers between devices  4.01 us (7%)
  local copies, waits for them, and re-layouts  0.62 us (1%)
    all_to_all x1, blocking collectives, on_device(): ends = lax.all_to_all(ends, 'sec', 0, 0, tiled=True)  16.9 us
    all_to_all x1, blocking collectives, on_device(): inflow = lax.all_to_all(inflow, 'sec', 0, 0, tiled=True)  12.3 us
    pallas_call x1, Pallas kernels, on_device(): pl.pallas_call(lambda *refs: local_kernel(cells, *refs), out_shape=(shape...  5.85 us
    ppermute x1, waiting for transfers between devices, on_device(): west = lax.ppermute(edge, 'cross', right)  4 us
    ppermute x1, starting transfers between devices, on_device(): east = lax.ppermute(edge, 'cross', [(j, i) for i, j in right])  3.85 us
    ppermute x1, starting transfers between devices, on_device(): before = lax.ppermute(last, 'sec', up)  3.67 us
    pallas_call x1, Pallas kernels, on_device(): pl.pallas_call(lambda *refs: final_kernel(cells, *refs), out_shape=shaped...  3.37 us
    pallas_call x1, Pallas kernels, on_device(): pl.pallas_call(lambda *refs: reduced_kernel(count, *refs), out_shape=shap...  2.06 us
  transfers between devices with their start and end apart: 4, of which 1 were waited for; matrix products, arithmetic and copies ran while one was open for 0% of the time, Pallas kernels for 0%

profile of v1, /device:TPU:385, one launch (start us, length us, event | category | flops | bytes accessed | tf_op | source)
XLA Modules:
  0.0 58.6 jit_solution(15069271384655934654)
XLA Ops:
  0.0 2.1 %edges.1 = (f32[40,128]{1,0:T(8,128)}, f32[80,128]{1,0:T(8,128)}, f32[80,128]{1,0:T(8,128)}, f32[16,128]{1,0:T(8,128)}) custom-call(f32[1280,128]{1,0:T(8,128)} %bitcast.19, f32[3,3,32]{2,1,0:T(4,128)} %refs_1_.1, f32[3,2,32]{2,1,0:T(2,128)} %refs_2_.1), custom_call_target="tpu_custom_call" | custom-call | tf_op jit(solution)/shard_map/edges/pallas_call | solution.py:289
  2.1 3.7 %collective-permute-start = (f32[80,128]{1,0:T(8,128)}, f32[80,128]{1,0:T(8,128)S(1)}, u32[]{:S(2)}, u32[]{:S(2)}) collective-permute-start(f32[80,128]{1,0:T(8,128)} %get-tuple-element.11), channel_id=1, source_target_pairs={{0,16},{16,32},{32,48},{48,64},{64,80},{80,96},{96,112},{112,128},... | collective-permute-start | bytes 122888 | tf_op jit(solution)/shard_map/ppermute | solution.py:298
  5.7 1.9 %collective-permute-start.1 = (f32[80,128]{1,0:T(8,128)}, f32[80,128]{1,0:T(8,128)S(1)}, u32[]{:S(2)}, u32[]{:S(2)}) collective-permute-start(f32[80,128]{1,0:T(8,128)} %get-tuple-element.12), channel_id=1, source_target_pairs={{16,0},{32,16},{48,32},{64,48},{80,64},{96,80},{112,96},{128,112},... | collective-permute-start | bytes 122888 | tf_op jit(solution)/shard_map/ppermute | solution.py:299
  7.7 3.8 %collective-permute-start.3 = (f32[40,128]{1,0:T(8,128)}, f32[40,128]{1,0:T(8,128)S(1)}, u32[]{:S(2)}, u32[]{:S(2)}) collective-permute-start(f32[40,128]{1,0:T(8,128)} %get-tuple-element.13), channel_id=1, source_target_pairs={{1,0},{2,1},{3,2},{4,3},{5,4},{6,5},{7,6},{8,7},{9,8},{10,9},{11,1... | collective-permute-start | bytes 61448 | tf_op jit(solution)/shard_map/ppermute | solution.py:301
  11.5 1.9 %collective-permute-start.2 = (f32[40,128]{1,0:T(8,128)}, f32[40,128]{1,0:T(8,128)S(1)}, u32[]{:S(2)}, u32[]{:S(2)}) collective-permute-start(f32[40,128]{1,0:T(8,128)} %get-tuple-element.13), channel_id=1, source_target_pairs={{0,1},{1,2},{2,3},{3,4},{4,5},{5,6},{6,7},{7,8},{8,9},{9,10},{10,1... | collective-permute-start | bytes 61448 | tf_op jit(solution)/shard_map/ppermute | solution.py:300
  13.4 0.0 collective-permute-done.3.refs_5_
  13.5 0.0 copy-start.2
  13.5 4.0 %collective-permute-done.2.refs_4_ = f32[40,128]{1,0:T(8,128)S(1)} collective-permute-done((f32[40,128]{1,0:T(8,128)}, f32[40,128]{1,0:T(8,128)S(1)}, u32[]{:S(2)}, u32[]{:S(2)}) %collective-permute-start.2) | collective-permute-done | bytes 20512 | tf_op jit(solution)/shard_map/ppermute | solution.py:300
  17.5 0.0 copy-start.3
  17.5 0.0 collective-permute-done.refs_2_
  17.5 0.0 copy-start
  17.5 0.0 collective-permute-done.1.refs_3_
  17.5 0.0 copy-start.1
  17.5 0.0 copy-done.2
  17.5 0.6 copy-done.3
  18.1 0.0 copy-done
  18.1 0.0 copy-done.1
  18.1 5.8 %local.1 = (f32[1280,128]{1,0:T(8,128)}, f32[256,128]{1,0:T(8,128)}) custom-call(f32[1280,128]{1,0:T(8,128)} %bitcast.20, f32[256,128]{1,0:T(8,128)} %bitcast.24, f32[80,128]{1,0:T(8,128)} %copy-done, f32[80,128]{1,0:T(8,128)} %copy-done.1, f32[40,128]{1,0:T(8,128)} %copy-done.3, f32[40,128]{1,0:T(8,128)} %copy-done.2, ...), custom_call_target="tpu_custom_call" | custom-call | tf_op jit(solution)/shard_map/local/pallas_call | solution.py:302
  24.0 16.9 %all_to_all.22 = f32[32,8,128]{2,1,0:T(8,128)} all-to-all(f32[32,8,128]{2,1,0:T(8,128)} %bitcast.25), channel_id=1, replica_groups=mesh['sec'=32,'cross'=16] {'sec'}, dimensions={0} | all-to-all | bytes 262144 | tf_op jit(solution)/shard_map/all_to_all | solution.py:313
  40.8 2.1 %reduced.1 = f32[256,128]{1,0:T(8,128)} custom-call(f32[256,128]{1,0:T(8,128)} %bitcast.21), custom_call_target="tpu_custom_call" | custom-call | tf_op jit(solution)/shard_map/reduced/pallas_call | solution.py:314
  42.9 12.3 %all_to_all.23 = f32[32,8,128]{2,1,0:T(8,128)} all-to-all(f32[32,8,128]{2,1,0:T(8,128)} %bitcast.22), channel_id=1, replica_groups=mesh['sec'=32,'cross'=16] {'sec'}, dimensions={0} | all-to-all | bytes 262144 | tf_op jit(solution)/shard_map/all_to_all | solution.py:326
  55.2 3.4 %final.1 = f32[1280,128]{1,0:T(8,128)} custom-call(f32[1280,128]{1,0:T(8,128)} %get-tuple-element.15.refs_0_, f32[256,128]{1,0:T(8,128)} %bitcast.23, f32[16,128]{1,0:T(8,128)} %get-tuple-element.14.refs_6_.refs_2_, f32[5,5]{1,0:T(8,128)} %refs_3_.1), custom_call_target="tpu_custom_call" | custom-call | tf_op jit(solution)/shard_map/final/pallas_call | solution.py:327
Async XLA Ops:
  2.1 15.4 %collective-permute-start = (f32[80,128]{1,0:T(8,128)}, f32[80,128]{1,0:T(8,128)S(1)}, u32[]{:S(2)}, u32[]{:S(2)}) collective-permute-start(f32[80,128]{1,0:T(8,128)} %get-tuple-element.11), channel_id=1, source_target_pairs={{0,16},{16,32},{32,48},{48,64},{64,80},{80,96},{96,112},{112,128},... | collective-permute-start | bytes 122888 | tf_op jit(solution)/shard_map/ppermute | solution.py:298
  5.7 11.7 %collective-permute-start.1 = (f32[80,128]{1,0:T(8,128)}, f32[80,128]{1,0:T(8,128)S(1)}, u32[]{:S(2)}, u32[]{:S(2)}) collective-permute-start(f32[80,128]{1,0:T(8,128)} %get-tuple-element.12), channel_id=1, source_target_pairs={{16,0},{32,16},{48,32},{64,48},{80,64},{96,80},{112,96},{128,112},... | collective-permute-start | bytes 122888 | tf_op jit(solution)/shard_map/ppermute | solution.py:299
  7.7 5.8 %collective-permute-start.3 = (f32[40,128]{1,0:T(8,128)}, f32[40,128]{1,0:T(8,128)S(1)}, u32[]{:S(2)}, u32[]{:S(2)}) collective-permute-start(f32[40,128]{1,0:T(8,128)} %get-tuple-element.13), channel_id=1, source_target_pairs={{1,0},{2,1},{3,2},{4,3},{5,4},{6,5},{7,6},{8,7},{9,8},{10,9},{11,1... | collective-permute-start | bytes 61448 | tf_op jit(solution)/shard_map/ppermute | solution.py:301
  11.5 5.9 %collective-permute-start.2 = (f32[40,128]{1,0:T(8,128)}, f32[40,128]{1,0:T(8,128)S(1)}, u32[]{:S(2)}, u32[]{:S(2)}) collective-permute-start(f32[40,128]{1,0:T(8,128)} %get-tuple-element.13), channel_id=1, source_target_pairs={{0,1},{1,2},{2,3},{3,4},{4,5},{5,6},{6,7},{7,8},{8,9},{9,10},{10,1... | collective-permute-start | bytes 61448 | tf_op jit(solution)/shard_map/ppermute | solution.py:300
  13.5 4.0 %copy-start.2 = (f32[40,128]{1,0:T(8,128)}, f32[40,128]{1,0:T(8,128)S(1)}, u32[]{:S(2)}) copy-start(f32[40,128]{1,0:T(8,128)S(1)} %collective-permute-done.3.refs_5_) | copy-start | bytes 61444
  17.5 0.6 %copy-start.3 = (f32[40,128]{1,0:T(8,128)}, f32[40,128]{1,0:T(8,128)S(1)}, u32[]{:S(2)}) copy-start(f32[40,128]{1,0:T(8,128)S(1)} %collective-permute-done.2.refs_4_) | copy-start | bytes 61444
  17.5 0.6 %copy-start = (f32[80,128]{1,0:T(8,128)}, f32[80,128]{1,0:T(8,128)S(1)}, u32[]{:S(2)}) copy-start(f32[80,128]{1,0:T(8,128)S(1)} %collective-permute-done.refs_2_) | copy-start | bytes 122884
  17.5 0.6 %copy-start.1 = (f32[80,128]{1,0:T(8,128)}, f32[80,128]{1,0:T(8,128)S(1)}, u32[]{:S(2)}) copy-start(f32[80,128]{1,0:T(8,128)S(1)} %collective-permute-done.1.refs_3_) | copy-start | bytes 122884

commit v2 on v1

v2 whole, which is shorter than its diff:
```python
import jax
import jax.numpy as jnp
from jax import lax
from jax.experimental import pallas as pl
from jax.experimental.pallas import tpu as pltpu
from jax.sharding import PartitionSpec as P

SYSTEM = (0, 0, 0, 1, 2)
F32 = jnp.float32
UNROLL = 8
TILE = (8, 128)


def iotas():
    sub = lax.broadcasted_iota(jnp.int32, TILE, 0)
    lane = lax.broadcasted_iota(jnp.int32, TILE, 1)
    return sub, lane


def roll(x, shift, axis):
    size = x.shape[axis]
    return pltpu.roll(x, shift % size if isinstance(shift, int) else shift, axis)


def primitives(q):
    inv = 1.0 / jnp.where(q[0] == 0.0, 1.0, q[0])
    kinetic = 0.5 * (q[1] * q[1] + q[2] * q[2] + q[3] * q[3]) * inv
    return inv, 0.4 * (q[4] - kinetic)


def flux(q, inv, pressure, k):
    velocity = q[1 + k] * inv
    parts = [q[1 + k], q[1] * velocity, q[2] * velocity, q[3] * velocity, (q[4] + pressure) * velocity]
    parts[1 + k] = parts[1 + k] + pressure
    return parts


def quarter_move(x, a, b):
    return x if a == b else roll(x, 32 * (b - a), 1)


def by_quarter(lane, xs):
    return jnp.where(
        lane < 64, jnp.where(lane < 32, xs[0], xs[1]), jnp.where(lane < 96, xs[2], xs[3])
    )


def packed_edges(cells, layer):
    sub, lane = iotas()
    total = jnp.zeros(TILE, F32)
    for i in range(cells):
        moved = roll(layer(i), i, 1) if i else layer(i)
        total = jnp.where(lane == jnp.where(sub < 4, i, (i - 1) % 128), moved, total)
    return total


def edges_kernel(
    cells, x_hbm, dt_hbm, lower_hbm, upper_hbm, char_hbm, cons_hbm,
    edge_ref, last_ref, first_ref, x_ref, dt_ref, dt_edge_ref, coef_ref, char_mat, cons_mat,
    lower_ref, upper_ref, made_ref, x_sems, sems,
):
    sub, _ = iotas()
    rows = cells * 8
    x_copies = [
        pltpu.make_async_copy(
            x_hbm.at[pl.ds(v * rows, rows)], x_ref.at[v, pl.ds(16, rows)], x_sems.at[v]
        )
        for v in range(5)
    ]
    pairs = (
        (lower_hbm, lower_ref),
        (upper_hbm, upper_ref),
        (dt_hbm, dt_ref),
        (char_hbm, char_mat),
        (cons_hbm, cons_mat),
    )
    copies = [pltpu.make_async_copy(a, b, sems.at[n]) for n, (a, b) in enumerate(pairs)]
    for copy in x_copies + copies:
        copy.start()
    for v in range(5):
        x_ref[v, 0:16] = jnp.zeros((16, 128), F32)
        x_ref[v, pl.ds(16 + rows, 16)] = jnp.zeros((16, 128), F32)
    made_ref[...] = jnp.zeros(made_ref.shape, F32)
    copies[0].wait()
    copies[1].wait()
    for s in range(3):
        inverse = 1.0 / lower_ref[s, 2:3, :]
        made_ref[s * 5 : s * 5 + 1, 0:cells] = lower_ref[s, 1:2, :] * inverse
        made_ref[s * 5 + 1 : s * 5 + 2, 0:cells] = lower_ref[s, 0:1, :] * inverse
        made_ref[s * 5 + 2 : s * 5 + 3, 0:cells] = inverse
        made_ref[s * 5 + 3 : s * 5 + 5, 0:cells] = upper_ref[s]
    made = pltpu.make_async_copy(made_ref, coef_ref, sems.at[5])
    made.start()
    packed = []
    for v in range(5):
        x_copies[v].wait()
        total = packed_edges(cells, lambda i, v=v: x_ref[v, pl.ds(16 + i * 8, 8), :])
        total = roll(total, 4, 0)
        packed.append(jnp.where(sub < 4, roll(total, 1, 1), roll(total, 127, 1)))
        last_ref[pl.ds(v * 16, 16), :] = x_ref[v, pl.ds(rows, 16), :]
        first_ref[pl.ds(v * 16, 16), :] = x_ref[v, 16:32, :]
    inv, pressure = primitives(packed)
    for v, part in enumerate(flux(packed, inv, pressure, 1)):
        edge_ref[pl.ds(v * 8, 8), :] = part
    copies[2].wait()
    dt_edge_ref[...] = packed_edges(cells, lambda i: dt_ref[pl.ds(i * 8, 8), :])
    copies[3].wait()
    copies[4].wait()
    made.wait()


def layer_at(i):
    return pl.ds(i * 8 if isinstance(i, int) else pl.multiple_of(i * 8, 8), 8)


def to_char(char_mat, right):
    return [sum(char_mat[u, v] * right[v] for v in range(5)) for u in range(5)]


def inner_kernel(cells, x_ref, dt_ref, coef_ref, char_mat, char_ref, response_ref, f_ref):
    sub, lane = iotas()
    third = sub % 4

    def layer(i):
        return [x_ref[v, layer_at(i + 2), :] for v in range(5)]

    def line(i):
        q = layer(i)
        inv, pressure = primitives(q)
        return flux(q, inv, pressure, 0), inv, pressure

    def cell(i, carry):
        flux_before, (flux_now, inv, pressure) = carry
        q = layer(i)
        flux_after, inv_after, pressure_after = line(i + 1)
        side = flux(q, inv, pressure, 1)
        over = flux(q, inv, pressure, 2)
        two, one, next_one, next_two = (layer(i + n) for n in (-2, -1, 1, 2))
        scale = -0.5 * dt_ref[layer_at(i), :]
        right = []
        for v in range(5):
            down, up = roll(side[v], 1, 1), roll(side[v], 127, 1)
            cut = roll(jnp.where(lane == 0, down, up), 4, 0)
            cut = jnp.where((lane == 0) == (sub < 4), 0.0, cut)
            side_diff = jnp.where(lane == 127, cut, up) - jnp.where(lane == 0, cut, down)
            over_diff = jnp.where(third == 3, roll(over[v], 3, 0), roll(over[v], 7, 0)) - jnp.where(
                third == 0, roll(over[v], 5, 0), roll(over[v], 1, 0)
            )
            fourth = (two[v] + next_two[v]) - 4.0 * (one[v] + next_one[v]) + 6.0 * q[v]
            total = (flux_after[v] - flux_before[v]) + side_diff + over_diff + 0.125 * fourth
            right.append(scale * total)
        for u, value in enumerate(to_char(char_mat, right)):
            char_ref[u, layer_at(i), :] = value
        return flux_now, (flux_after, inv_after, pressure_after)

    lax.fori_loop(0, cells, cell, (line(-1)[0], line(0)), unroll=UNROLL)

    unit = [jnp.where((lane == n) & (sub >= 0), 1.0, 0.0).astype(F32) for n in range(4)]

    def forward(i, carry):
        one, two = carry
        new = [-(coef_ref[s * 5, i] * one[s]) - coef_ref[s * 5 + 1, i] * two[s] for s in range(3)]
        for s in range(3):
            f_ref[s, layer_at(i), :] = new[s]
        return new, one

    def backward(step, carry):
        i = cells - 1 - step
        one, two = carry
        new = [
            f_ref[s, layer_at(i), :] - coef_ref[s * 5 + 3, i] * one[s] - coef_ref[s * 5 + 4, i] * two[s]
            for s in range(3)
        ]
        return new, one

    last = lax.fori_loop(0, cells, forward, ([unit[0]] * 3, [unit[1]] * 3), unroll=UNROLL)
    first = lax.fori_loop(0, cells, backward, ([unit[2]] * 3, [unit[3]] * 3), unroll=UNROLL)
    ends = last + first
    response = jnp.zeros(TILE, F32)
    for s in range(3):
        for k in range(4):
            at = (s * 4 + k) * 4
            moved = ends[k][s] if at == 0 else roll(ends[k][s], at, 1)
            response = jnp.where((lane >= at) & (lane < at + 4), moved, response)
    response_ref[...] = response


def local_kernel(
    cells, char_ref, response_ref, dt_ref, dt_edge_ref, before_ref, after_ref, west_ref, east_ref, coef_ref, char_mat,
    out_ref, f_ref,
):
    sub, lane = iotas()
    before = [[before_ref[pl.ds(v * 16 + n, 8), :] for v in range(5)] for n in (0, 8)]
    after = [[after_ref[pl.ds(v * 16 + n, 8), :] for v in range(5)] for n in (0, 8)]
    flux_before = flux(before[1], *primitives(before[1]), 0)
    flux_after = flux(after[0], *primitives(after[0]), 0)
    terms = (
        (0, lambda v: 0.125 * (before[0][v] - 4.0 * before[1][v]) - flux_before[v]),
        (1, lambda v: 0.125 * before[1][v]),
        (cells - 2, lambda v: 0.125 * after[0][v]),
        (cells - 1, lambda v: 0.125 * (after[1][v] - 4.0 * after[0][v]) + flux_after[v]),
    )
    added = {}
    for i, term in terms:
        scale = -0.5 * dt_ref[pl.ds(i * 8, 8), :]
        added[i] = to_char(char_mat, [scale * term(v) for v in range(5)])
    scale = -0.5 * dt_edge_ref[...]
    beside = to_char(
        char_mat,
        [
            scale * jnp.where(sub < 4, -west_ref[pl.ds(v * 8, 8), :], east_ref[pl.ds(v * 8, 8), :])
            for v in range(5)
        ],
    )
    outside = (lane == jnp.where(sub < 4, 0, 127)) & (sub >= 0)
    zero = jnp.where((lane < 0) & (sub < 0), 1.0, 0.0).astype(F32)

    def forward(i, carry, more=None):
        one, two = carry
        new = []
        for n, s in enumerate(SYSTEM):
            char = char_ref[n, layer_at(i), :] + jnp.where(
                outside, roll(beside[n], (128 - i) % 128, 1), 0.0
            )
            if more:
                char = char + more[n]
            value = coef_ref[s * 5 + 2, i] * char - coef_ref[s * 5 + 1, i] * two[n] - coef_ref[s * 5, i] * one[n]
            f_ref[n, layer_at(i), :] = value
            new.append(value)
        return new, one

    def backward(step, carry):
        i = cells - 1 - step
        one, two = carry
        new = [
            f_ref[n, layer_at(i), :] - coef_ref[s * 5 + 4, i] * two[n] - coef_ref[s * 5 + 3, i] * one[n]
            for n, s in enumerate(SYSTEM)
        ]
        return new, one

    start = ([zero] * 5, [zero] * 5)
    last = start
    for i in (0, 1):
        last = forward(i, last, added[i])
    last = lax.fori_loop(2, cells - 2, forward, last, unroll=7)
    for i in (cells - 2, cells - 1):
        last = forward(i, last, added[i])
    first = lax.fori_loop(0, cells, backward, start, unroll=UNROLL)
    ends = last + first
    response = jnp.broadcast_to(response_ref[0:1, :], TILE)
    for quarter in range(4):
        base = quarter * 64
        for k in range(4):
            out_ref[pl.ds(base + k, 8, stride=8), :] = by_quarter(
                lane, [quarter_move(ends[k][u], quarter, u) for u in range(4)]
            )
        out_ref[pl.ds(base + 4, 8, stride=8), :] = by_quarter(
            lane, [quarter_move(ends[k][4], quarter, k) for k in range(4)]
        )
        out_ref[pl.ds(base + 5, 8, stride=8), :] = response
        for k in (6, 7):
            out_ref[pl.ds(base + k, 8, stride=8), :] = jnp.zeros(TILE, F32)


def reduced_kernel(count, in_ref, out_ref, part_ref, coef_ref, four_ref):
    lane = lax.broadcasted_iota(jnp.int32, (count, 128), 1)
    fifth = in_ref[pl.ds(4, count, stride=8), :]
    response = in_ref[pl.ds(5, count, stride=8), :]
    for k in range(4):
        part_ref[k, 0] = in_ref[pl.ds(k, count, stride=8), :]
        part_ref[k, 1] = quarter_move(fifth, k, 0)
        for c in range(4):
            if k < 2 and c >= 2:
                continue
            wide = [
                jnp.broadcast_to(response[:, (s * 4 + k) * 4 + c : (s * 4 + k) * 4 + c + 1], (count, 128))
                for s in range(3)
            ]
            coef_ref[k * 4 + c, 0] = jnp.where(lane < 96, wide[0], wide[1])
            coef_ref[k * 4 + c, 1] = wide[2]
    zero = jnp.zeros((1, 128), F32)

    def take(ref, n, tile, t):
        return ref[n, tile, t : t + 1, :]

    inflow = [(zero, zero), (zero, zero)]
    sums = []
    for t in range(count):
        row = []
        for tile in range(2):
            one, two = inflow[tile]
            for k, value in ((0, one), (1, two)):
                if tile == 0:
                    out_ref[t * 8 + k : t * 8 + k + 1, :] = value
                else:
                    four_ref[k, t : t + 1, :] = value
            made = [
                take(part_ref, k, tile, t)
                + take(coef_ref, k * 4, tile, t) * one
                + take(coef_ref, k * 4 + 1, tile, t) * two
                for k in range(4)
            ]
            inflow[tile] = (made[0], made[1])
            row.append((made[2], made[3]))
        sums.append(row)
    inflow = [(zero, zero), (zero, zero)]
    for t in reversed(range(count)):
        for tile in range(2):
            one, two = inflow[tile]
            for k, value in ((2, one), (3, two)):
                if tile == 0:
                    out_ref[t * 8 + k : t * 8 + k + 1, :] = value
                else:
                    four_ref[k, t : t + 1, :] = value
            inflow[tile] = tuple(
                sums[t][tile][k - 2]
                + take(coef_ref, k * 4 + 2, tile, t) * one
                + take(coef_ref, k * 4 + 3, tile, t) * two
                for k in (2, 3)
            )
    out_ref[pl.ds(4, count, stride=8), :] = by_quarter(
        lane, [quarter_move(four_ref[k], 0, k) for k in range(4)]
    )
    for k in (5, 6, 7):
        out_ref[pl.ds(k, count, stride=8), :] = jnp.zeros((count, 128), F32)


def final_kernel(cells, f_ref, in_ref, coef_ref, cons_mat, out_ref, shift_ref):
    _, lane = iotas()
    inflow = []
    for k in range(4):
        parts = [in_ref[pl.ds(q * 64 + k, 8, stride=8), :] for q in range(4)]
        inflow.append(
            [by_quarter(lane, [quarter_move(parts[q], u, q) for q in range(4)]) for u in range(4)]
        )
    parts = [in_ref[pl.ds(q * 64 + 4, 8, stride=8), :] for q in range(4)]
    for k in range(4):
        inflow[k].append(by_quarter(lane, [quarter_move(parts[q], k, q) for q in range(4)]))

    def forward(i, carry):
        one, two = carry
        new = []
        for n, s in enumerate(SYSTEM):
            value = -(coef_ref[s * 5 + 1, i] * two[n]) - coef_ref[s * 5, i] * one[n]
            shift_ref[n, layer_at(i), :] = f_ref[n, layer_at(i), :] + value
            new.append(value)
        return new, one

    lax.fori_loop(0, cells, forward, (inflow[0], inflow[1]), unroll=UNROLL)

    def backward(step, carry):
        i = cells - 1 - step
        one, two = carry
        new = [
            shift_ref[n, layer_at(i), :] - coef_ref[s * 5 + 4, i] * two[n] - coef_ref[s * 5 + 3, i] * one[n]
            for n, s in enumerate(SYSTEM)
        ]
        for n in range(5):
            out_ref[layer_at(n * cells + i), :] = sum(cons_mat[n, v] * new[v] for v in range(5))
        return new, one

    lax.fori_loop(0, cells, backward, (inflow[2], inflow[3]), unroll=UNROLL)


def shaped(*shape):
    return jax.ShapeDtypeStruct(shape, F32)


def kept(*shape):
    return pltpu.VMEM(shape, F32)


def near(x):
    return pltpu.with_memory_space_constraint(x, pltpu.VMEM)


def near_scalars(x):
    return pltpu.with_memory_space_constraint(x, pltpu.SMEM)


VMEM = pl.BlockSpec(memory_space=pltpu.VMEM)
SMEM = pl.BlockSpec(memory_space=pltpu.SMEM)
ANY = pl.BlockSpec(memory_space=pl.ANY)


def on_device(state, time_step, to_char, to_cons, lower_bands, upper_bands):
    cells = state.shape[1]
    count = lax.axis_size("sec")
    columns = lax.axis_size("cross")
    flat = state.reshape(5, cells, 4, 2, 128).transpose(0, 1, 3, 2, 4).reshape(5 * cells * 8, 128)
    steps = time_step.reshape(cells, 4, 2, 128).transpose(0, 2, 1, 3).reshape(cells * 8, 128)
    block = (5, cells * 8, 128)
    edge, last, first, padded, steps, step_edge, coef, char_mat, cons_mat = pl.pallas_call(
        lambda *refs: edges_kernel(cells, *refs),
        out_shape=(
            kept(40, 128),
            kept(80, 128),
            kept(80, 128),
            kept(5, (cells + 4) * 8, 128),
            kept(cells * 8, 128),
            kept(*TILE),
            pltpu.SMEM((16, 128), F32),
            pltpu.SMEM((5, 5), F32),
            pltpu.SMEM((5, 5), F32),
        ),
        in_specs=[ANY] * 6,
        out_specs=(VMEM,) * 6 + (SMEM,) * 3,
        scratch_shapes=[
            pltpu.VMEM(lower_bands.shape, F32),
            pltpu.VMEM(upper_bands.shape, F32),
            pltpu.VMEM((16, 128), F32),
            pltpu.SemaphoreType.DMA((5,)),
            pltpu.SemaphoreType.DMA((6,)),
        ],
        name="edges",
    )(flat, steps, lower_bands, upper_bands, to_char, to_cons)
    coef, char_mat, cons_mat = near_scalars(coef), near_scalars(char_mat), near_scalars(cons_mat)
    up = [(i, i + 1) for i in range(count - 1)]
    right = [(i, i + 1) for i in range(columns - 1)]
    before = near(lax.ppermute(last, "sec", up))
    west = near(lax.ppermute(edge, "cross", right))
    after = near(lax.ppermute(first, "sec", [(j, i) for i, j in up]))
    east = near(lax.ppermute(edge, "cross", [(j, i) for i, j in right]))
    char, response = pl.pallas_call(
        lambda *refs: inner_kernel(cells, *refs),
        out_shape=(kept(*block), kept(*TILE)),
        in_specs=[VMEM] * 2 + [SMEM] * 2,
        out_specs=(VMEM, VMEM),
        scratch_shapes=[pltpu.VMEM((3, cells * 8, 128), F32)],
        name="inner",
    )(near(padded), near(steps), coef, char_mat)
    ends, swept = pl.pallas_call(
        lambda *refs: local_kernel(cells, *refs),
        out_shape=(kept(256, 128), kept(*block)),
        in_specs=[VMEM] * 8 + [SMEM] * 2,
        out_specs=(VMEM, VMEM),
        name="local",
    )(near(char), near(response), near(steps), near(step_edge), before, after, west, east, coef, char_mat)
    ends = lax.all_to_all(ends, "sec", 0, 0, tiled=True)
    inflow = pl.pallas_call(
        lambda *refs: reduced_kernel(count, *refs),
        out_shape=kept(256, 128),
        in_specs=[VMEM],
        out_specs=VMEM,
        scratch_shapes=[
            pltpu.VMEM((4, 2, count, 128), F32),
            pltpu.VMEM((16, 2, count, 128), F32),
            pltpu.VMEM((4, count, 128), F32),
        ],
        name="reduced",
    )(near(ends))
    inflow = lax.all_to_all(inflow, "sec", 0, 0, tiled=True)
    result = pl.pallas_call(
        lambda *refs: final_kernel(cells, *refs),
        out_shape=shaped(5 * cells * 8, 128),
        in_specs=[VMEM, VMEM, SMEM, SMEM],
        out_specs=VMEM,
        scratch_shapes=[pltpu.VMEM(block, F32)],
        name="final",
    )(near(swept), near(inflow), coef, cons_mat)
    return result.reshape(5, cells, 2, 4, 128).transpose(0, 1, 3, 2, 4).reshape(state.shape)


def solution(mesh):
    in_specs = (
        P(None, "sec", None, "cross"),
        P("sec", None, "cross"),
        P(),
        P(),
        P(None, None, "sec"),
        P(None, None, "sec"),
    )
    out_specs = P(None, "sec", None, "cross")
    return jax.shard_map(
        on_device, mesh=mesh, in_specs=in_specs, out_specs=out_specs, check_vma=False
    )
```

time: 59 us -> 49.4 us (0.84)
  Pallas kernels: 13.3 us -> 7.72 us
  waiting for transfers between devices: 4.01 us -> 2.16 us
  blocking collectives: 29.2 us -> 27.8 us
  local copies, waits for them, and re-layouts: 0.62 us -> 0 us
    pallas_call x3 -> x4, Pallas kernels: 9.97 us -> 5.26 us  [the longest x1 1.98 us: on_device(): pl.pallas_call(lambda *refs: edges_kernel(cells, *refs), out_shape=(kept(...]
    ppermute x4, waiting for transfers between devices: 4.01 us -> 2.16 us  [the longest x1 2.15 us: on_device(): west = near(lax.ppermute(edge, 'cross', right))]
    all_to_all x1, blocking collectives: 12.3 us -> 11.3 us  [on_device(): inflow = lax.all_to_all(inflow, 'sec', 0, 0, tiled=True)]
    pallas_call x1, Pallas kernels: 3.37 us -> 2.46 us  [on_device(): pl.pallas_call(lambda *refs: final_kernel(cells, *refs), out_shape=shaped...]
    unnamed x8 -> x0, local copies, waits for them, and re-layouts: 0.62 us -> none
  transfers between devices with their start and end apart: 4 -> 4, of which waited for: 1 -> 1; matrix products, arithmetic and copies ran while one was open for 0% -> 0% of each run, Pallas kernels for 0% -> 3%
where the time goes in v2:
time: 49.4 us; the launch traced here: 49.2 us
  blocking collectives  27.8 us (56%)
  starting transfers between devices  11.4 us (23%)
  Pallas kernels  7.72 us (16%)
  waiting for transfers between devices  2.16 us (4%)
    all_to_all x1, blocking collectives, on_device(): ends = lax.all_to_all(ends, 'sec', 0, 0, tiled=True)  16.6 us
    all_to_all x1, blocking collectives, on_device(): inflow = lax.all_to_all(inflow, 'sec', 0, 0, tiled=True)  11.3 us
    ppermute x1, starting transfers between devices, on_device(): east = near(lax.ppermute(edge, 'cross', [(j, i) for i, j in right]))  3.85 us
    ppermute x1, starting transfers between devices, on_device(): before = near(lax.ppermute(last, 'sec', up))  3.68 us
    pallas_call x1, Pallas kernels, on_device(): pl.pallas_call(lambda *refs: final_kernel(cells, *refs), out_shape=shaped...  2.46 us
    ppermute x1, waiting for transfers between devices, on_device(): west = near(lax.ppermute(edge, 'cross', right))  2.15 us
    pallas_call x1, Pallas kernels, on_device(): pl.pallas_call(lambda *refs: edges_kernel(cells, *refs), out_shape=(kept(...  1.98 us
    ppermute x1, starting transfers between devices, on_device(): after = near(lax.ppermute(first, 'sec', [(j, i) for i, j in up]))  1.92 us
  transfers between devices with their start and end apart: 4, of which 1 were waited for; matrix products, arithmetic and copies ran while one was open for 0% of the time, Pallas kernels for 3%

profile of v2, /device:TPU:385, one launch (start us, length us, event | category | flops | bytes accessed | tf_op | source)
XLA Modules:
  0.0 49.2 jit_solution(8707434014836662809)
XLA Ops:
  0.0 2.0 %edges.1 = (f32[40,128]{1,0:T(8,128)S(1)}, f32[80,128]{1,0:T(8,128)S(1)}, f32[80,128]{1,0:T(8,128)S(1)}, f32[5,288,128]{2,1,0:T(8,128)S(1)}, f32[256,128]{1,0:T(...) custom-call(f32[1280,128]{1,0:T(8,128)} %bitcast.23, ...), custom_call_target="tpu_custom_call" | custom-call | tf_op jit(solution)/shard_map/edges/pallas_call | solution.py:393
  2.0 3.7 %collective-permute-start = (f32[80,128]{1,0:T(8,128)S(1)}, f32[80,128]{1,0:T(8,128)S(1)}, u32[]{:S(2)}, u32[]{:S(2)}) collective-permute-start(f32[80,128]{1,0:T(8,128)S(1)} %get-tuple-element.25), channel_id=1, source_target_pairs={{0,16},{16,32},{32,48},{48,64},{64,80},{80,96},{96,112},{112,128},... | collective-permute-start | bytes 122888 | tf_op jit(solution)/shard_map/ppermute | solution.py:420
  5.7 1.9 %collective-permute-start.1 = (f32[80,128]{1,0:T(8,128)S(1)}, f32[80,128]{1,0:T(8,128)S(1)}, u32[]{:S(2)}, u32[]{:S(2)}) collective-permute-start(f32[80,128]{1,0:T(8,128)S(1)} %get-tuple-element.26), channel_id=1, source_target_pairs={{16,0},{32,16},{48,32},{64,48},{80,64},{96,80},{112,96},{128,112},... | collective-permute-start | bytes 122888 | tf_op jit(solution)/shard_map/ppermute | solution.py:422
  7.6 3.8 %collective-permute-start.3 = (f32[40,128]{1,0:T(8,128)S(1)}, f32[40,128]{1,0:T(8,128)S(1)}, u32[]{:S(2)}, u32[]{:S(2)}) collective-permute-start(f32[40,128]{1,0:T(8,128)S(1)} %get-tuple-element.27), channel_id=1, source_target_pairs={{1,0},{2,1},{3,2},{4,3},{5,4},{6,5},{7,6},{8,7},{9,8},{10,9},{11,1... | collective-permute-start | bytes 61448 | tf_op jit(solution)/shard_map/ppermute | solution.py:423
  11.5 1.9 %collective-permute-start.2 = (f32[40,128]{1,0:T(8,128)S(1)}, f32[40,128]{1,0:T(8,128)S(1)}, u32[]{:S(2)}, u32[]{:S(2)}) collective-permute-start(f32[40,128]{1,0:T(8,128)S(1)} %get-tuple-element.27), channel_id=1, source_target_pairs={{0,1},{1,2},{2,3},{3,4},{4,5},{5,6},{6,7},{7,8},{8,9},{9,10},{10,1... | collective-permute-start | bytes 61448 | tf_op jit(solution)/shard_map/ppermute | solution.py:421
  13.4 1.6 %inner.1 = (f32[5,256,128]{2,1,0:T(8,128)S(1)}, f32[8,128]{1,0:T(8,128)S(1)}) custom-call(f32[5,288,128]{2,1,0:T(8,128)S(1)} %get-tuple-element.18.refs_0_, f32[256,128]{1,0:T(8,128)S(1)} %get-tuple-element.19.refs_1_.refs_2_, f32[16,128]{1,0:T(8,128)S(4)} %get-tuple-element.20.refs_2_.refs_8_, f32[5,5]{1,0:T(8,128)S(4)} %get-tuple-element.21.refs_3_.refs_9_), custom_call_target="tpu_custom_call" | custom-call | tf_op jit(solution)/shard_map/inner/pallas_call | solution.py:424
  15.0 0.0 collective-permute-done.3.refs_7_
  15.0 2.1 %collective-permute-done.2.refs_6_ = f32[40,128]{1,0:T(8,128)S(1)} collective-permute-done((f32[40,128]{1,0:T(8,128)S(1)}, f32[40,128]{1,0:T(8,128)S(1)}, u32[]{:S(2)}, u32[]{:S(2)}) %collective-permute-start.2) | collective-permute-done | bytes 20512 | tf_op jit(solution)/shard_map/ppermute | solution.py:421
  17.2 0.0 collective-permute-done.refs_4_
  17.2 0.0 collective-permute-done.1.refs_5_
  17.2 1.1 %local.1 = (f32[256,128]{1,0:T(8,128)S(1)}, f32[5,256,128]{2,1,0:T(8,128)S(1)}) custom-call(f32[5,256,128]{2,1,0:T(8,128)S(1)} %get-tuple-element.22.refs_0_, f32[8,128]{1,0:T(8,128)S(1)} %get-tuple-element.23.refs_1_, f32[256,128]{1,0:T(8,128)S(1)} %get-tuple-element.19.refs_1_.refs_2_, f32[8,128]{1,0:T(8,128)S(1)} %get-tuple-element.24.refs_3_, ...), custom_call_target="tpu_custom_call" | custom-call | tf_op jit(solution)/shard_map/local/pallas_call | solution.py:432
  18.4 16.6 %all_to_all.22 = f32[32,8,128]{2,1,0:T(8,128)S(1)} all-to-all(f32[32,8,128]{2,1,0:T(8,128)S(1)} %bitcast.22), channel_id=1, replica_groups=mesh['sec'=32,'cross'=16] {'sec'}, dimensions={0} | all-to-all | bytes 262144 | tf_op jit(solution)/shard_map/all_to_all | solution.py:439
  34.9 0.5 %reduced.1 = f32[256,128]{1,0:T(8,128)S(1)} custom-call(f32[256,128]{1,0:T(8,128)S(1)} %bitcast.19), custom_call_target="tpu_custom_call" | custom-call | tf_op jit(solution)/shard_map/reduced/pallas_call | solution.py:440
  35.4 11.3 %all_to_all.23 = f32[32,8,128]{2,1,0:T(8,128)S(1)} all-to-all(f32[32,8,128]{2,1,0:T(8,128)S(1)} %bitcast.20), channel_id=1, replica_groups=mesh['sec'=32,'cross'=16] {'sec'}, dimensions={0} | all-to-all | bytes 262144 | tf_op jit(solution)/shard_map/all_to_all | solution.py:452
  46.7 2.5 %final.1 = f32[1280,128]{1,0:T(8,128)} custom-call(f32[5,256,128]{2,1,0:T(8,128)S(1)} %get-tuple-element.28.refs_0_, f32[256,128]{1,0:T(8,128)S(1)} %bitcast.21, f32[16,128]{1,0:T(8,128)S(4)} %get-tuple-element.20.refs_2_.refs_8_, f32[5,5]{1,0:T(8,128)S(4)} %get-tuple-element.30.refs_3_), custom_call_target="tpu_custom_call" | custom-call | tf_op jit(solution)/shard_map/final/pallas_call | solution.py:453
Async XLA Ops:
  2.0 15.2 %collective-permute-start = (f32[80,128]{1,0:T(8,128)S(1)}, f32[80,128]{1,0:T(8,128)S(1)}, u32[]{:S(2)}, u32[]{:S(2)}) collective-permute-start(f32[80,128]{1,0:T(8,128)S(1)} %get-tuple-element.25), channel_id=1, source_target_pairs={{0,16},{16,32},{32,48},{48,64},{64,80},{80,96},{96,112},{112,128},... | collective-permute-start | bytes 122888 | tf_op jit(solution)/shard_map/ppermute | solution.py:420
  5.7 11.5 %collective-permute-start.1 = (f32[80,128]{1,0:T(8,128)S(1)}, f32[80,128]{1,0:T(8,128)S(1)}, u32[]{:S(2)}, u32[]{:S(2)}) collective-permute-start(f32[80,128]{1,0:T(8,128)S(1)} %get-tuple-element.26), channel_id=1, source_target_pairs={{16,0},{32,16},{48,32},{64,48},{80,64},{96,80},{112,96},{128,112},... | collective-permute-start | bytes 122888 | tf_op jit(solution)/shard_map/ppermute | solution.py:422
  7.6 7.4 %collective-permute-start.3 = (f32[40,128]{1,0:T(8,128)S(1)}, f32[40,128]{1,0:T(8,128)S(1)}, u32[]{:S(2)}, u32[]{:S(2)}) collective-permute-start(f32[40,128]{1,0:T(8,128)S(1)} %get-tuple-element.27), channel_id=1, source_target_pairs={{1,0},{2,1},{3,2},{4,3},{5,4},{6,5},{7,6},{8,7},{9,8},{10,9},{11,1... | collective-permute-start | bytes 61448 | tf_op jit(solution)/shard_map/ppermute | solution.py:423
  11.5 5.7 %collective-permute-start.2 = (f32[40,128]{1,0:T(8,128)S(1)}, f32[40,128]{1,0:T(8,128)S(1)}, u32[]{:S(2)}, u32[]{:S(2)}) collective-permute-start(f32[40,128]{1,0:T(8,128)S(1)} %get-tuple-element.27), channel_id=1, source_target_pairs={{0,1},{1,2},{2,3},{3,4},{4,5},{5,6},{6,7},{7,8},{8,9},{9,10},{10,1... | collective-permute-start | bytes 61448 | tf_op jit(solution)/shard_map/ppermute | solution.py:421

commit v3 on v2

--- a/solution.py
+++ b/solution.py
@@ -7,6 +7,7 @@
 
 SYSTEM = (0, 0, 0, 1, 2)
 F32 = jnp.float32
+CHUNK = 16
 UNROLL = 8
 TILE = (8, 128)
 
@@ -56,7 +57,7 @@
 
 def edges_kernel(
     cells, x_hbm, dt_hbm, lower_hbm, upper_hbm, char_hbm, cons_hbm,
-    edge_ref, last_ref, first_ref, x_ref, dt_ref, dt_edge_ref, coef_ref, char_mat, cons_mat,
+    edge_ref, x_ref, dt_ref, dt_edge_ref, coef_ref, char_mat, cons_mat,
     lower_ref, upper_ref, made_ref, x_sems, sems,
 ):
     sub, _ = iotas()
@@ -97,8 +98,6 @@
         total = packed_edges(cells, lambda i, v=v: x_ref[v, pl.ds(16 + i * 8, 8), :])
         total = roll(total, 4, 0)
         packed.append(jnp.where(sub < 4, roll(total, 1, 1), roll(total, 127, 1)))
-        last_ref[pl.ds(v * 16, 16), :] = x_ref[v, pl.ds(rows, 16), :]
-        first_ref[pl.ds(v * 16, 16), :] = x_ref[v, 16:32, :]
     inv, pressure = primitives(packed)
     for v, part in enumerate(flux(packed, inv, pressure, 1)):
         edge_ref[pl.ds(v * 8, 8), :] = part
@@ -117,7 +116,7 @@
     return [sum(char_mat[u, v] * right[v] for v in range(5)) for u in range(5)]
 
 
-def inner_kernel(cells, x_ref, dt_ref, coef_ref, char_mat, char_ref, response_ref, f_ref):
+def inner_kernel(cells, x_ref, dt_ref, coef_ref, char_mat, char_ref, give_ref, response_ref, f_ref):
     sub, lane = iotas()
     third = sub % 4
 
@@ -155,13 +154,29 @@
 
     lax.fori_loop(0, cells, cell, (line(-1)[0], line(0)), unroll=UNROLL)
 
-    unit = [jnp.where((lane == n) & (sub >= 0), 1.0, 0.0).astype(F32) for n in range(4)]
-
-    def forward(i, carry):
+    top, bottom = line(0), line(cells - 1)
+    first_two, last_two = (layer(0), layer(1)), (layer(cells - 2), layer(cells - 1))
+    gives = (
+        [0.125 * (last_two[0][v] - 4.0 * last_two[1][v]) - bottom[0][v] for v in range(5)],
+        [0.125 * last_two[1][v] for v in range(5)],
+        [0.125 * first_two[0][v] for v in range(5)],
+        [0.125 * (first_two[1][v] - 4.0 * first_two[0][v]) + top[0][v] for v in range(5)],
+    )
+    for m, give in enumerate(gives):
+        for u, value in enumerate(to_char(char_mat, give)):
+            give_ref[m, u] = value
+
+    unit = [jnp.where((lane == n) & (sub >= 0), 1.0, 0.0).astype(F32) for n in range(8)]
+
+    def forward(i, carry, right=None):
         one, two = carry
-        new = [-(coef_ref[s * 5, i] * one[s]) - coef_ref[s * 5 + 1, i] * two[s] for s in range(3)]
+        new = []
         for s in range(3):
-            f_ref[s, layer_at(i), :] = new[s]
+            value = -(coef_ref[s * 5, i] * one[s]) - coef_ref[s * 5 + 1, i] * two[s]
+            if right is not None:
+                value = value + coef_ref[s * 5 + 2, i] * right
+            f_ref[s, layer_at(i), :] = value
+            new.append(value)
         return new, one
 
     def backward(step, carry):
@@ -173,37 +188,49 @@
         ]
         return new, one
 
-    last = lax.fori_loop(0, cells, forward, ([unit[0]] * 3, [unit[1]] * 3), unroll=UNROLL)
+    last = ([unit[0]] * 3, [unit[1]] * 3)
+    for i in (0, 1):
+        last = forward(i, last, unit[4 + i])
+    last = lax.fori_loop(2, cells - 2, forward, last, unroll=7)
+    for i in (0, 1):
+        last = forward(cells - 2 + i, last, unit[6 + i])
     first = lax.fori_loop(0, cells, backward, ([unit[2]] * 3, [unit[3]] * 3), unroll=UNROLL)
     ends = last + first
     response = jnp.zeros(TILE, F32)
     for s in range(3):
         for k in range(4):
-            at = (s * 4 + k) * 4
+            at = (s * 4 + k) * 8
             moved = ends[k][s] if at == 0 else roll(ends[k][s], at, 1)
-            response = jnp.where((lane >= at) & (lane < at + 4), moved, response)
+            response = jnp.where((lane >= at) & (lane < at + 8), moved, response)
     response_ref[...] = response
 
 
+def spread(out_ref, row, lane, groups):
+    for quarter in range(4):
+        for k, four in enumerate(groups):
+            out_ref[pl.ds(quarter * 8 * CHUNK + row + k, 8, stride=CHUNK), :] = by_quarter(
+                lane, [quarter_move(four[u], quarter, u) for u in range(4)]
+            )
+
+
+def with_fifth(values):
+    return [values[k][:4] for k in range(4)] + [[values[k][4] for k in range(4)]]
+
+
+def gathered(in_ref, row, lane):
+    values = []
+    for k in range(5):
+        parts = [in_ref[pl.ds(q * 8 * CHUNK + row + k, 8, stride=CHUNK), :] for q in range(4)]
+        values.append(
+            [by_quarter(lane, [quarter_move(parts[q], u, q) for q in range(4)]) for u in range(4)]
+        )
+    return [values[k] + [values[4][k]] for k in range(4)]
+
+
 def local_kernel(
-    cells, char_ref, response_ref, dt_ref, dt_edge_ref, before_ref, after_ref, west_ref, east_ref, coef_ref, char_mat,
-    out_ref, f_ref,
+    cells, char_ref, give_ref, response_ref, dt_ref, dt_edge_ref, west_ref, east_ref, coef_ref, char_mat, out_ref, f_ref
 ):
     sub, lane = iotas()
-    before = [[before_ref[pl.ds(v * 16 + n, 8), :] for v in range(5)] for n in (0, 8)]
-    after = [[after_ref[pl.ds(v * 16 + n, 8), :] for v in range(5)] for n in (0, 8)]
-    flux_before = flux(before[1], *primitives(before[1]), 0)
-    flux_after = flux(after[0], *primitives(after[0]), 0)
-    terms = (
-        (0, lambda v: 0.125 * (before[0][v] - 4.0 * before[1][v]) - flux_before[v]),
-        (1, lambda v: 0.125 * before[1][v]),
-        (cells - 2, lambda v: 0.125 * after[0][v]),
-        (cells - 1, lambda v: 0.125 * (after[1][v] - 4.0 * after[0][v]) + flux_after[v]),
-    )
-    added = {}
-    for i, term in terms:
-        scale = -0.5 * dt_ref[pl.ds(i * 8, 8), :]
-        added[i] = to_char(char_mat, [scale * term(v) for v in range(5)])
     scale = -0.5 * dt_edge_ref[...]
     beside = to_char(
         char_mat,
@@ -215,15 +242,13 @@
     outside = (lane == jnp.where(sub < 4, 0, 127)) & (sub >= 0)
     zero = jnp.where((lane < 0) & (sub < 0), 1.0, 0.0).astype(F32)
 
-    def forward(i, carry, more=None):
+    def forward(i, carry):
         one, two = carry
         new = []
         for n, s in enumerate(SYSTEM):
             char = char_ref[n, layer_at(i), :] + jnp.where(
                 outside, roll(beside[n], (128 - i) % 128, 1), 0.0
             )
-            if more:
-                char = char + more[n]
             value = coef_ref[s * 5 + 2, i] * char - coef_ref[s * 5 + 1, i] * two[n] - coef_ref[s * 5, i] * one[n]
             f_ref[n, layer_at(i), :] = value
             new.append(value)
@@ -239,45 +264,63 @@
         return new, one
 
     start = ([zero] * 5, [zero] * 5)
-    last = start
-    for i in (0, 1):
-        last = forward(i, last, added[i])
-    last = lax.fori_loop(2, cells - 2, forward, last, unroll=7)
-    for i in (cells - 2, cells - 1):
-        last = forward(i, last, added[i])
+    last = lax.fori_loop(0, cells, forward, start, unroll=UNROLL)
     first = lax.fori_loop(0, cells, backward, start, unroll=UNROLL)
-    ends = last + first
+    spread(out_ref, 0, lane, with_fifth(last + first))
+    spread(out_ref, 6, lane, with_fifth([[give_ref[m, u] for u in range(5)] for m in range(4)]))
+    spread(out_ref, 11, lane, [[-0.5 * dt_ref[pl.ds(i * 8, 8), :] for i in (0, 1, cells - 2, cells - 1)]])
     response = jnp.broadcast_to(response_ref[0:1, :], TILE)
     for quarter in range(4):
-        base = quarter * 64
-        for k in range(4):
-            out_ref[pl.ds(base + k, 8, stride=8), :] = by_quarter(
-                lane, [quarter_move(ends[k][u], quarter, u) for u in range(4)]
-            )
-        out_ref[pl.ds(base + 4, 8, stride=8), :] = by_quarter(
-            lane, [quarter_move(ends[k][4], quarter, k) for k in range(4)]
-        )
-        out_ref[pl.ds(base + 5, 8, stride=8), :] = response
-        for k in (6, 7):
-            out_ref[pl.ds(base + k, 8, stride=8), :] = jnp.zeros(TILE, F32)
+        base = quarter * 8 * CHUNK
+        out_ref[pl.ds(base + 5, 8, stride=CHUNK), :] = response
+        for k in range(12, CHUNK):
+            out_ref[pl.ds(base + k, 8, stride=CHUNK), :] = jnp.zeros(TILE, F32)
 
 
 def reduced_kernel(count, in_ref, out_ref, part_ref, coef_ref, four_ref):
     lane = lax.broadcasted_iota(jnp.int32, (count, 128), 1)
-    fifth = in_ref[pl.ds(4, count, stride=8), :]
-    response = in_ref[pl.ds(5, count, stride=8), :]
+    place = lax.broadcasted_iota(jnp.int32, (count, 128), 0)
+
+    def rows(n):
+        return in_ref[pl.ds(n, count, stride=CHUNK), :]
+
+    def put(n, value):
+        out_ref[pl.ds(n, count, stride=CHUNK), :] = value
+
+    response = rows(5)
+
+    def factor(k, c):
+        wide = []
+        for s in range(3):
+            at = (s * 4 + k) * 8 + c
+            wide.append(jnp.broadcast_to(response[:, at : at + 1], (count, 128)))
+        return jnp.where(lane < 96, wide[0], wide[1]), wide[2]
+
+    step, fifth = rows(11), rows(10)
+    added = []
+    for m in range(4):
+        scales = by_quarter(lane, [quarter_move(step, m, u) for u in range(4)])
+        pair = []
+        for give, scale in ((rows(6 + m), scales), (quarter_move(fifth, m, 0), quarter_move(step, m, 0))):
+            if m < 2:
+                give = jnp.where(place == 0, 0.0, roll(give, 1, 0))
+            else:
+                give = jnp.where(place == count - 1, 0.0, roll(give, count - 1, 0))
+            pair.append(scale * give)
+        added.append(pair)
+        put(6 + m, pair[0])
+    put(10, by_quarter(lane, [quarter_move(added[m][1], 0, m) for m in range(4)]))
+    fifth = rows(4)
     for k in range(4):
-        part_ref[k, 0] = in_ref[pl.ds(k, count, stride=8), :]
-        part_ref[k, 1] = quarter_move(fifth, k, 0)
-        for c in range(4):
-            if k < 2 and c >= 2:
-                continue
-            wide = [
-                jnp.broadcast_to(response[:, (s * 4 + k) * 4 + c : (s * 4 + k) * 4 + c + 1], (count, 128))
-                for s in range(3)
-            ]
-            coef_ref[k * 4 + c, 0] = jnp.where(lane < 96, wide[0], wide[1])
-            coef_ref[k * 4 + c, 1] = wide[2]
+        values = [rows(k), quarter_move(fifth, k, 0)]
+        for m in range(4):
+            for tile, part in enumerate(factor(k, 4 + m)):
+                values[tile] = values[tile] + part * added[m][tile]
+        for tile in range(2):
+            part_ref[k, tile] = values[tile]
+        for c in range(2 if k < 2 else 4):
+            for tile, part in enumerate(factor(k, c)):
+                coef_ref[k * 4 + c, tile] = part
     zero = jnp.zeros((1, 128), F32)
 
     def take(ref, n, tile, t):
@@ -291,7 +334,7 @@
             one, two = inflow[tile]
             for k, value in ((0, one), (1, two)):
                 if tile == 0:
-                    out_ref[t * 8 + k : t * 8 + k + 1, :] = value
+                    out_ref[t * CHUNK + k : t * CHUNK + k + 1, :] = value
                 else:
                     four_ref[k, t : t + 1, :] = value
             made = [
@@ -309,7 +352,7 @@
             one, two = inflow[tile]
             for k, value in ((2, one), (3, two)):
                 if tile == 0:
-                    out_ref[t * 8 + k : t * 8 + k + 1, :] = value
+                    out_ref[t * CHUNK + k : t * CHUNK + k + 1, :] = value
                 else:
                     four_ref[k, t : t + 1, :] = value
             inflow[tile] = tuple(
@@ -318,35 +361,33 @@
                 + take(coef_ref, k * 4 + 3, tile, t) * two
                 for k in (2, 3)
             )
-    out_ref[pl.ds(4, count, stride=8), :] = by_quarter(
-        lane, [quarter_move(four_ref[k], 0, k) for k in range(4)]
-    )
-    for k in (5, 6, 7):
-        out_ref[pl.ds(k, count, stride=8), :] = jnp.zeros((count, 128), F32)
+    put(4, by_quarter(lane, [quarter_move(four_ref[k], 0, k) for k in range(4)]))
+    for k in (5,) + tuple(range(11, CHUNK)):
+        put(k, jnp.zeros((count, 128), F32))
 
 
 def final_kernel(cells, f_ref, in_ref, coef_ref, cons_mat, out_ref, shift_ref):
     _, lane = iotas()
-    inflow = []
-    for k in range(4):
-        parts = [in_ref[pl.ds(q * 64 + k, 8, stride=8), :] for q in range(4)]
-        inflow.append(
-            [by_quarter(lane, [quarter_move(parts[q], u, q) for q in range(4)]) for u in range(4)]
-        )
-    parts = [in_ref[pl.ds(q * 64 + 4, 8, stride=8), :] for q in range(4)]
-    for k in range(4):
-        inflow[k].append(by_quarter(lane, [quarter_move(parts[q], k, q) for q in range(4)]))
-
-    def forward(i, carry):
+    inflow = gathered(in_ref, 0, lane)
+    added = gathered(in_ref, 6, lane)
+
+    def forward(i, carry, right=None):
         one, two = carry
         new = []
         for n, s in enumerate(SYSTEM):
             value = -(coef_ref[s * 5 + 1, i] * two[n]) - coef_ref[s * 5, i] * one[n]
+            if right is not None:
+                value = value + coef_ref[s * 5 + 2, i] * right[n]
             shift_ref[n, layer_at(i), :] = f_ref[n, layer_at(i), :] + value
             new.append(value)
         return new, one
 
-    lax.fori_loop(0, cells, forward, (inflow[0], inflow[1]), unroll=UNROLL)
+    last = (inflow[0], inflow[1])
+    for i in (0, 1):
+        last = forward(i, last, added[i])
+    last = lax.fori_loop(2, cells - 2, forward, last, unroll=7)
+    for i in (0, 1):
+        last = forward(cells - 2 + i, last, added[2 + i])
 
     def backward(step, carry):
         i = cells - 1 - step
@@ -390,12 +431,10 @@
     flat = state.reshape(5, cells, 4, 2, 128).transpose(0, 1, 3, 2, 4).reshape(5 * cells * 8, 128)
     steps = time_step.reshape(cells, 4, 2, 128).transpose(0, 2, 1, 3).reshape(cells * 8, 128)
     block = (5, cells * 8, 128)
-    edge, last, first, padded, steps, step_edge, coef, char_mat, cons_mat = pl.pallas_call(
+    edge, padded, steps, step_edge, coef, char_mat, cons_mat = pl.pallas_call(
         lambda *refs: edges_kernel(cells, *refs),
         out_shape=(
             kept(40, 128),
-            kept(80, 128),
-            kept(80, 128),
             kept(5, (cells + 4) * 8, 128),
             kept(cells * 8, 128),
             kept(*TILE),
@@ -404,7 +443,7 @@
             pltpu.SMEM((5, 5), F32),
         ),
         in_specs=[ANY] * 6,
-        out_specs=(VMEM,) * 6 + (SMEM,) * 3,
+        out_specs=(VMEM,) * 4 + (SMEM,) * 3,
         scratch_shapes=[
             pltpu.VMEM(lower_bands.shape, F32),
             pltpu.VMEM(upper_bands.shape, F32),
@@ -415,31 +454,28 @@
         name="edges",
     )(flat, steps, lower_bands, upper_bands, to_char, to_cons)
     coef, char_mat, cons_mat = near_scalars(coef), near_scalars(char_mat), near_scalars(cons_mat)
-    up = [(i, i + 1) for i in range(count - 1)]
     right = [(i, i + 1) for i in range(columns - 1)]
-    before = near(lax.ppermute(last, "sec", up))
     west = near(lax.ppermute(edge, "cross", right))
-    after = near(lax.ppermute(first, "sec", [(j, i) for i, j in up]))
     east = near(lax.ppermute(edge, "cross", [(j, i) for i, j in right]))
-    char, response = pl.pallas_call(
+    char, give, response = pl.pallas_call(
         lambda *refs: inner_kernel(cells, *refs),
-        out_shape=(kept(*block), kept(*TILE)),
+        out_shape=(kept(*block), kept(4, 5, *TILE), kept(*TILE)),
         in_specs=[VMEM] * 2 + [SMEM] * 2,
-        out_specs=(VMEM, VMEM),
+        out_specs=(VMEM,) * 3,
         scratch_shapes=[pltpu.VMEM((3, cells * 8, 128), F32)],
         name="inner",
     )(near(padded), near(steps), coef, char_mat)
     ends, swept = pl.pallas_call(
         lambda *refs: local_kernel(cells, *refs),
-        out_shape=(kept(256, 128), kept(*block)),
-        in_specs=[VMEM] * 8 + [SMEM] * 2,
+        out_shape=(kept(count * CHUNK, 128), kept(*block)),
+        in_specs=[VMEM] * 7 + [SMEM] * 2,
         out_specs=(VMEM, VMEM),
         name="local",
-    )(near(char), near(response), near(steps), near(step_edge), before, after, west, east, coef, char_mat)
+    )(near(char), near(give), near(response), near(steps), near(step_edge), west, east, coef, char_mat)
     ends = lax.all_to_all(ends, "sec", 0, 0, tiled=True)
     inflow = pl.pallas_call(
         lambda *refs: reduced_kernel(count, *refs),
-        out_shape=kept(256, 128),
+        out_shape=kept(count * CHUNK, 128),
         in_specs=[VMEM],
         out_specs=VMEM,
         scratch_shapes=[

time: 49.4 us -> 46.6 us (0.943)
  starting transfers between devices: 11.4 us -> 5.77 us
  blocking collectives: 27.8 us -> 30.3 us
    ppermute x2 -> x0, starting transfers between devices: 5.6 us -> none  [the longest x1 3.68 us: on_device(): before = near(lax.ppermute(last, 'sec', up))]
    all_to_all x1, blocking collectives: 16.6 us -> 17.9 us  [on_device(): ends = lax.all_to_all(ends, 'sec', 0, 0, tiled=True)]
    all_to_all x1, blocking collectives: 11.3 us -> 12.5 us  [on_device(): inflow = lax.all_to_all(inflow, 'sec', 0, 0, tiled=True)]
  transfers between devices with their start and end apart: 4 -> 2, of which waited for: 1 -> 1; matrix products, arithmetic and copies ran while one was open for 0% -> 0% of each run, Pallas kernels for 3% -> 4%
where the time goes in v3:
time: 46.6 us; the launch traced here: 46.4 us
  blocking collectives  30.3 us (65%)
  Pallas kernels  8.12 us (17%)
  starting transfers between devices  5.77 us (12%)
  waiting for transfers between devices  2.09 us (4%)
    all_to_all x1, blocking collectives, on_device(): ends = lax.all_to_all(ends, 'sec', 0, 0, tiled=True)  17.9 us
    all_to_all x1, blocking collectives, on_device(): inflow = lax.all_to_all(inflow, 'sec', 0, 0, tiled=True)  12.5 us
    ppermute x1, starting transfers between devices, on_device(): east = near(lax.ppermute(edge, 'cross', [(j, i) for i, j in right]))  3.85 us
    pallas_call x1, Pallas kernels, on_device(): pl.pallas_call(lambda *refs: final_kernel(cells, *refs), out_shape=shaped...  2.52 us
    ppermute x1, waiting for transfers between devices, on_device(): west = near(lax.ppermute(edge, 'cross', right))  2.09 us
    pallas_call x1, Pallas kernels, on_device(): pl.pallas_call(lambda *refs: edges_kernel(cells, *refs), out_shape=(kept(...  1.98 us
    ppermute x1, starting transfers between devices, on_device(): west = near(lax.ppermute(edge, 'cross', right))  1.92 us
    pallas_call x1, Pallas kernels, on_device(): pl.pallas_call(lambda *refs: inner_kernel(cells, *refs), out_shape=(kept(...  1.7 us
  transfers between devices with their start and end apart: 2, of which 1 were waited for; matrix products, arithmetic and copies ran while one was open for 0% of the time, Pallas kernels for 4%

profile of v3, /device:TPU:385, one launch (start us, length us, event | category | flops | bytes accessed | tf_op | source)
XLA Modules:
  0.0 46.4 jit_solution(9859870215744941166)
XLA Ops:
  0.0 2.0 %edges.1 = (f32[40,128]{1,0:T(8,128)S(1)}, f32[5,288,128]{2,1,0:T(8,128)S(1)}, f32[256,128]{1,0:T(8,128)S(1)}, f32[8,128]{1,0:T(8,128)S(1)}, f32[16,128]{1,0:T(8...) custom-call(f32[1280,128]{1,0:T(8,128)} %bitcast.23, f32[256,128]{1,0:T(8,128)} %bitcast.24, f32[3,3,32]{2,1,0:T(4,128)} %refs_2_.1, ...), custom_call_target="tpu_custom_call" | custom-call | tf_op jit(solution)/shard_map/edges/pallas_call | solution.py:434
  2.0 3.8 %collective-permute-start.1 = (f32[40,128]{1,0:T(8,128)S(1)}, f32[40,128]{1,0:T(8,128)S(1)}, u32[]{:S(2)}, u32[]{:S(2)}) collective-permute-start(f32[40,128]{1,0:T(8,128)S(1)} %get-tuple-element.25), channel_id=1, source_target_pairs={{1,0},{2,1},{3,2},{4,3},{5,4},{6,5},{7,6},{8,7},{9,8},{10,9},{11,1... | collective-permute-start | bytes 61448 | tf_op jit(solution)/shard_map/ppermute | solution.py:459
  5.8 1.9 %collective-permute-start = (f32[40,128]{1,0:T(8,128)S(1)}, f32[40,128]{1,0:T(8,128)S(1)}, u32[]{:S(2)}, u32[]{:S(2)}) collective-permute-start(f32[40,128]{1,0:T(8,128)S(1)} %get-tuple-element.25), channel_id=1, source_target_pairs={{0,1},{1,2},{2,3},{3,4},{4,5},{5,6},{6,7},{7,8},{8,9},{9,10},{10,1... | collective-permute-start | bytes 61448 | tf_op jit(solution)/shard_map/ppermute | solution.py:458
  7.8 1.7 %inner.1 = (f32[5,256,128]{2,1,0:T(8,128)S(1)}, f32[4,5,8,128]{3,2,1,0:T(8,128)S(1)}, f32[8,128]{1,0:T(8,128)S(1)}) custom-call(f32[5,288,128]{2,1,0:T(8,128)S(1)} %get-tuple-element.17.refs_0_, f32[256,128]{1,0:T(8,128)S(1)} %get-tuple-element.18.refs_1_.refs_3_, f32[16,128]{1,0:T(8,128)S(4)} %get-tuple-element.19.refs_2_.refs_7_, ...), custom_call_target="tpu_custom_call" | custom-call | tf_op jit(solution)/shard_map/inner/pallas_call | solution.py:460
  9.5 0.0 collective-permute-done.1.refs_6_
  9.5 2.1 %collective-permute-done.refs_5_ = f32[40,128]{1,0:T(8,128)S(1)} collective-permute-done((f32[40,128]{1,0:T(8,128)S(1)}, f32[40,128]{1,0:T(8,128)S(1)}, u32[]{:S(2)}, u32[]{:S(2)}) %collective-permute-start) | collective-permute-done | bytes 20512 | tf_op jit(solution)/shard_map/ppermute | solution.py:458
  11.6 1.1 %local.1 = (f32[512,128]{1,0:T(8,128)S(1)}, f32[5,256,128]{2,1,0:T(8,128)S(1)}) custom-call(f32[5,256,128]{2,1,0:T(8,128)S(1)} %get-tuple-element.21.refs_0_, f32[4,5,8,128]{3,2,1,0:T(8,128)S(1)} %get-tuple-element.22.refs_1_, f32[8,128]{1,0:T(8,128)S(1)} %get-tuple-element.23.refs_2_, f32[256,128]{1,0:T(8,128)S(1)} %get-tuple-element.18.refs_1_.refs_3_, ...), custom_call_target="tpu_custom_call" | custom-call | tf_op jit(solution)/shard_map/local/pallas_call | solution.py:468
  12.7 17.9 %all_to_all.22 = f32[32,16,128]{2,1,0:T(8,128)S(1)} all-to-all(f32[32,16,128]{2,1,0:T(8,128)S(1)} %bitcast.22), channel_id=1, replica_groups=mesh['sec'=32,'cross'=16] {'sec'}, dimensions={0} | all-to-all | bytes 524288 | tf_op jit(solution)/shard_map/all_to_all | solution.py:475
  30.6 0.8 %reduced.1 = f32[512,128]{1,0:T(8,128)S(1)} custom-call(f32[512,128]{1,0:T(8,128)S(1)} %bitcast.19), custom_call_target="tpu_custom_call" | custom-call | tf_op jit(solution)/shard_map/reduced/pallas_call | solution.py:476
  31.4 12.5 %all_to_all.23 = f32[32,16,128]{2,1,0:T(8,128)S(1)} all-to-all(f32[32,16,128]{2,1,0:T(8,128)S(1)} %bitcast.20), channel_id=1, replica_groups=mesh['sec'=32,'cross'=16] {'sec'}, dimensions={0} | all-to-all | bytes 524288 | tf_op jit(solution)/shard_map/all_to_all | solution.py:488
  43.9 2.5 %final.1 = f32[1280,128]{1,0:T(8,128)} custom-call(f32[5,256,128]{2,1,0:T(8,128)S(1)} %get-tuple-element.26.refs_0_, f32[512,128]{1,0:T(8,128)S(1)} %bitcast.21, f32[16,128]{1,0:T(8,128)S(4)} %get-tuple-element.19.refs_2_.refs_7_, f32[5,5]{1,0:T(8,128)S(4)} %get-tuple-element.28.refs_3_), custom_call_target="tpu_custom_call" | custom-call | tf_op jit(solution)/shard_map/final/pallas_call | solution.py:489
Async XLA Ops:
  2.0 7.5 %collective-permute-start.1 = (f32[40,128]{1,0:T(8,128)S(1)}, f32[40,128]{1,0:T(8,128)S(1)}, u32[]{:S(2)}, u32[]{:S(2)}) collective-permute-start(f32[40,128]{1,0:T(8,128)S(1)} %get-tuple-element.25), channel_id=1, source_target_pairs={{1,0},{2,1},{3,2},{4,3},{5,4},{6,5},{7,6},{8,7},{9,8},{10,9},{11,1... | collective-permute-start | bytes 61448 | tf_op jit(solution)/shard_map/ppermute | solution.py:459
  5.8 5.7 %collective-permute-start = (f32[40,128]{1,0:T(8,128)S(1)}, f32[40,128]{1,0:T(8,128)S(1)}, u32[]{:S(2)}, u32[]{:S(2)}) collective-permute-start(f32[40,128]{1,0:T(8,128)S(1)} %get-tuple-element.25), channel_id=1, source_target_pairs={{0,1},{1,2},{2,3},{3,4},{4,5},{5,6},{6,7},{7,8},{8,9},{9,10},{10,1... | collective-permute-start | bytes 61448 | tf_op jit(solution)/shard_map/ppermute | solution.py:458

commit v4 on v3

--- a/solution.py
+++ b/solution.py
@@ -7,8 +7,9 @@
 
 SYSTEM = (0, 0, 0, 1, 2)
 F32 = jnp.float32
-CHUNK = 16
-UNROLL = 8
+OUT = 12
+BACK = 10
+UNROLL = 32
 TILE = (8, 128)
 
 
@@ -208,7 +209,7 @@
 def spread(out_ref, row, lane, groups):
     for quarter in range(4):
         for k, four in enumerate(groups):
-            out_ref[pl.ds(quarter * 8 * CHUNK + row + k, 8, stride=CHUNK), :] = by_quarter(
+            out_ref[pl.ds(quarter * 8 * OUT + row + k, 8, stride=OUT), :] = by_quarter(
                 lane, [quarter_move(four[u], quarter, u) for u in range(4)]
             )
 
@@ -220,7 +221,7 @@
 def gathered(in_ref, row, lane):
     values = []
     for k in range(5):
-        parts = [in_ref[pl.ds(q * 8 * CHUNK + row + k, 8, stride=CHUNK), :] for q in range(4)]
+        parts = [in_ref[pl.ds(q * 8 * BACK + row + k, 8, stride=BACK), :] for q in range(4)]
         values.append(
             [by_quarter(lane, [quarter_move(parts[q], u, q) for q in range(4)]) for u in range(4)]
         )
@@ -271,10 +272,7 @@
     spread(out_ref, 11, lane, [[-0.5 * dt_ref[pl.ds(i * 8, 8), :] for i in (0, 1, cells - 2, cells - 1)]])
     response = jnp.broadcast_to(response_ref[0:1, :], TILE)
     for quarter in range(4):
-        base = quarter * 8 * CHUNK
-        out_ref[pl.ds(base + 5, 8, stride=CHUNK), :] = response
-        for k in range(12, CHUNK):
-            out_ref[pl.ds(base + k, 8, stride=CHUNK), :] = jnp.zeros(TILE, F32)
+        out_ref[pl.ds(quarter * 8 * OUT + 5, 8, stride=OUT), :] = response
 
 
 def reduced_kernel(count, in_ref, out_ref, part_ref, coef_ref, four_ref):
@@ -282,10 +280,10 @@
     place = lax.broadcasted_iota(jnp.int32, (count, 128), 0)
 
     def rows(n):
-        return in_ref[pl.ds(n, count, stride=CHUNK), :]
+        return in_ref[pl.ds(n, count, stride=OUT), :]
 
     def put(n, value):
-        out_ref[pl.ds(n, count, stride=CHUNK), :] = value
+        out_ref[pl.ds(n, count, stride=BACK), :] = value
 
     response = rows(5)
 
@@ -308,8 +306,8 @@
                 give = jnp.where(place == count - 1, 0.0, roll(give, count - 1, 0))
             pair.append(scale * give)
         added.append(pair)
-        put(6 + m, pair[0])
-    put(10, by_quarter(lane, [quarter_move(added[m][1], 0, m) for m in range(4)]))
+        put(5 + m, pair[0])
+    put(9, by_quarter(lane, [quarter_move(added[m][1], 0, m) for m in range(4)]))
     fifth = rows(4)
     for k in range(4):
         values = [rows(k), quarter_move(fifth, k, 0)]
@@ -334,7 +332,7 @@
             one, two = inflow[tile]
             for k, value in ((0, one), (1, two)):
                 if tile == 0:
-                    out_ref[t * CHUNK + k : t * CHUNK + k + 1, :] = value
+                    out_ref[t * BACK + k : t * BACK + k + 1, :] = value
                 else:
                     four_ref[k, t : t + 1, :] = value
             made = [
@@ -352,7 +350,7 @@
             one, two = inflow[tile]
             for k, value in ((2, one), (3, two)):
                 if tile == 0:
-                    out_ref[t * CHUNK + k : t * CHUNK + k + 1, :] = value
+                    out_ref[t * BACK + k : t * BACK + k + 1, :] = value
                 else:
                     four_ref[k, t : t + 1, :] = value
             inflow[tile] = tuple(
@@ -362,14 +360,12 @@
                 for k in (2, 3)
             )
     put(4, by_quarter(lane, [quarter_move(four_ref[k], 0, k) for k in range(4)]))
-    for k in (5,) + tuple(range(11, CHUNK)):
-        put(k, jnp.zeros((count, 128), F32))
 
 
 def final_kernel(cells, f_ref, in_ref, coef_ref, cons_mat, out_ref, shift_ref):
     _, lane = iotas()
     inflow = gathered(in_ref, 0, lane)
-    added = gathered(in_ref, 6, lane)
+    added = gathered(in_ref, 5, lane)
 
     def forward(i, carry, right=None):
         one, two = carry
@@ -413,6 +409,11 @@
 
 def near(x):
     return pltpu.with_memory_space_constraint(x, pltpu.VMEM)
+
+
+def exchanged(x, count):
+    chunks = x.reshape(count, 1, x.size // count)
+    return lax.all_to_all(chunks, "sec", 0, 0, tiled=True).reshape(x.shape)
 
 
 def near_scalars(x):
@@ -467,15 +468,15 @@
     )(near(padded), near(steps), coef, char_mat)
     ends, swept = pl.pallas_call(
         lambda *refs: local_kernel(cells, *refs),
-        out_shape=(kept(count * CHUNK, 128), kept(*block)),
+        out_shape=(kept(count * OUT, 128), kept(*block)),
         in_specs=[VMEM] * 7 + [SMEM] * 2,
         out_specs=(VMEM, VMEM),
         name="local",
     )(near(char), near(give), near(response), near(steps), near(step_edge), west, east, coef, char_mat)
-    ends = lax.all_to_all(ends, "sec", 0, 0, tiled=True)
+    ends = exchanged(ends, count)
     inflow = pl.pallas_call(
         lambda *refs: reduced_kernel(count, *refs),
-        out_shape=kept(count * CHUNK, 128),
+        out_shape=kept(count * BACK, 128),
         in_specs=[VMEM],
         out_specs=VMEM,
         scratch_shapes=[
@@ -485,7 +486,7 @@
         ],
         name="reduced",
     )(near(ends))
-    inflow = lax.all_to_all(inflow, "sec", 0, 0, tiled=True)
+    inflow = exchanged(inflow, count)
     result = pl.pallas_call(
         lambda *refs: final_kernel(cells, *refs),
         out_shape=shaped(5 * cells * 8, 128),

time: 46.6 us -> 44 us (0.944)
  blocking collectives: 30.3 us -> 28.8 us
  Pallas kernels: 8.12 us -> 6.88 us
    all_to_all x2, blocking collectives: 30.3 us -> 28.8 us  [exchanged(): return lax.all_to_all(chunks, 'sec', 0, 0, tiled=True).reshape(x.shape)]
    pallas_call x1, Pallas kernels: 2.52 us -> 1.78 us  [on_device(): pl.pallas_call(lambda *refs: final_kernel(cells, *refs), out_shape=shaped...]
  transfers between devices with their start and end apart: 2 -> 2, of which waited for: 1 -> 1; matrix products, arithmetic and copies ran while one was open for 0% -> 0% of each run, Pallas kernels for 4% -> 3%
where the time goes in v4:
time: 44 us; the launch traced here: 43.8 us
  blocking collectives  28.8 us (65%)
  Pallas kernels  6.88 us (16%)
  starting transfers between devices  5.77 us (13%)
  waiting for transfers between devices  2.28 us (5%)
    all_to_all x2, blocking collectives, exchanged(): return lax.all_to_all(chunks, 'sec', 0, 0, tiled=True).reshape(x.shape)  28.8 us
    ppermute x1, starting transfers between devices, on_device(): east = near(lax.ppermute(edge, 'cross', [(j, i) for i, j in right]))  3.85 us
    ppermute x1, waiting for transfers between devices, on_device(): west = near(lax.ppermute(edge, 'cross', right))  2.28 us
    pallas_call x1, Pallas kernels, on_device(): pl.pallas_call(lambda *refs: edges_kernel(cells, *refs), out_shape=(kept(...  1.98 us
    ppermute x1, starting transfers between devices, on_device(): west = near(lax.ppermute(edge, 'cross', right))  1.92 us
    pallas_call x1, Pallas kernels, on_device(): pl.pallas_call(lambda *refs: final_kernel(cells, *refs), out_shape=shaped...  1.78 us
    pallas_call x1, Pallas kernels, on_device(): pl.pallas_call(lambda *refs: inner_kernel(cells, *refs), out_shape=(kept(...  1.52 us
  transfers between devices with their start and end apart: 2, of which 1 were waited for; matrix products, arithmetic and copies ran while one was open for 0% of the time, Pallas kernels for 3%

profile of v4, /device:TPU:385, one launch (start us, length us, event | category | flops | bytes accessed | tf_op | source)
XLA Modules:
  0.0 43.8 jit_solution(3919972296173833641)
XLA Ops:
  0.0 2.0 %edges.1 = (f32[40,128]{1,0:T(8,128)S(1)}, f32[5,288,128]{2,1,0:T(8,128)S(1)}, f32[256,128]{1,0:T(8,128)S(1)}, f32[8,128]{1,0:T(8,128)S(1)}, f32[16,128]{1,0:T(8...) custom-call(f32[1280,128]{1,0:T(8,128)} %bitcast.23, f32[256,128]{1,0:T(8,128)} %bitcast.24, f32[3,3,32]{2,1,0:T(4,128)} %refs_2_.1, ...), custom_call_target="tpu_custom_call" | custom-call | tf_op jit(solution)/shard_map/edges/pallas_call | solution.py:435
  2.0 3.8 %collective-permute-start.1 = (f32[40,128]{1,0:T(8,128)S(1)}, f32[40,128]{1,0:T(8,128)S(1)}, u32[]{:S(2)}, u32[]{:S(2)}) collective-permute-start(f32[40,128]{1,0:T(8,128)S(1)} %get-tuple-element.25), channel_id=1, source_target_pairs={{1,0},{2,1},{3,2},{4,3},{5,4},{6,5},{7,6},{8,7},{9,8},{10,9},{11,1... | collective-permute-start | bytes 61448 | tf_op jit(solution)/shard_map/ppermute | solution.py:460
  5.8 1.9 %collective-permute-start = (f32[40,128]{1,0:T(8,128)S(1)}, f32[40,128]{1,0:T(8,128)S(1)}, u32[]{:S(2)}, u32[]{:S(2)}) collective-permute-start(f32[40,128]{1,0:T(8,128)S(1)} %get-tuple-element.25), channel_id=1, source_target_pairs={{0,1},{1,2},{2,3},{3,4},{4,5},{5,6},{6,7},{7,8},{8,9},{9,10},{10,1... | collective-permute-start | bytes 61448 | tf_op jit(solution)/shard_map/ppermute | solution.py:459
  7.8 1.5 %inner.1 = (f32[5,256,128]{2,1,0:T(8,128)S(1)}, f32[4,5,8,128]{3,2,1,0:T(8,128)S(1)}, f32[8,128]{1,0:T(8,128)S(1)}) custom-call(f32[5,288,128]{2,1,0:T(8,128)S(1)} %get-tuple-element.17.refs_0_, f32[256,128]{1,0:T(8,128)S(1)} %get-tuple-element.18.refs_1_.refs_3_, f32[16,128]{1,0:T(8,128)S(4)} %get-tuple-element.19.refs_2_.refs_7_, ...), custom_call_target="tpu_custom_call" | custom-call | tf_op jit(solution)/shard_map/inner/pallas_call | solution.py:461
  9.3 0.0 collective-permute-done.1.refs_6_
  9.3 2.3 %collective-permute-done.refs_5_ = f32[40,128]{1,0:T(8,128)S(1)} collective-permute-done((f32[40,128]{1,0:T(8,128)S(1)}, f32[40,128]{1,0:T(8,128)S(1)}, u32[]{:S(2)}, u32[]{:S(2)}) %collective-permute-start) | collective-permute-done | bytes 20512 | tf_op jit(solution)/shard_map/ppermute | solution.py:459
  11.6 0.8 %local.1 = (f32[384,128]{1,0:T(8,128)S(1)}, f32[5,256,128]{2,1,0:T(8,128)S(1)}) custom-call(f32[5,256,128]{2,1,0:T(8,128)S(1)} %get-tuple-element.21.refs_0_, f32[4,5,8,128]{3,2,1,0:T(8,128)S(1)} %get-tuple-element.22.refs_1_, f32[8,128]{1,0:T(8,128)S(1)} %get-tuple-element.23.refs_2_, f32[256,128]{1,0:T(8,128)S(1)} %get-tuple-element.18.refs_1_.refs_3_, ...), custom_call_target="tpu_custom_call" | custom-call | tf_op jit(solution)/shard_map/local/pallas_call | solution.py:469
  12.4 17.3 %all_to_all.10 = f32[32,1,1536]{2,1,0:T(1,128)S(1)} all-to-all(f32[32,1,1536]{2,1,0:T(1,128)S(1)} %bitcast.22), channel_id=1, replica_groups=mesh['sec'=32,'cross'=16] {'sec'}, dimensions={0} | all-to-all | bytes 393216 | tf_op jit(solution)/shard_map/all_to_all | solution.py:416
  29.7 0.8 %reduced.1 = f32[320,128]{1,0:T(8,128)S(1)} custom-call(f32[384,128]{1,0:T(8,128)S(1)} %bitcast.19), custom_call_target="tpu_custom_call" | custom-call | tf_op jit(solution)/shard_map/reduced/pallas_call | solution.py:477
  30.4 11.5 %all_to_all.11 = f32[32,1,1280]{2,1,0:T(1,128)S(1)} all-to-all(f32[32,1,1280]{2,1,0:T(1,128)S(1)} %bitcast.20), channel_id=1, replica_groups=mesh['sec'=32,'cross'=16] {'sec'}, dimensions={0} | all-to-all | bytes 327680 | tf_op jit(solution)/shard_map/all_to_all | solution.py:416
  42.0 1.8 %final.1 = f32[1280,128]{1,0:T(8,128)} custom-call(f32[5,256,128]{2,1,0:T(8,128)S(1)} %get-tuple-element.26.refs_0_, f32[320,128]{1,0:T(8,128)S(1)} %bitcast.21, f32[16,128]{1,0:T(8,128)S(4)} %get-tuple-element.19.refs_2_.refs_7_, f32[5,5]{1,0:T(8,128)S(4)} %get-tuple-element.28.refs_3_), custom_call_target="tpu_custom_call" | custom-call | tf_op jit(solution)/shard_map/final/pallas_call | solution.py:490
Async XLA Ops:
  2.0 7.3 %collective-permute-start.1 = (f32[40,128]{1,0:T(8,128)S(1)}, f32[40,128]{1,0:T(8,128)S(1)}, u32[]{:S(2)}, u32[]{:S(2)}) collective-permute-start(f32[40,128]{1,0:T(8,128)S(1)} %get-tuple-element.25), channel_id=1, source_target_pairs={{1,0},{2,1},{3,2},{4,3},{5,4},{6,5},{7,6},{8,7},{9,8},{10,9},{11,1... | collective-permute-start | bytes 61448 | tf_op jit(solution)/shard_map/ppermute | solution.py:460
  5.8 5.7 %collective-permute-start = (f32[40,128]{1,0:T(8,128)S(1)}, f32[40,128]{1,0:T(8,128)S(1)}, u32[]{:S(2)}, u32[]{:S(2)}) collective-permute-start(f32[40,128]{1,0:T(8,128)S(1)} %get-tuple-element.25), channel_id=1, source_target_pairs={{0,1},{1,2},{2,3},{3,4},{4,5},{5,6},{6,7},{7,8},{8,9},{9,10},{10,1... | collective-permute-start | bytes 61448 | tf_op jit(solution)/shard_map/ppermute | solution.py:459

commit v5 on v4

--- a/solution.py
+++ b/solution.py
@@ -8,7 +8,7 @@
 SYSTEM = (0, 0, 0, 1, 2)
 F32 = jnp.float32
 OUT = 12
-BACK = 10
+BACK = 12
 UNROLL = 32
 TILE = (8, 128)
 
@@ -56,12 +56,72 @@
     return total
 
 
-def edges_kernel(
+def edges_kernel(cells, x_ref, dt_ref, edge_ref, dt_edge_ref):
+    sub, _ = iotas()
+    packed = []
+    for v in range(5):
+        total = packed_edges(cells, lambda i, v=v: x_ref[v, pl.ds(16 + i * 8, 8), :])
+        total = roll(total, 4, 0)
+        packed.append(jnp.where(sub < 4, roll(total, 1, 1), roll(total, 127, 1)))
+    inv, pressure = primitives(packed)
+    for v, part in enumerate(flux(packed, inv, pressure, 1)):
+        edge_ref[pl.ds(v * 8, 8), :] = part
+    dt_edge_ref[...] = packed_edges(cells, lambda i: dt_ref[pl.ds(i * 8, 8), :])
+
+
+def layer_at(i):
+    return pl.ds(i * 8 if isinstance(i, int) else pl.multiple_of(i * 8, 8), 8)
+
+
+def to_char(char_mat, right):
+    return [sum(char_mat[u, v] * right[v] for v in range(5)) for u in range(5)]
+
+
+def spread(out_ref, row, lane, groups):
+    for quarter in range(4):
+        for k, four in enumerate(groups):
+            out_ref[pl.ds(quarter * 8 * OUT + row + k, 8, stride=OUT), :] = by_quarter(
+                lane, [quarter_move(four[u], quarter, u) for u in range(4)]
+            )
+
+
+def with_fifth(values):
+    return [values[k][:4] for k in range(4)] + [[values[k][4] for k in range(4)]]
+
+
+def gathered(in_ref, row, lane):
+    values = []
+    for k in range(5):
+        parts = [in_ref[pl.ds(q * 8 * BACK + row + k, 8, stride=BACK), :] for q in range(4)]
+        values.append(
+            [by_quarter(lane, [quarter_move(parts[q], u, q) for q in range(4)]) for u in range(4)]
+        )
+    return [values[k] + [values[4][k]] for k in range(4)]
+
+
+def outer(sub, lane):
+    return (lane == jnp.where(sub < 4, 0, 127)) & (sub >= 0)
+
+
+def swept_back(cells, f_ref, coef_ref):
+    def backward(step, carry):
+        i = cells - 1 - step
+        one, two = carry
+        new = [
+            f_ref[n, layer_at(i), :] - coef_ref[s * 5 + 4, i] * two[n] - coef_ref[s * 5 + 3, i] * one[n]
+            for n, s in enumerate(SYSTEM)
+        ]
+        return new, one
+
+    return backward
+
+
+def own_kernel(
     cells, x_hbm, dt_hbm, lower_hbm, upper_hbm, char_hbm, cons_hbm,
-    edge_ref, x_ref, dt_ref, dt_edge_ref, coef_ref, char_mat, cons_mat,
-    lower_ref, upper_ref, made_ref, x_sems, sems,
+    out_ref, f_ref, x_ref, dt_ref, coef_ref, char_mat, cons_mat,
+    char_ref, answer_ref, lower_ref, upper_ref, made_ref, x_sems, sems,
 ):
-    sub, _ = iotas()
+    sub, lane = iotas()
     rows = cells * 8
     x_copies = [
         pltpu.make_async_copy(
@@ -77,7 +137,7 @@
         (cons_hbm, cons_mat),
     )
     copies = [pltpu.make_async_copy(a, b, sems.at[n]) for n, (a, b) in enumerate(pairs)]
-    for copy in x_copies + copies:
+    for copy in copies[:2] + x_copies + copies[2:]:
         copy.start()
     for v in range(5):
         x_ref[v, 0:16] = jnp.zeros((16, 128), F32)
@@ -93,32 +153,9 @@
         made_ref[s * 5 + 3 : s * 5 + 5, 0:cells] = upper_ref[s]
     made = pltpu.make_async_copy(made_ref, coef_ref, sems.at[5])
     made.start()
-    packed = []
-    for v in range(5):
-        x_copies[v].wait()
-        total = packed_edges(cells, lambda i, v=v: x_ref[v, pl.ds(16 + i * 8, 8), :])
-        total = roll(total, 4, 0)
-        packed.append(jnp.where(sub < 4, roll(total, 1, 1), roll(total, 127, 1)))
-    inv, pressure = primitives(packed)
-    for v, part in enumerate(flux(packed, inv, pressure, 1)):
-        edge_ref[pl.ds(v * 8, 8), :] = part
-    copies[2].wait()
-    dt_edge_ref[...] = packed_edges(cells, lambda i: dt_ref[pl.ds(i * 8, 8), :])
-    copies[3].wait()
-    copies[4].wait()
-    made.wait()
-
-
-def layer_at(i):
-    return pl.ds(i * 8 if isinstance(i, int) else pl.multiple_of(i * 8, 8), 8)
-
-
-def to_char(char_mat, right):
-    return [sum(char_mat[u, v] * right[v] for v in range(5)) for u in range(5)]
-
-
-def inner_kernel(cells, x_ref, dt_ref, coef_ref, char_mat, char_ref, give_ref, response_ref, f_ref):
-    sub, lane = iotas()
+    for copy in x_copies + copies[2:] + [made]:
+        copy.wait()
+
     third = sub % 4
 
     def layer(i):
@@ -154,7 +191,6 @@
         return flux_now, (flux_after, inv_after, pressure_after)
 
     lax.fori_loop(0, cells, cell, (line(-1)[0], line(0)), unroll=UNROLL)
-
     top, bottom = line(0), line(cells - 1)
     first_two, last_two = (layer(0), layer(1)), (layer(cells - 2), layer(cells - 1))
     gives = (
@@ -163,39 +199,37 @@
         [0.125 * first_two[0][v] for v in range(5)],
         [0.125 * (first_two[1][v] - 4.0 * first_two[0][v]) + top[0][v] for v in range(5)],
     )
-    for m, give in enumerate(gives):
-        for u, value in enumerate(to_char(char_mat, give)):
-            give_ref[m, u] = value
+    gives = [to_char(char_mat, give) for give in gives]
 
     unit = [jnp.where((lane == n) & (sub >= 0), 1.0, 0.0).astype(F32) for n in range(8)]
 
-    def forward(i, carry, right=None):
+    def answer(i, carry, right=None):
         one, two = carry
         new = []
         for s in range(3):
             value = -(coef_ref[s * 5, i] * one[s]) - coef_ref[s * 5 + 1, i] * two[s]
             if right is not None:
                 value = value + coef_ref[s * 5 + 2, i] * right
-            f_ref[s, layer_at(i), :] = value
+            answer_ref[s, layer_at(i), :] = value
             new.append(value)
         return new, one
 
-    def backward(step, carry):
+    def answer_back(step, carry):
         i = cells - 1 - step
         one, two = carry
         new = [
-            f_ref[s, layer_at(i), :] - coef_ref[s * 5 + 3, i] * one[s] - coef_ref[s * 5 + 4, i] * two[s]
+            answer_ref[s, layer_at(i), :] - coef_ref[s * 5 + 3, i] * one[s] - coef_ref[s * 5 + 4, i] * two[s]
             for s in range(3)
         ]
         return new, one
 
     last = ([unit[0]] * 3, [unit[1]] * 3)
     for i in (0, 1):
-        last = forward(i, last, unit[4 + i])
-    last = lax.fori_loop(2, cells - 2, forward, last, unroll=7)
+        last = answer(i, last, unit[4 + i])
+    last = lax.fori_loop(2, cells - 2, answer, last, unroll=7)
     for i in (0, 1):
-        last = forward(cells - 2 + i, last, unit[6 + i])
-    first = lax.fori_loop(0, cells, backward, ([unit[2]] * 3, [unit[3]] * 3), unroll=UNROLL)
+        last = answer(cells - 2 + i, last, unit[6 + i])
+    first = lax.fori_loop(0, cells, answer_back, ([unit[2]] * 3, [unit[3]] * 3), unroll=UNROLL)
     ends = last + first
     response = jnp.zeros(TILE, F32)
     for s in range(3):
@@ -203,33 +237,32 @@
             at = (s * 4 + k) * 8
             moved = ends[k][s] if at == 0 else roll(ends[k][s], at, 1)
             response = jnp.where((lane >= at) & (lane < at + 8), moved, response)
-    response_ref[...] = response
-
-
-def spread(out_ref, row, lane, groups):
+    response = jnp.broadcast_to(response[0:1, :], TILE)
+
+    zero = jnp.where((lane < 0) & (sub < 0), 1.0, 0.0).astype(F32)
+
+    def forward(i, carry):
+        one, two = carry
+        new = []
+        for n, s in enumerate(SYSTEM):
+            value = coef_ref[s * 5 + 2, i] * char_ref[n, layer_at(i), :]
+            value = value - coef_ref[s * 5 + 1, i] * two[n] - coef_ref[s * 5, i] * one[n]
+            f_ref[n, layer_at(i), :] = value
+            new.append(value)
+        return new, one
+
+    start = ([zero] * 5, [zero] * 5)
+    last = lax.fori_loop(0, cells, forward, start, unroll=UNROLL)
+    first = lax.fori_loop(0, cells, swept_back(cells, f_ref, coef_ref), start, unroll=UNROLL)
+    spread(out_ref, 0, lane, with_fifth(last + first))
+    spread(out_ref, 6, lane, with_fifth(gives))
+    spread(out_ref, 11, lane, [[-0.5 * dt_ref[pl.ds(i * 8, 8), :] for i in (0, 1, cells - 2, cells - 1)]])
     for quarter in range(4):
-        for k, four in enumerate(groups):
-            out_ref[pl.ds(quarter * 8 * OUT + row + k, 8, stride=OUT), :] = by_quarter(
-                lane, [quarter_move(four[u], quarter, u) for u in range(4)]
-            )
-
-
-def with_fifth(values):
-    return [values[k][:4] for k in range(4)] + [[values[k][4] for k in range(4)]]
-
-
-def gathered(in_ref, row, lane):
-    values = []
-    for k in range(5):
-        parts = [in_ref[pl.ds(q * 8 * BACK + row + k, 8, stride=BACK), :] for q in range(4)]
-        values.append(
-            [by_quarter(lane, [quarter_move(parts[q], u, q) for q in range(4)]) for u in range(4)]
-        )
-    return [values[k] + [values[4][k]] for k in range(4)]
-
-
-def local_kernel(
-    cells, char_ref, give_ref, response_ref, dt_ref, dt_edge_ref, west_ref, east_ref, coef_ref, char_mat, out_ref, f_ref
+        out_ref[pl.ds(quarter * 8 * OUT + 5, 8, stride=OUT), :] = response
+
+
+def beside_kernel(
+    cells, f_in, dt_edge_ref, east_ref, west_ref, coef_ref, char_mat, f_ref, row_ref, sweep_ref
 ):
     sub, lane = iotas()
     scale = -0.5 * dt_edge_ref[...]
@@ -240,42 +273,35 @@
             for v in range(5)
         ],
     )
-    outside = (lane == jnp.where(sub < 4, 0, 127)) & (sub >= 0)
+    outside = outer(sub, lane)
     zero = jnp.where((lane < 0) & (sub < 0), 1.0, 0.0).astype(F32)
 
     def forward(i, carry):
         one, two = carry
         new = []
         for n, s in enumerate(SYSTEM):
-            char = char_ref[n, layer_at(i), :] + jnp.where(
-                outside, roll(beside[n], (128 - i) % 128, 1), 0.0
-            )
+            char = jnp.where(outside, roll(beside[n], (128 - i) % 128, 1), 0.0)
             value = coef_ref[s * 5 + 2, i] * char - coef_ref[s * 5 + 1, i] * two[n] - coef_ref[s * 5, i] * one[n]
-            f_ref[n, layer_at(i), :] = value
+            sweep_ref[n, layer_at(i), :] = value
+            f_ref[n, layer_at(i), :] = f_in[n, layer_at(i), :] + value
             new.append(value)
-        return new, one
-
-    def backward(step, carry):
-        i = cells - 1 - step
-        one, two = carry
-        new = [
-            f_ref[n, layer_at(i), :] - coef_ref[s * 5 + 4, i] * two[n] - coef_ref[s * 5 + 3, i] * one[n]
-            for n, s in enumerate(SYSTEM)
-        ]
         return new, one
 
     start = ([zero] * 5, [zero] * 5)
     last = lax.fori_loop(0, cells, forward, start, unroll=UNROLL)
-    first = lax.fori_loop(0, cells, backward, start, unroll=UNROLL)
-    spread(out_ref, 0, lane, with_fifth(last + first))
-    spread(out_ref, 6, lane, with_fifth([[give_ref[m, u] for u in range(5)] for m in range(4)]))
-    spread(out_ref, 11, lane, [[-0.5 * dt_ref[pl.ds(i * 8, 8), :] for i in (0, 1, cells - 2, cells - 1)]])
-    response = jnp.broadcast_to(response_ref[0:1, :], TILE)
-    for quarter in range(4):
-        out_ref[pl.ds(quarter * 8 * OUT + 5, 8, stride=OUT), :] = response
-
-
-def reduced_kernel(count, in_ref, out_ref, part_ref, coef_ref, four_ref):
+    first = lax.fori_loop(0, cells, swept_back(cells, sweep_ref, coef_ref), start, unroll=UNROLL)
+    ends = last + first
+    row_ref[...] = jnp.zeros(TILE, F32)
+    for pair in range(2):
+        total = jnp.zeros(TILE, F32)
+        for n in range(2):
+            for u in range(5):
+                value = jnp.sum(ends[pair * 2 + n][u], axis=1, keepdims=True)
+                total = jnp.where(lane == n * 64 + u * 8 + sub, value, total)
+        row_ref[pair : pair + 1, :] = jnp.sum(total, axis=0, keepdims=True)
+
+
+def reduced_kernel(count, in_ref, row_ref, out_ref, edge_coef_ref, part_ref, coef_ref, four_ref):
     lane = lax.broadcasted_iota(jnp.int32, (count, 128), 1)
     place = lax.broadcasted_iota(jnp.int32, (count, 128), 0)
 
@@ -287,12 +313,12 @@
 
     response = rows(5)
 
-    def factor(k, c):
-        wide = []
-        for s in range(3):
-            at = (s * 4 + k) * 8 + c
-            wide.append(jnp.broadcast_to(response[:, at : at + 1], (count, 128)))
-        return jnp.where(lane < 96, wide[0], wide[1]), wide[2]
+    def wide(k, c):
+        at = [(s * 4 + k) * 8 + c for s in range(3)]
+        return [jnp.broadcast_to(response[:, n : n + 1], (count, 128)) for n in at]
+
+    def factor(systems):
+        return jnp.where(lane < 96, systems[0], systems[1]), systems[2]
 
     step, fifth = rows(11), rows(10)
     added = []
@@ -312,13 +338,19 @@
     for k in range(4):
         values = [rows(k), quarter_move(fifth, k, 0)]
         for m in range(4):
-            for tile, part in enumerate(factor(k, 4 + m)):
+            for tile, part in enumerate(factor(wide(k, 4 + m))):
                 values[tile] = values[tile] + part * added[m][tile]
         for tile in range(2):
             part_ref[k, tile] = values[tile]
         for c in range(2 if k < 2 else 4):
-            for tile, part in enumerate(factor(k, c)):
+            systems = wide(k, c)
+            for tile, part in enumerate(factor(systems)):
                 coef_ref[k * 4 + c, tile] = part
+            edge_coef_ref[k * 4 + c] = jnp.where(
+                lane < 24, systems[0], jnp.where(lane < 32, systems[1], systems[2])
+            )
+    for n in range(2):
+        put(10 + n, jnp.broadcast_to(row_ref[n : n + 1, :], (count, 128)))
     zero = jnp.zeros((1, 128), F32)
 
     def take(ref, n, tile, t):
@@ -362,9 +394,42 @@
     put(4, by_quarter(lane, [quarter_move(four_ref[k], 0, k) for k in range(4)]))
 
 
-def final_kernel(cells, f_ref, in_ref, coef_ref, cons_mat, out_ref, shift_ref):
-    _, lane = iotas()
+def edge_inflow(count, in_ref, coef_ref, edge_ref, flow_ref):
+    for pair in range(2):
+        both = in_ref[pl.ds(10 + pair, count, stride=BACK), :]
+        edge_ref[pair * 2] = both
+        edge_ref[pair * 2 + 1] = roll(both, 64, 1)
+
+    def take(k, c, t):
+        return coef_ref[k * 4 + c, t : t + 1, :]
+
+    zero = jnp.zeros((1, 128), F32)
+    one, two = zero, zero
+    sums = []
+    for t in range(count):
+        flow_ref[0, t : t + 1, :] = one
+        flow_ref[1, t : t + 1, :] = two
+        made = [edge_ref[k, t : t + 1, :] + take(k, 0, t) * one + take(k, 1, t) * two for k in range(4)]
+        one, two = made[:2]
+        sums.append(made[2:])
+    one, two = zero, zero
+    for t in reversed(range(count)):
+        flow_ref[2, t : t + 1, :] = one
+        flow_ref[3, t : t + 1, :] = two
+        one, two = [sums[t][k - 2] + take(k, 2, t) * one + take(k, 3, t) * two for k in (2, 3)]
+
+
+def final_kernel(cells, count, f_ref, in_ref, edge_coef_ref, coef_ref, cons_mat, out_ref, shift_ref, edge_ref, flow_ref):
+    sub, lane = iotas()
+    edge_inflow(count, in_ref, edge_coef_ref, edge_ref, flow_ref)
+    place = lax.axis_index("sec")
+    outside = outer(sub, lane)
     inflow = gathered(in_ref, 0, lane)
+    for k in range(4):
+        row = jnp.broadcast_to(flow_ref[k, pl.ds(place, 1), :], TILE)
+        for u in range(5):
+            value = jnp.sum(jnp.where(lane == u * 8 + sub, row, 0.0), axis=1, keepdims=True)
+            inflow[k][u] = inflow[k][u] + jnp.where(outside, value, 0.0)
     added = gathered(in_ref, 5, lane)
 
     def forward(i, carry, right=None):
@@ -432,13 +497,13 @@
     flat = state.reshape(5, cells, 4, 2, 128).transpose(0, 1, 3, 2, 4).reshape(5 * cells * 8, 128)
     steps = time_step.reshape(cells, 4, 2, 128).transpose(0, 2, 1, 3).reshape(cells * 8, 128)
     block = (5, cells * 8, 128)
-    edge, padded, steps, step_edge, coef, char_mat, cons_mat = pl.pallas_call(
-        lambda *refs: edges_kernel(cells, *refs),
+    ends, swept, padded, steps, coef, char_mat, cons_mat = pl.pallas_call(
+        lambda *refs: own_kernel(cells, *refs),
         out_shape=(
-            kept(40, 128),
+            kept(count * OUT, 128),
+            kept(*block),
             kept(5, (cells + 4) * 8, 128),
             kept(cells * 8, 128),
-            kept(*TILE),
             pltpu.SMEM((16, 128), F32),
             pltpu.SMEM((5, 5), F32),
             pltpu.SMEM((5, 5), F32),
@@ -446,55 +511,61 @@
         in_specs=[ANY] * 6,
         out_specs=(VMEM,) * 4 + (SMEM,) * 3,
         scratch_shapes=[
+            pltpu.VMEM(block, F32),
+            pltpu.VMEM((3, cells * 8, 128), F32),
             pltpu.VMEM(lower_bands.shape, F32),
             pltpu.VMEM(upper_bands.shape, F32),
             pltpu.VMEM((16, 128), F32),
             pltpu.SemaphoreType.DMA((5,)),
             pltpu.SemaphoreType.DMA((6,)),
         ],
-        name="edges",
+        name="own",
     )(flat, steps, lower_bands, upper_bands, to_char, to_cons)
     coef, char_mat, cons_mat = near_scalars(coef), near_scalars(char_mat), near_scalars(cons_mat)
+    ends = exchanged(ends, count)
+    edge, step_edge = pl.pallas_call(
+        lambda *refs: edges_kernel(cells, *refs),
+        out_shape=(kept(40, 128), kept(*TILE)),
+        in_specs=[VMEM] * 2,
+        out_specs=(VMEM, VMEM),
+        name="edges",
+    )(near(padded), near(steps))
     right = [(i, i + 1) for i in range(columns - 1)]
     west = near(lax.ppermute(edge, "cross", right))
     east = near(lax.ppermute(edge, "cross", [(j, i) for i, j in right]))
-    char, give, response = pl.pallas_call(
-        lambda *refs: inner_kernel(cells, *refs),
-        out_shape=(kept(*block), kept(4, 5, *TILE), kept(*TILE)),
-        in_specs=[VMEM] * 2 + [SMEM] * 2,
-        out_specs=(VMEM,) * 3,
-        scratch_shapes=[pltpu.VMEM((3, cells * 8, 128), F32)],
-        name="inner",
-    )(near(padded), near(steps), coef, char_mat)
-    ends, swept = pl.pallas_call(
-        lambda *refs: local_kernel(cells, *refs),
-        out_shape=(kept(count * OUT, 128), kept(*block)),
-        in_specs=[VMEM] * 7 + [SMEM] * 2,
+    swept, row = pl.pallas_call(
+        lambda *refs: beside_kernel(cells, *refs),
+        out_shape=(kept(*block), kept(*TILE)),
+        in_specs=[VMEM] * 4 + [SMEM] * 2,
         out_specs=(VMEM, VMEM),
-        name="local",
-    )(near(char), near(give), near(response), near(steps), near(step_edge), west, east, coef, char_mat)
-    ends = exchanged(ends, count)
-    inflow = pl.pallas_call(
+        scratch_shapes=[pltpu.VMEM(block, F32)],
+        name="beside",
+    )(near(swept), near(step_edge), east, west, coef, char_mat)
+    inflow, edge_coef = pl.pallas_call(
         lambda *refs: reduced_kernel(count, *refs),
-        out_shape=kept(count * BACK, 128),
-        in_specs=[VMEM],
-        out_specs=VMEM,
+        out_shape=(kept(count * BACK, 128), kept(16, count, 128)),
+        in_specs=[VMEM] * 2,
+        out_specs=(VMEM, VMEM),
         scratch_shapes=[
             pltpu.VMEM((4, 2, count, 128), F32),
             pltpu.VMEM((16, 2, count, 128), F32),
             pltpu.VMEM((4, count, 128), F32),
         ],
         name="reduced",
-    )(near(ends))
+    )(near(ends), near(row))
     inflow = exchanged(inflow, count)
     result = pl.pallas_call(
-        lambda *refs: final_kernel(cells, *refs),
+        lambda *refs: final_kernel(cells, count, *refs),
         out_shape=shaped(5 * cells * 8, 128),
-        in_specs=[VMEM, VMEM, SMEM, SMEM],
+        in_specs=[VMEM] * 3 + [SMEM] * 2,
         out_specs=VMEM,
-        scratch_shapes=[pltpu.VMEM(block, F32)],
+        scratch_shapes=[
+            pltpu.VMEM(block, F32),
+            pltpu.VMEM((4, count, 128), F32),
+            pltpu.VMEM((4, count, 128), F32),
+        ],
         name="final",
-    )(near(swept), near(inflow), coef, cons_mat)
+    )(near(swept), near(inflow), near(edge_coef), coef, cons_mat)
     return result.reshape(5, cells, 2, 4, 128).transpose(0, 1, 3, 2, 4).reshape(state.shape)
 
 

time: 44 us -> 42.7 us (0.970)
  blocking collectives: 28.8 us -> 16.9 us
  starting transfers between devices: 5.77 us -> 13.5 us
  waiting for transfers between devices: 2.28 us -> 3.82 us
  Pallas kernels: 6.88 us -> 8.12 us
    all_to_all x2 -> x1, blocking collectives: 28.8 us -> 16.9 us  [exchanged(): return lax.all_to_all(chunks, 'sec', 0, 0, tiled=True).reshape(x.shape)]
    all_to_all x0 -> x1, starting transfers between devices: none -> 7.77 us  [exchanged(): return lax.all_to_all(chunks, 'sec', 0, 0, tiled=True).reshape(x.shape)]
    pallas_call x4, Pallas kernels: 4.89 us -> 7.69 us  [the longest x1 4.27 us: on_device(): pl.pallas_call(lambda *refs: own_kernel(cells, *refs), out_shape=(kept(co...]
    pallas_call x1, Pallas kernels: 1.98 us -> 0.43 us  [on_device(): pl.pallas_call(lambda *refs: edges_kernel(cells, *refs), out_shape=(kept(...]
    ppermute x1, waiting for transfers between devices: 2.28 us -> 3.8 us  [on_device(): west = near(lax.ppermute(edge, 'cross', right))]
  transfers between devices with their start and end apart: 2 -> 3, of which waited for: 1 -> 1; matrix products, arithmetic and copies ran while one was open for 0% -> 0% of each run, Pallas kernels for 3% -> 3%
where the time goes in v5:
time: 42.7 us; the launch traced here: 42.4 us
  blocking collectives  16.9 us (40%)
  starting transfers between devices  13.5 us (32%)
  Pallas kernels  8.12 us (19%)
  waiting for transfers between devices  3.82 us (9%)
    all_to_all x1, blocking collectives, exchanged(): return lax.all_to_all(chunks, 'sec', 0, 0, tiled=True).reshape(x.shape)  16.9 us
    all_to_all x1, starting transfers between devices, exchanged(): return lax.all_to_all(chunks, 'sec', 0, 0, tiled=True).reshape(x.shape)  7.77 us
    pallas_call x1, Pallas kernels, on_device(): pl.pallas_call(lambda *refs: own_kernel(cells, *refs), out_shape=(kept(co...  4.27 us
    ppermute x1, starting transfers between devices, on_device(): east = near(lax.ppermute(edge, 'cross', [(j, i) for i, j in right]))  3.85 us
    ppermute x1, waiting for transfers between devices, on_device(): west = near(lax.ppermute(edge, 'cross', right))  3.8 us
    pallas_call x1, Pallas kernels, on_device(): pl.pallas_call(lambda *refs: final_kernel(cells, count, *refs), out_shape...  1.97 us
    ppermute x1, starting transfers between devices, on_device(): west = near(lax.ppermute(edge, 'cross', right))  1.92 us
  transfers between devices with their start and end apart: 3, of which 1 were waited for; matrix products, arithmetic and copies ran while one was open for 0% of the time, Pallas kernels for 3%

profile of v5, /device:TPU:385, one launch (start us, length us, event | category | flops | bytes accessed | tf_op | source)
XLA Modules:
  0.0 42.4 jit_solution(17709614973438837833)
XLA Ops:
  0.0 4.3 %own.1 = (f32[384,128]{1,0:T(8,128)}, f32[5,256,128]{2,1,0:T(8,128)S(1)}, f32[5,288,128]{2,1,0:T(8,128)S(1)}, f32[256,128]{1,0:T(8,128)S(1)}, f32[16,128]{1,0:T(...) custom-call(f32[1280,128]{1,0:T(8,128)} %bitcast.22, f32[256,128]{1,0:T(8,128)} %bitcast.23, f32[3,3,32]{2,1,0:T(4,128)} %refs_2_.1, ...), custom_call_target="tpu_custom_call" | custom-call | tf_op jit(solution)/shard_map/own/pallas_call | solution.py:500
  4.3 7.8 %all-to-all-start = ((f32[32,1,1536]{2,1,0:T(1,128)}), f32[32,1,1536]{2,1,0:T(1,128)S(1)}, u32[]{:S(2)}, u32[]{:S(2)}) async-start(f32[32,1,1536]{2,1,0:T(1,128)} %bitcast.6), calls=%async_computation | async-start | bytes 393216 | tf_op jit(solution)/shard_map/all_to_all | solution.py:481
  12.1 0.4 %edges.1 = (f32[40,128]{1,0:T(8,128)S(1)}, f32[8,128]{1,0:T(8,128)S(1)}) custom-call(f32[5,288,128]{2,1,0:T(8,128)S(1)} %get-tuple-element.19.refs_0_, f32[256,128]{1,0:T(8,128)S(1)} %get-tuple-element.20.refs_1_), custom_call_target="tpu_custom_call" | custom-call | tf_op jit(solution)/shard_map/edges/pallas_call | solution.py:526
  12.5 3.8 %collective-permute-start = (f32[40,128]{1,0:T(8,128)S(1)}, f32[40,128]{1,0:T(8,128)S(1)}, u32[]{:S(2)}, u32[]{:S(2)}) collective-permute-start(f32[40,128]{1,0:T(8,128)S(1)} %get-tuple-element.22), channel_id=1, source_target_pairs={{1,0},{2,1},{3,2},{4,3},{5,4},{6,5},{7,6},{8,7},{9,8},{10,9},{11,1... | collective-permute-start | bytes 61448 | tf_op jit(solution)/shard_map/ppermute | solution.py:535
  16.3 1.9 %collective-permute-start.1 = (f32[40,128]{1,0:T(8,128)S(1)}, f32[40,128]{1,0:T(8,128)S(1)}, u32[]{:S(2)}, u32[]{:S(2)}) collective-permute-start(f32[40,128]{1,0:T(8,128)S(1)} %get-tuple-element.22), channel_id=1, source_target_pairs={{0,1},{1,2},{2,3},{3,4},{4,5},{5,6},{6,7},{7,8},{8,9},{9,10},{10,1... | collective-permute-start | bytes 61448 | tf_op jit(solution)/shard_map/ppermute | solution.py:534
  18.3 0.0 collective-permute-done.refs_2_
  18.3 3.8 %collective-permute-done.1.refs_3_ = f32[40,128]{1,0:T(8,128)S(1)} collective-permute-done((f32[40,128]{1,0:T(8,128)S(1)}, f32[40,128]{1,0:T(8,128)S(1)}, u32[]{:S(2)}, u32[]{:S(2)}) %collective-permute-start.1) | collective-permute-done | bytes 20512 | tf_op jit(solution)/shard_map/ppermute | solution.py:534
  22.1 0.7 %beside.1 = (f32[5,256,128]{2,1,0:T(8,128)S(1)}, f32[8,128]{1,0:T(8,128)S(1)}) custom-call(f32[5,256,128]{2,1,0:T(8,128)S(1)} %get-tuple-element.18.refs_0_, f32[8,128]{1,0:T(8,128)S(1)} %get-tuple-element.21.refs_1_, f32[40,128]{1,0:T(8,128)S(1)} %collective-permute-done.refs_2_, f32[40,128]{1,0:T(8,128)S(1)} %collective-permute-done.1.refs_3_, ...), custom_call_target="tpu_custom_call" | custom-call | tf_op jit(solution)/shard_map/beside/pallas_call | solution.py:536
  22.8 0.0 all-to-all-done
  22.8 0.8 %reduced.1 = (f32[384,128]{1,0:T(8,128)S(1)}, f32[16,32,128]{2,1,0:T(8,128)S(1)}) custom-call(f32[384,128]{1,0:T(8,128)S(1)} %bitcast.20, f32[8,128]{1,0:T(8,128)S(1)} %get-tuple-element.27.refs_1_), custom_call_target="tpu_custom_call" | custom-call | tf_op jit(solution)/shard_map/reduced/pallas_call | solution.py:544
  23.6 16.9 %all_to_all.10 = f32[32,1,1536]{2,1,0:T(1,128)S(1)} all-to-all(f32[32,1,1536]{2,1,0:T(1,128)S(1)} %bitcast.21), channel_id=1, replica_groups=mesh['sec'=32,'cross'=16] {'sec'}, dimensions={0} | all-to-all | bytes 393216 | tf_op jit(solution)/shard_map/all_to_all | solution.py:481
  40.4 2.0 %final.1 = f32[1280,128]{1,0:T(8,128)} custom-call(f32[5,256,128]{2,1,0:T(8,128)S(1)} %get-tuple-element.25.refs_0_, f32[384,128]{1,0:T(8,128)S(1)} %bitcast.19, f32[16,32,128]{2,1,0:T(8,128)S(1)} %get-tuple-element.29.refs_2_, f32[16,128]{1,0:T(8,128)S(4)} %get-tuple-element.23.refs_4_.refs_3_, f32[5,5]{1,0:T(8,128)S(4)} %get-tuple-element.30.refs_4_), custom_call_target="tpu_custom_call" | custom-call | tf_op jit(solution)/shard_map/final/pallas_call | solution.py:557
Async XLA Ops:
  4.3 18.5 %all-to-all-start = ((f32[32,1,1536]{2,1,0:T(1,128)}), f32[32,1,1536]{2,1,0:T(1,128)S(1)}, u32[]{:S(2)}, u32[]{:S(2)}) async-start(f32[32,1,1536]{2,1,0:T(1,128)} %bitcast.6), calls=%async_computation | async-start | bytes 393216 | tf_op jit(solution)/shard_map/all_to_all | solution.py:481
  12.5 5.8 %collective-permute-start = (f32[40,128]{1,0:T(8,128)S(1)}, f32[40,128]{1,0:T(8,128)S(1)}, u32[]{:S(2)}, u32[]{:S(2)}) collective-permute-start(f32[40,128]{1,0:T(8,128)S(1)} %get-tuple-element.22), channel_id=1, source_target_pairs={{1,0},{2,1},{3,2},{4,3},{5,4},{6,5},{7,6},{8,7},{9,8},{10,9},{11,1... | collective-permute-start | bytes 61448 | tf_op jit(solution)/shard_map/ppermute | solution.py:535
  16.3 5.7 %collective-permute-start.1 = (f32[40,128]{1,0:T(8,128)S(1)}, f32[40,128]{1,0:T(8,128)S(1)}, u32[]{:S(2)}, u32[]{:S(2)}) collective-permute-start(f32[40,128]{1,0:T(8,128)S(1)} %get-tuple-element.22), channel_id=1, source_target_pairs={{0,1},{1,2},{2,3},{3,4},{4,5},{5,6},{6,7},{7,8},{8,9},{9,10},{10,1... | collective-permute-start | bytes 61448 | tf_op jit(solution)/shard_map/ppermute | solution.py:534

commit v6 on v5

--- a/solution.py
+++ b/solution.py
@@ -9,6 +9,8 @@
 F32 = jnp.float32
 OUT = 12
 BACK = 12
+PARTS = 2
+STORES = 4
 UNROLL = 32
 TILE = (8, 128)
 
@@ -123,11 +125,12 @@
 ):
     sub, lane = iotas()
     rows = cells * 8
+    part = rows // PARTS
     x_copies = [
         pltpu.make_async_copy(
-            x_hbm.at[pl.ds(v * rows, rows)], x_ref.at[v, pl.ds(16, rows)], x_sems.at[v]
+            x_hbm.at[:, pl.ds(n * part, part)], x_ref.at[:, pl.ds(16 + n * part, part)], x_sems.at[n]
         )
-        for v in range(5)
+        for n in range(PARTS)
     ]
     pairs = (
         (lower_hbm, lower_ref),
@@ -137,7 +140,7 @@
         (cons_hbm, cons_mat),
     )
     copies = [pltpu.make_async_copy(a, b, sems.at[n]) for n, (a, b) in enumerate(pairs)]
-    for copy in copies[:2] + x_copies + copies[2:]:
+    for copy in copies[:2] + x_copies[:1] + copies[2:4] + x_copies[1:] + copies[4:]:
         copy.start()
     for v in range(5):
         x_ref[v, 0:16] = jnp.zeros((16, 128), F32)
@@ -153,8 +156,8 @@
         made_ref[s * 5 + 3 : s * 5 + 5, 0:cells] = upper_ref[s]
     made = pltpu.make_async_copy(made_ref, coef_ref, sems.at[5])
     made.start()
-    for copy in x_copies + copies[2:] + [made]:
-        copy.wait()
+    copies[2].wait()
+    copies[3].wait()
 
     third = sub % 4
 
@@ -190,7 +193,16 @@
             char_ref[u, layer_at(i), :] = value
         return flux_now, (flux_after, inv_after, pressure_after)
 
-    lax.fori_loop(0, cells, cell, (line(-1)[0], line(0)), unroll=UNROLL)
+    begin = 0
+    for n in range(PARTS):
+        x_copies[n].wait()
+        if n == 0:
+            carry = (line(-1)[0], line(0))
+        end = cells if n == PARTS - 1 else (n + 1) * cells // PARTS - 2
+        carry = lax.fori_loop(begin, end, cell, carry, unroll=end - begin)
+        begin = end
+    copies[4].wait()
+    made.wait()
     top, bottom = line(0), line(cells - 1)
     first_two, last_two = (layer(0), layer(1)), (layer(cells - 2), layer(cells - 1))
     gives = (
@@ -202,59 +214,51 @@
     gives = [to_char(char_mat, give) for give in gives]
 
     unit = [jnp.where((lane == n) & (sub >= 0), 1.0, 0.0).astype(F32) for n in range(8)]
-
-    def answer(i, carry, right=None):
+    zero = jnp.where((lane < 0) & (sub < 0), 1.0, 0.0).astype(F32)
+
+    def forward(i, carry, right=None):
         one, two = carry
         new = []
-        for s in range(3):
-            value = -(coef_ref[s * 5, i] * one[s]) - coef_ref[s * 5 + 1, i] * two[s]
-            if right is not None:
-                value = value + coef_ref[s * 5 + 2, i] * right
-            answer_ref[s, layer_at(i), :] = value
+        for n, s in enumerate(SYSTEM + (0, 1, 2)):
+            value = -(coef_ref[s * 5 + 1, i] * two[n])
+            if n < 5:
+                value = coef_ref[s * 5 + 2, i] * char_ref[n, layer_at(i), :] + value
+            elif right is not None:
+                value = coef_ref[s * 5 + 2, i] * right + value
+            value = value - coef_ref[s * 5, i] * one[n]
+            if n < 5:
+                f_ref[n, layer_at(i), :] = value
+            else:
+                answer_ref[n - 5, layer_at(i), :] = value
             new.append(value)
         return new, one
 
-    def answer_back(step, carry):
+    def backward(step, carry):
         i = cells - 1 - step
         one, two = carry
-        new = [
-            answer_ref[s, layer_at(i), :] - coef_ref[s * 5 + 3, i] * one[s] - coef_ref[s * 5 + 4, i] * two[s]
-            for s in range(3)
-        ]
+        new = []
+        for n, s in enumerate(SYSTEM + (0, 1, 2)):
+            value = f_ref[n, layer_at(i), :] if n < 5 else answer_ref[n - 5, layer_at(i), :]
+            new.append(value - coef_ref[s * 5 + 4, i] * two[n] - coef_ref[s * 5 + 3, i] * one[n])
         return new, one
 
-    last = ([unit[0]] * 3, [unit[1]] * 3)
+    start = [zero] * 5
+    last = (start + [unit[0]] * 3, start + [unit[1]] * 3)
     for i in (0, 1):
-        last = answer(i, last, unit[4 + i])
-    last = lax.fori_loop(2, cells - 2, answer, last, unroll=7)
+        last = forward(i, last, unit[4 + i])
+    last = lax.fori_loop(2, cells - 2, forward, last, unroll=cells - 4)
     for i in (0, 1):
-        last = answer(cells - 2 + i, last, unit[6 + i])
-    first = lax.fori_loop(0, cells, answer_back, ([unit[2]] * 3, [unit[3]] * 3), unroll=UNROLL)
+        last = forward(cells - 2 + i, last, unit[6 + i])
+    first = lax.fori_loop(0, cells, backward, (start + [unit[2]] * 3, start + [unit[3]] * 3), unroll=UNROLL)
     ends = last + first
     response = jnp.zeros(TILE, F32)
     for s in range(3):
         for k in range(4):
             at = (s * 4 + k) * 8
-            moved = ends[k][s] if at == 0 else roll(ends[k][s], at, 1)
+            moved = ends[k][5 + s] if at == 0 else roll(ends[k][5 + s], at, 1)
             response = jnp.where((lane >= at) & (lane < at + 8), moved, response)
     response = jnp.broadcast_to(response[0:1, :], TILE)
-
-    zero = jnp.where((lane < 0) & (sub < 0), 1.0, 0.0).astype(F32)
-
-    def forward(i, carry):
-        one, two = carry
-        new = []
-        for n, s in enumerate(SYSTEM):
-            value = coef_ref[s * 5 + 2, i] * char_ref[n, layer_at(i), :]
-            value = value - coef_ref[s * 5 + 1, i] * two[n] - coef_ref[s * 5, i] * one[n]
-            f_ref[n, layer_at(i), :] = value
-            new.append(value)
-        return new, one
-
-    start = ([zero] * 5, [zero] * 5)
-    last = lax.fori_loop(0, cells, forward, start, unroll=UNROLL)
-    first = lax.fori_loop(0, cells, swept_back(cells, f_ref, coef_ref), start, unroll=UNROLL)
-    spread(out_ref, 0, lane, with_fifth(last + first))
+    spread(out_ref, 0, lane, with_fifth(ends))
     spread(out_ref, 6, lane, with_fifth(gives))
     spread(out_ref, 11, lane, [[-0.5 * dt_ref[pl.ds(i * 8, 8), :] for i in (0, 1, cells - 2, cells - 1)]])
     for quarter in range(4):
@@ -419,7 +423,9 @@
         one, two = [sums[t][k - 2] + take(k, 2, t) * one + take(k, 3, t) * two for k in (2, 3)]
 
 
-def final_kernel(cells, count, f_ref, in_ref, edge_coef_ref, coef_ref, cons_mat, out_ref, shift_ref, edge_ref, flow_ref):
+def final_kernel(
+    cells, count, f_ref, in_ref, edge_coef_ref, coef_ref, cons_mat, out_hbm, shift_ref, edge_ref, flow_ref, made_ref, sems
+):
     sub, lane = iotas()
     edge_inflow(count, in_ref, edge_coef_ref, edge_ref, flow_ref)
     place = lax.axis_index("sec")
@@ -458,10 +464,19 @@
             for n, s in enumerate(SYSTEM)
         ]
         for n in range(5):
-            out_ref[layer_at(n * cells + i), :] = sum(cons_mat[n, v] * new[v] for v in range(5))
+            made_ref[n, layer_at(i), :] = sum(cons_mat[n, v] * new[v] for v in range(5))
         return new, one
 
-    lax.fori_loop(0, cells, backward, (inflow[2], inflow[3]), unroll=UNROLL)
+    carry = (inflow[2], inflow[3])
+    part = cells // STORES
+    copies = []
+    for p in range(STORES):
+        carry = lax.fori_loop(p * part, (p + 1) * part, backward, carry, unroll=part)
+        at = pl.ds((cells - (p + 1) * part) * 8, part * 8)
+        copies.append(pltpu.make_async_copy(made_ref.at[:, at], out_hbm.at[:, at], sems.at[p]))
+        copies[-1].start()
+    for copy in copies:
+        copy.wait()
 
 
 def shaped(*shape):
@@ -494,7 +509,7 @@
     cells = state.shape[1]
     count = lax.axis_size("sec")
     columns = lax.axis_size("cross")
-    flat = state.reshape(5, cells, 4, 2, 128).transpose(0, 1, 3, 2, 4).reshape(5 * cells * 8, 128)
+    flat = state.reshape(5, cells, 4, 2, 128).transpose(0, 1, 3, 2, 4).reshape(5, cells * 8, 128)
     steps = time_step.reshape(cells, 4, 2, 128).transpose(0, 2, 1, 3).reshape(cells * 8, 128)
     block = (5, cells * 8, 128)
     ends, swept, padded, steps, coef, char_mat, cons_mat = pl.pallas_call(
@@ -516,7 +531,7 @@
             pltpu.VMEM(lower_bands.shape, F32),
             pltpu.VMEM(upper_bands.shape, F32),
             pltpu.VMEM((16, 128), F32),
-            pltpu.SemaphoreType.DMA((5,)),
+            pltpu.SemaphoreType.DMA((PARTS,)),
             pltpu.SemaphoreType.DMA((6,)),
         ],
         name="own",
@@ -556,13 +571,15 @@
     inflow = exchanged(inflow, count)
     result = pl.pallas_call(
         lambda *refs: final_kernel(cells, count, *refs),
-        out_shape=shaped(5 * cells * 8, 128),
+        out_shape=shaped(*block),
         in_specs=[VMEM] * 3 + [SMEM] * 2,
-        out_specs=VMEM,
+        out_specs=ANY,
         scratch_shapes=[
             pltpu.VMEM(block, F32),
             pltpu.VMEM((4, count, 128), F32),
             pltpu.VMEM((4, count, 128), F32),
+            pltpu.VMEM(block, F32),
+            pltpu.SemaphoreType.DMA((STORES,)),
         ],
         name="final",
     )(near(swept), near(inflow), near(edge_coef), coef, cons_mat)

time: 42.7 us -> 42 us (0.984)
  Pallas kernels: 8.12 us -> 7.41 us
    pallas_call x1, Pallas kernels: 4.27 us -> 3.69 us  [on_device(): pl.pallas_call(lambda *refs: own_kernel(cells, *refs), out_shape=(kept(co...]
where the time goes in v6:
time: 42 us; the launch traced here: 41.7 us
  blocking collectives  16.9 us (40%)
  starting transfers between devices  13.5 us (32%)
  Pallas kernels  7.41 us (18%)
  waiting for transfers between devices  3.82 us (9%)
    all_to_all x1, blocking collectives, exchanged(): return lax.all_to_all(chunks, 'sec', 0, 0, tiled=True).reshape(x.shape)  16.9 us
    all_to_all x1, starting transfers between devices, exchanged(): return lax.all_to_all(chunks, 'sec', 0, 0, tiled=True).reshape(x.shape)  7.77 us
    ppermute x1, starting transfers between devices, on_device(): east = near(lax.ppermute(edge, 'cross', [(j, i) for i, j in right]))  3.85 us
    ppermute x1, waiting for transfers between devices, on_device(): west = near(lax.ppermute(edge, 'cross', right))  3.8 us
    pallas_call x1, Pallas kernels, on_device(): pl.pallas_call(lambda *refs: own_kernel(cells, *refs), out_shape=(kept(co...  3.69 us
    ppermute x1, starting transfers between devices, on_device(): west = near(lax.ppermute(edge, 'cross', right))  1.92 us
    pallas_call x1, Pallas kernels, on_device(): pl.pallas_call(lambda *refs: final_kernel(cells, count, *refs), out_shape...  1.84 us
  transfers between devices with their start and end apart: 3, of which 1 were waited for; matrix products, arithmetic and copies ran while one was open for 0% of the time, Pallas kernels for 3%

profile of v6, /device:TPU:385, one launch (start us, length us, event | category | flops | bytes accessed | tf_op | source)
XLA Modules:
  0.0 41.7 jit_solution(1883487517229484659)
XLA Ops:
  0.0 3.7 %own.1 = (f32[384,128]{1,0:T(8,128)}, f32[5,256,128]{2,1,0:T(8,128)S(1)}, f32[5,288,128]{2,1,0:T(8,128)S(1)}, f32[256,128]{1,0:T(8,128)S(1)}, f32[16,128]{1,0:T(...) custom-call(f32[5,256,128]{2,1,0:T(8,128)} %bitcast.22, f32[256,128]{1,0:T(8,128)} %bitcast.23, f32[3,3,32]{2,1,0:T(4,128)} %refs_2_.1, ...), custom_call_target="tpu_custom_call" | custom-call | tf_op jit(solution)/shard_map/own/pallas_call | solution.py:515
  3.7 7.8 %all-to-all-start = ((f32[32,1,1536]{2,1,0:T(1,128)}), f32[32,1,1536]{2,1,0:T(1,128)S(1)}, u32[]{:S(2)}, u32[]{:S(2)}) async-start(f32[32,1,1536]{2,1,0:T(1,128)} %bitcast.6), calls=%async_computation | async-start | bytes 393216 | tf_op jit(solution)/shard_map/all_to_all | solution.py:496
  11.5 0.4 %edges.1 = (f32[40,128]{1,0:T(8,128)S(1)}, f32[8,128]{1,0:T(8,128)S(1)}) custom-call(f32[5,288,128]{2,1,0:T(8,128)S(1)} %get-tuple-element.19.refs_0_, f32[256,128]{1,0:T(8,128)S(1)} %get-tuple-element.20.refs_1_), custom_call_target="tpu_custom_call" | custom-call | tf_op jit(solution)/shard_map/edges/pallas_call | solution.py:541
  11.9 3.8 %collective-permute-start = (f32[40,128]{1,0:T(8,128)S(1)}, f32[40,128]{1,0:T(8,128)S(1)}, u32[]{:S(2)}, u32[]{:S(2)}) collective-permute-start(f32[40,128]{1,0:T(8,128)S(1)} %get-tuple-element.22), channel_id=1, source_target_pairs={{1,0},{2,1},{3,2},{4,3},{5,4},{6,5},{7,6},{8,7},{9,8},{10,9},{11,1... | collective-permute-start | bytes 61448 | tf_op jit(solution)/shard_map/ppermute | solution.py:550
  15.8 1.9 %collective-permute-start.1 = (f32[40,128]{1,0:T(8,128)S(1)}, f32[40,128]{1,0:T(8,128)S(1)}, u32[]{:S(2)}, u32[]{:S(2)}) collective-permute-start(f32[40,128]{1,0:T(8,128)S(1)} %get-tuple-element.22), channel_id=1, source_target_pairs={{0,1},{1,2},{2,3},{3,4},{4,5},{5,6},{6,7},{7,8},{8,9},{9,10},{10,1... | collective-permute-start | bytes 61448 | tf_op jit(solution)/shard_map/ppermute | solution.py:549
  17.7 0.0 collective-permute-done.refs_2_
  17.7 3.8 %collective-permute-done.1.refs_3_ = f32[40,128]{1,0:T(8,128)S(1)} collective-permute-done((f32[40,128]{1,0:T(8,128)S(1)}, f32[40,128]{1,0:T(8,128)S(1)}, u32[]{:S(2)}, u32[]{:S(2)}) %collective-permute-start.1) | collective-permute-done | bytes 20512 | tf_op jit(solution)/shard_map/ppermute | solution.py:549
  21.5 0.7 %beside.1 = (f32[5,256,128]{2,1,0:T(8,128)S(1)}, f32[8,128]{1,0:T(8,128)S(1)}) custom-call(f32[5,256,128]{2,1,0:T(8,128)S(1)} %get-tuple-element.18.refs_0_, f32[8,128]{1,0:T(8,128)S(1)} %get-tuple-element.21.refs_1_, f32[40,128]{1,0:T(8,128)S(1)} %collective-permute-done.refs_2_, f32[40,128]{1,0:T(8,128)S(1)} %collective-permute-done.1.refs_3_, ...), custom_call_target="tpu_custom_call" | custom-call | tf_op jit(solution)/shard_map/beside/pallas_call | solution.py:551
  22.2 0.0 all-to-all-done
  22.2 0.8 %reduced.1 = (f32[384,128]{1,0:T(8,128)S(1)}, f32[16,32,128]{2,1,0:T(8,128)S(1)}) custom-call(f32[384,128]{1,0:T(8,128)S(1)} %bitcast.20, f32[8,128]{1,0:T(8,128)S(1)} %get-tuple-element.27.refs_1_), custom_call_target="tpu_custom_call" | custom-call | tf_op jit(solution)/shard_map/reduced/pallas_call | solution.py:559
  23.0 16.9 %all_to_all.10 = f32[32,1,1536]{2,1,0:T(1,128)S(1)} all-to-all(f32[32,1,1536]{2,1,0:T(1,128)S(1)} %bitcast.21), channel_id=1, replica_groups=mesh['sec'=32,'cross'=16] {'sec'}, dimensions={0} | all-to-all | bytes 393216 | tf_op jit(solution)/shard_map/all_to_all | solution.py:496
  39.9 1.8 %final.1 = f32[5,256,128]{2,1,0:T(8,128)} custom-call(f32[5,256,128]{2,1,0:T(8,128)S(1)} %get-tuple-element.25.refs_0_, f32[384,128]{1,0:T(8,128)S(1)} %bitcast.19, f32[16,32,128]{2,1,0:T(8,128)S(1)} %get-tuple-element.29.refs_2_, f32[16,128]{1,0:T(8,128)S(4)} %get-tuple-element.23.refs_4_.refs_3_, f32[5,5]{1,0:T(8,128)S(4)} %get-tuple-element.30.refs_4_), custom_call_target="tpu_custom_call" | custom-call | tf_op jit(solution)/shard_map/final/pallas_call | solution.py:572
Async XLA Ops:
  3.7 18.5 %all-to-all-start = ((f32[32,1,1536]{2,1,0:T(1,128)}), f32[32,1,1536]{2,1,0:T(1,128)S(1)}, u32[]{:S(2)}, u32[]{:S(2)}) async-start(f32[32,1,1536]{2,1,0:T(1,128)} %bitcast.6), calls=%async_computation | async-start | bytes 393216 | tf_op jit(solution)/shard_map/all_to_all | solution.py:496
  11.9 5.8 %collective-permute-start = (f32[40,128]{1,0:T(8,128)S(1)}, f32[40,128]{1,0:T(8,128)S(1)}, u32[]{:S(2)}, u32[]{:S(2)}) collective-permute-start(f32[40,128]{1,0:T(8,128)S(1)} %get-tuple-element.22), channel_id=1, source_target_pairs={{1,0},{2,1},{3,2},{4,3},{5,4},{6,5},{7,6},{8,7},{9,8},{10,9},{11,1... | collective-permute-start | bytes 61448 | tf_op jit(solution)/shard_map/ppermute | solution.py:550
  15.8 5.7 %collective-permute-start.1 = (f32[40,128]{1,0:T(8,128)S(1)}, f32[40,128]{1,0:T(8,128)S(1)}, u32[]{:S(2)}, u32[]{:S(2)}) collective-permute-start(f32[40,128]{1,0:T(8,128)S(1)} %get-tuple-element.22), channel_id=1, source_target_pairs={{0,1},{1,2},{2,3},{3,4},{4,5},{5,6},{6,7},{7,8},{8,9},{9,10},{10,1... | collective-permute-start | bytes 61448 | tf_op jit(solution)/shard_map/ppermute | solution.py:549

commit v7 on v6

--- a/solution.py
+++ b/solution.py
@@ -265,47 +265,10 @@
         out_ref[pl.ds(quarter * 8 * OUT + 5, 8, stride=OUT), :] = response
 
 
-def beside_kernel(
-    cells, f_in, dt_edge_ref, east_ref, west_ref, coef_ref, char_mat, f_ref, row_ref, sweep_ref
+def reduced_kernel(
+    cells, count, in_ref, f_in, dt_edge_ref, west_ref, east_ref, scalars, char_mat,
+    out_ref, edge_coef_ref, f_ref, part_ref, coef_ref, four_ref, sweep_ref,
 ):
-    sub, lane = iotas()
-    scale = -0.5 * dt_edge_ref[...]
-    beside = to_char(
-        char_mat,
-        [
-            scale * jnp.where(sub < 4, -west_ref[pl.ds(v * 8, 8), :], east_ref[pl.ds(v * 8, 8), :])
-            for v in range(5)
-        ],
-    )
-    outside = outer(sub, lane)
-    zero = jnp.where((lane < 0) & (sub < 0), 1.0, 0.0).astype(F32)
-
-    def forward(i, carry):
-        one, two = carry
-        new = []
-        for n, s in enumerate(SYSTEM):
-            char = jnp.where(outside, roll(beside[n], (128 - i) % 128, 1), 0.0)
-            value = coef_ref[s * 5 + 2, i] * char - coef_ref[s * 5 + 1, i] * two[n] - coef_ref[s * 5, i] * one[n]
-            sweep_ref[n, layer_at(i), :] = value
-            f_ref[n, layer_at(i), :] = f_in[n, layer_at(i), :] + value
-            new.append(value)
-        return new, one
-
-    start = ([zero] * 5, [zero] * 5)
-    last = lax.fori_loop(0, cells, forward, start, unroll=UNROLL)
-    first = lax.fori_loop(0, cells, swept_back(cells, sweep_ref, coef_ref), start, unroll=UNROLL)
-    ends = last + first
-    row_ref[...] = jnp.zeros(TILE, F32)
-    for pair in range(2):
-        total = jnp.zeros(TILE, F32)
-        for n in range(2):
-            for u in range(5):
-                value = jnp.sum(ends[pair * 2 + n][u], axis=1, keepdims=True)
-                total = jnp.where(lane == n * 64 + u * 8 + sub, value, total)
-        row_ref[pair : pair + 1, :] = jnp.sum(total, axis=0, keepdims=True)
-
-
-def reduced_kernel(count, in_ref, row_ref, out_ref, edge_coef_ref, part_ref, coef_ref, four_ref):
     lane = lax.broadcasted_iota(jnp.int32, (count, 128), 1)
     place = lax.broadcasted_iota(jnp.int32, (count, 128), 0)
 
@@ -353,8 +316,30 @@
             edge_coef_ref[k * 4 + c] = jnp.where(
                 lane < 24, systems[0], jnp.where(lane < 32, systems[1], systems[2])
             )
-    for n in range(2):
-        put(10 + n, jnp.broadcast_to(row_ref[n : n + 1, :], (count, 128)))
+    sub, tile_lane = iotas()
+    scale = -0.5 * dt_edge_ref[...]
+    beside = to_char(
+        char_mat,
+        [
+            scale * jnp.where(sub < 4, -west_ref[pl.ds(v * 8, 8), :], east_ref[pl.ds(v * 8, 8), :])
+            for v in range(5)
+        ],
+    )
+    outside = outer(sub, tile_lane)
+
+    def forward(i, carry):
+        one, two = carry
+        new = []
+        for n, s in enumerate(SYSTEM):
+            char = jnp.where(outside, roll(beside[n], (128 - i) % 128, 1), 0.0)
+            value = scalars[s * 5 + 2, i] * char - scalars[s * 5 + 1, i] * two[n] - scalars[s * 5, i] * one[n]
+            sweep_ref[n, layer_at(i), :] = value
+            f_ref[n, layer_at(i), :] = f_in[n, layer_at(i), :] + value
+            new.append(value)
+        return new, one
+
+    backward = swept_back(cells, sweep_ref, scalars)
+    blank = jnp.zeros(TILE, F32)
     zero = jnp.zeros((1, 128), F32)
 
     def take(ref, n, tile, t):
@@ -362,7 +347,10 @@
 
     inflow = [(zero, zero), (zero, zero)]
     sums = []
+    last = ([blank] * 5, [blank] * 5)
     for t in range(count):
+        for i in range(t * cells // count, (t + 1) * cells // count):
+            last = forward(i, last)
         row = []
         for tile in range(2):
             one, two = inflow[tile]
@@ -381,7 +369,10 @@
             row.append((made[2], made[3]))
         sums.append(row)
     inflow = [(zero, zero), (zero, zero)]
+    first = ([blank] * 5, [blank] * 5)
     for t in reversed(range(count)):
+        for i in reversed(range(t * cells // count, (t + 1) * cells // count)):
+            first = backward(cells - 1 - i, first)
         for tile in range(2):
             one, two = inflow[tile]
             for k, value in ((2, one), (3, two)):
@@ -396,6 +387,14 @@
                 for k in (2, 3)
             )
     put(4, by_quarter(lane, [quarter_move(four_ref[k], 0, k) for k in range(4)]))
+    ends = last + first
+    for pair in range(2):
+        total = blank
+        for n in range(2):
+            for u in range(5):
+                value = jnp.sum(ends[pair * 2 + n][u], axis=1, keepdims=True)
+                total = jnp.where(tile_lane == n * 64 + u * 8 + sub, value, total)
+        put(10 + pair, jnp.broadcast_to(jnp.sum(total, axis=0, keepdims=True), (count, 128)))
 
 
 def edge_inflow(count, in_ref, coef_ref, edge_ref, flow_ref):
@@ -515,7 +514,7 @@
     ends, swept, padded, steps, coef, char_mat, cons_mat = pl.pallas_call(
         lambda *refs: own_kernel(cells, *refs),
         out_shape=(
-            kept(count * OUT, 128),
+            shaped(count * OUT, 128),
             kept(*block),
             kept(5, (cells + 4) * 8, 128),
             kept(cells * 8, 128),
@@ -548,26 +547,19 @@
     right = [(i, i + 1) for i in range(columns - 1)]
     west = near(lax.ppermute(edge, "cross", right))
     east = near(lax.ppermute(edge, "cross", [(j, i) for i, j in right]))
-    swept, row = pl.pallas_call(
-        lambda *refs: beside_kernel(cells, *refs),
-        out_shape=(kept(*block), kept(*TILE)),
-        in_specs=[VMEM] * 4 + [SMEM] * 2,
-        out_specs=(VMEM, VMEM),
-        scratch_shapes=[pltpu.VMEM(block, F32)],
-        name="beside",
-    )(near(swept), near(step_edge), east, west, coef, char_mat)
-    inflow, edge_coef = pl.pallas_call(
-        lambda *refs: reduced_kernel(count, *refs),
-        out_shape=(kept(count * BACK, 128), kept(16, count, 128)),
-        in_specs=[VMEM] * 2,
-        out_specs=(VMEM, VMEM),
+    inflow, edge_coef, swept = pl.pallas_call(
+        lambda *refs: reduced_kernel(cells, count, *refs),
+        out_shape=(kept(count * BACK, 128), kept(16, count, 128), kept(*block)),
+        in_specs=[VMEM] * 5 + [SMEM] * 2,
+        out_specs=(VMEM,) * 3,
         scratch_shapes=[
             pltpu.VMEM((4, 2, count, 128), F32),
             pltpu.VMEM((16, 2, count, 128), F32),
             pltpu.VMEM((4, count, 128), F32),
+            pltpu.VMEM(block, F32),
         ],
         name="reduced",
-    )(near(ends), near(row))
+    )(near(ends), near(swept), near(step_edge), west, east, coef, char_mat)
     inflow = exchanged(inflow, count)
     result = pl.pallas_call(
         lambda *refs: final_kernel(cells, count, *refs),

time: 42 us -> 41.8 us (level)
    pallas_call x3 -> x2, Pallas kernels: 5.14 us -> 5 us  [the longest x1 3.71 us: on_device(): pl.pallas_call(lambda *refs: own_kernel(cells, *refs), out_shape=(shaped(...]
  transfers between devices with their start and end apart: 3 -> 3, of which waited for: 1 -> 1; matrix products, arithmetic and copies ran while one was open for 0% -> 0% of each run, Pallas kernels for 3% -> 1%
where the time goes in v7:
time: 41.8 us; the launch traced here: 41.5 us
  blocking collectives  16.9 us (40%)
  starting transfers between devices  13.5 us (32%)
  Pallas kernels  7.27 us (17%)
  waiting for transfers between devices  3.8 us (9%)
    all_to_all x1, blocking collectives, exchanged(): return lax.all_to_all(chunks, 'sec', 0, 0, tiled=True).reshape(x.shape)  16.9 us
    all_to_all x1, starting transfers between devices, exchanged(): return lax.all_to_all(chunks, 'sec', 0, 0, tiled=True).reshape(x.shape)  7.77 us
    ppermute x1, starting transfers between devices, on_device(): east = near(lax.ppermute(edge, 'cross', [(j, i) for i, j in right]))  3.85 us
    ppermute x1, waiting for transfers between devices, on_device(): west = near(lax.ppermute(edge, 'cross', right))  3.8 us
    pallas_call x1, Pallas kernels, on_device(): pl.pallas_call(lambda *refs: own_kernel(cells, *refs), out_shape=(shaped(...  3.71 us
    ppermute x1, starting transfers between devices, on_device(): west = near(lax.ppermute(edge, 'cross', right))  1.92 us
    pallas_call x1, Pallas kernels, on_device(): pl.pallas_call(lambda *refs: final_kernel(cells, count, *refs), out_shape...  1.84 us
    pallas_call x1, Pallas kernels, on_device(): pl.pallas_call(lambda *refs: reduced_kernel(cells, count, *refs), out_sha...  1.29 us
  transfers between devices with their start and end apart: 3, of which 1 were waited for; matrix products, arithmetic and copies ran while one was open for 0% of the time, Pallas kernels for 1%

profile of v7, /device:TPU:385, one launch (start us, length us, event | category | flops | bytes accessed | tf_op | source)
XLA Modules:
  0.0 41.5 jit_solution(18280081720496153919)
XLA Ops:
  0.0 3.7 %own.1 = (f32[384,128]{1,0:T(8,128)}, f32[5,256,128]{2,1,0:T(8,128)S(1)}, f32[5,288,128]{2,1,0:T(8,128)S(1)}, f32[256,128]{1,0:T(8,128)S(1)}, f32[16,128]{1,0:T(...) custom-call(f32[5,256,128]{2,1,0:T(8,128)} %bitcast.22, f32[256,128]{1,0:T(8,128)} %bitcast.24, f32[3,3,32]{2,1,0:T(4,128)} %refs_2_.1, ...), custom_call_target="tpu_custom_call" | custom-call | tf_op jit(solution)/shard_map/own/pallas_call | solution.py:514
  3.7 7.8 %all-to-all-start = ((f32[32,1,1536]{2,1,0:T(1,128)}), f32[32,1,1536]{2,1,0:T(1,128)S(1)}, u32[]{:S(2)}, u32[]{:S(2)}) async-start(f32[32,1,1536]{2,1,0:T(1,128)} %bitcast.23), calls=%async_computation | async-start | bytes 393216 | tf_op jit(solution)/shard_map/all_to_all | solution.py:495
  11.5 0.4 %edges.1 = (f32[40,128]{1,0:T(8,128)S(1)}, f32[8,128]{1,0:T(8,128)S(1)}) custom-call(f32[5,288,128]{2,1,0:T(8,128)S(1)} %get-tuple-element.19.refs_0_, f32[256,128]{1,0:T(8,128)S(1)} %get-tuple-element.20.refs_1_), custom_call_target="tpu_custom_call" | custom-call | tf_op jit(solution)/shard_map/edges/pallas_call | solution.py:540
  11.9 3.8 %collective-permute-start.1 = (f32[40,128]{1,0:T(8,128)S(1)}, f32[40,128]{1,0:T(8,128)S(1)}, u32[]{:S(2)}, u32[]{:S(2)}) collective-permute-start(f32[40,128]{1,0:T(8,128)S(1)} %get-tuple-element.22), channel_id=1, source_target_pairs={{1,0},{2,1},{3,2},{4,3},{5,4},{6,5},{7,6},{8,7},{9,8},{10,9},{11,1... | collective-permute-start | bytes 61448 | tf_op jit(solution)/shard_map/ppermute | solution.py:549
  15.8 1.9 %collective-permute-start = (f32[40,128]{1,0:T(8,128)S(1)}, f32[40,128]{1,0:T(8,128)S(1)}, u32[]{:S(2)}, u32[]{:S(2)}) collective-permute-start(f32[40,128]{1,0:T(8,128)S(1)} %get-tuple-element.22), channel_id=1, source_target_pairs={{0,1},{1,2},{2,3},{3,4},{4,5},{5,6},{6,7},{7,8},{8,9},{9,10},{10,1... | collective-permute-start | bytes 61448 | tf_op jit(solution)/shard_map/ppermute | solution.py:548
  17.7 0.0 collective-permute-done.1.refs_4_
  17.7 3.8 %collective-permute-done.refs_3_ = f32[40,128]{1,0:T(8,128)S(1)} collective-permute-done((f32[40,128]{1,0:T(8,128)S(1)}, f32[40,128]{1,0:T(8,128)S(1)}, u32[]{:S(2)}, u32[]{:S(2)}) %collective-permute-start) | collective-permute-done | bytes 20512 | tf_op jit(solution)/shard_map/ppermute | solution.py:548
  21.5 0.0 all-to-all-done
  21.5 1.3 %reduced.1 = (f32[384,128]{1,0:T(8,128)S(1)}, f32[16,32,128]{2,1,0:T(8,128)S(1)}, f32[5,256,128]{2,1,0:T(8,128)S(1)}) custom-call(f32[384,128]{1,0:T(8,128)S(1)} %bitcast.19, f32[5,256,128]{2,1,0:T(8,128)S(1)} %get-tuple-element.18.refs_1_, f32[8,128]{1,0:T(8,128)S(1)} %get-tuple-element.21.refs_2_, f32[40,128]{1,0:T(8,128)S(1)} %collective-permute-done.refs_3_, ...), custom_call_target="tpu_custom_call" | custom-call | tf_op jit(solution)/shard_map/reduced/pallas_call | solution.py:550
  22.8 16.9 %all_to_all.10 = f32[32,1,1536]{2,1,0:T(1,128)S(1)} all-to-all(f32[32,1,1536]{2,1,0:T(1,128)S(1)} %bitcast.21), channel_id=1, replica_groups=mesh['sec'=32,'cross'=16] {'sec'}, dimensions={0} | all-to-all | bytes 393216 | tf_op jit(solution)/shard_map/all_to_all | solution.py:495
  39.7 1.8 %final.1 = f32[5,256,128]{2,1,0:T(8,128)} custom-call(f32[5,256,128]{2,1,0:T(8,128)S(1)} %get-tuple-element.25.refs_0_, f32[384,128]{1,0:T(8,128)S(1)} %bitcast.20, f32[16,32,128]{2,1,0:T(8,128)S(1)} %get-tuple-element.27.refs_2_, f32[16,128]{1,0:T(8,128)S(4)} %get-tuple-element.23.refs_5_.refs_3_, f32[5,5]{1,0:T(8,128)S(4)} %get-tuple-element.28.refs_4_), custom_call_target="tpu_custom_call" | custom-call | tf_op jit(solution)/shard_map/final/pallas_call | solution.py:564
Async XLA Ops:
  3.7 17.8 %all-to-all-start = ((f32[32,1,1536]{2,1,0:T(1,128)}), f32[32,1,1536]{2,1,0:T(1,128)S(1)}, u32[]{:S(2)}, u32[]{:S(2)}) async-start(f32[32,1,1536]{2,1,0:T(1,128)} %bitcast.23), calls=%async_computation | async-start | bytes 393216 | tf_op jit(solution)/shard_map/all_to_all | solution.py:495
  11.9 5.8 %collective-permute-start.1 = (f32[40,128]{1,0:T(8,128)S(1)}, f32[40,128]{1,0:T(8,128)S(1)}, u32[]{:S(2)}, u32[]{:S(2)}) collective-permute-start(f32[40,128]{1,0:T(8,128)S(1)} %get-tuple-element.22), channel_id=1, source_target_pairs={{1,0},{2,1},{3,2},{4,3},{5,4},{6,5},{7,6},{8,7},{9,8},{10,9},{11,1... | collective-permute-start | bytes 61448 | tf_op jit(solution)/shard_map/ppermute | solution.py:549
  15.8 5.7 %collective-permute-start = (f32[40,128]{1,0:T(8,128)S(1)}, f32[40,128]{1,0:T(8,128)S(1)}, u32[]{:S(2)}, u32[]{:S(2)}) collective-permute-start(f32[40,128]{1,0:T(8,128)S(1)} %get-tuple-element.22), channel_id=1, source_target_pairs={{0,1},{1,2},{2,3},{3,4},{4,5},{5,6},{6,7},{7,8},{8,9},{9,10},{10,1... | collective-permute-start | bytes 61448 | tf_op jit(solution)/shard_map/ppermute | solution.py:548

commit v8 on v7

--- a/solution.py
+++ b/solution.py
@@ -58,7 +58,7 @@
     return total
 
 
-def edges_kernel(cells, x_ref, dt_ref, edge_ref, dt_edge_ref):
+def edges_kernel(cells, x_ref, dt_ref, east_ref, west_ref, dt_edge_ref):
     sub, _ = iotas()
     packed = []
     for v in range(5):
@@ -66,9 +66,17 @@
         total = roll(total, 4, 0)
         packed.append(jnp.where(sub < 4, roll(total, 1, 1), roll(total, 127, 1)))
     inv, pressure = primitives(packed)
-    for v, part in enumerate(flux(packed, inv, pressure, 1)):
-        edge_ref[pl.ds(v * 8, 8), :] = part
+    parts = flux(packed, inv, pressure, 1)
+    for n in range(3):
+        one, two = parts[2 * n], parts[min(2 * n + 1, 4)]
+        east_ref[pl.ds(n * 8, 8), :] = jnp.where(sub < 4, one, roll(two, 4, 0))
+        west_ref[pl.ds(n * 8, 8), :] = jnp.where(sub < 4, roll(two, 4, 0), one)
     dt_edge_ref[...] = packed_edges(cells, lambda i: dt_ref[pl.ds(i * 8, 8), :])
+
+
+def halved(ref, v):
+    pair = ref[pl.ds(v // 2 * 8, 8), :]
+    return roll(pair, 4, 0) if v % 2 else pair
 
 
 def layer_at(i):
@@ -266,7 +274,7 @@
 
 
 def reduced_kernel(
-    cells, count, in_ref, f_in, dt_edge_ref, west_ref, east_ref, scalars, char_mat,
+    cells, count, in_ref, f_in, dt_edge_ref, east_ref, west_ref, scalars, char_mat,
     out_ref, edge_coef_ref, f_ref, part_ref, coef_ref, four_ref, sweep_ref,
 ):
     lane = lax.broadcasted_iota(jnp.int32, (count, 128), 1)
@@ -321,7 +329,7 @@
     beside = to_char(
         char_mat,
         [
-            scale * jnp.where(sub < 4, -west_ref[pl.ds(v * 8, 8), :], east_ref[pl.ds(v * 8, 8), :])
+            scale * jnp.where(sub < 4, -halved(west_ref, v), halved(east_ref, v))
             for v in range(5)
         ],
     )
@@ -537,16 +545,16 @@
     )(flat, steps, lower_bands, upper_bands, to_char, to_cons)
     coef, char_mat, cons_mat = near_scalars(coef), near_scalars(char_mat), near_scalars(cons_mat)
     ends = exchanged(ends, count)
-    edge, step_edge = pl.pallas_call(
+    to_east, to_west, step_edge = pl.pallas_call(
         lambda *refs: edges_kernel(cells, *refs),
-        out_shape=(kept(40, 128), kept(*TILE)),
+        out_shape=(kept(24, 128), kept(24, 128), kept(*TILE)),
         in_specs=[VMEM] * 2,
-        out_specs=(VMEM, VMEM),
+        out_specs=(VMEM,) * 3,
         name="edges",
     )(near(padded), near(steps))
     right = [(i, i + 1) for i in range(columns - 1)]
-    west = near(lax.ppermute(edge, "cross", right))
-    east = near(lax.ppermute(edge, "cross", [(j, i) for i, j in right]))
+    west = near(lax.ppermute(to_east, "cross", right))
+    east = near(lax.ppermute(to_west, "cross", [(j, i) for i, j in right]))
     inflow, edge_coef, swept = pl.pallas_call(
         lambda *refs: reduced_kernel(cells, count, *refs),
         out_shape=(kept(count * BACK, 128), kept(16, count, 128), kept(*block)),
@@ -559,7 +567,7 @@
             pltpu.VMEM(block, F32),
         ],
         name="reduced",
-    )(near(ends), near(swept), near(step_edge), west, east, coef, char_mat)
+    )(near(ends), near(swept), near(step_edge), east, west, coef, char_mat)
     inflow = exchanged(inflow, count)
     result = pl.pallas_call(
         lambda *refs: final_kernel(cells, count, *refs),

time: 41.8 us -> 41.8 us (level)
  no operation moved by 1% of the time
where the time goes in v8:
time: 41.8 us; the launch traced here: 41.5 us
  blocking collectives  16.9 us (40%)
  starting transfers between devices  13.5 us (32%)
  Pallas kernels  7.32 us (18%)
  waiting for transfers between devices  3.72 us (9%)
    all_to_all x1, blocking collectives, exchanged(): return lax.all_to_all(chunks, 'sec', 0, 0, tiled=True).reshape(x.shape)  16.9 us
    all_to_all x1, starting transfers between devices, exchanged(): return lax.all_to_all(chunks, 'sec', 0, 0, tiled=True).reshape(x.shape)  7.77 us
    ppermute x1, starting transfers between devices, on_device(): east = near(lax.ppermute(to_west, 'cross', [(j, i) for i, j in right]))  3.85 us
    pallas_call x1, Pallas kernels, on_device(): pl.pallas_call(lambda *refs: own_kernel(cells, *refs), out_shape=(shaped(...  3.72 us
    ppermute x1, waiting for transfers between devices, on_device(): west = near(lax.ppermute(to_east, 'cross', right))  3.71 us
    ppermute x1, starting transfers between devices, on_device(): west = near(lax.ppermute(to_east, 'cross', right))  1.92 us
    pallas_call x1, Pallas kernels, on_device(): pl.pallas_call(lambda *refs: final_kernel(cells, count, *refs), out_shape...  1.88 us
    pallas_call x1, Pallas kernels, on_device(): pl.pallas_call(lambda *refs: reduced_kernel(cells, count, *refs), out_sha...  1.29 us
  transfers between devices with their start and end apart: 3, of which 1 were waited for; matrix products, arithmetic and copies ran while one was open for 0% of the time, Pallas kernels for 1%

profile of v8, /device:TPU:385, one launch (start us, length us, event | category | flops | bytes accessed | tf_op | source)
XLA Modules:
  0.0 41.5 jit_solution(17617011864955041718)
XLA Ops:
  0.0 3.7 %own.1 = (f32[384,128]{1,0:T(8,128)}, f32[5,256,128]{2,1,0:T(8,128)S(1)}, f32[5,288,128]{2,1,0:T(8,128)S(1)}, f32[256,128]{1,0:T(8,128)S(1)}, f32[16,128]{1,0:T(...) custom-call(f32[5,256,128]{2,1,0:T(8,128)} %bitcast.22, f32[256,128]{1,0:T(8,128)} %bitcast.24, f32[3,3,32]{2,1,0:T(4,128)} %refs_2_.1, ...), custom_call_target="tpu_custom_call" | custom-call | tf_op jit(solution)/shard_map/own/pallas_call | solution.py:522
  3.7 7.8 %all-to-all-start = ((f32[32,1,1536]{2,1,0:T(1,128)}), f32[32,1,1536]{2,1,0:T(1,128)S(1)}, u32[]{:S(2)}, u32[]{:S(2)}) async-start(f32[32,1,1536]{2,1,0:T(1,128)} %bitcast.23), calls=%async_computation | async-start | bytes 393216 | tf_op jit(solution)/shard_map/all_to_all | solution.py:503
  11.5 0.4 %edges.1 = (f32[24,128]{1,0:T(8,128)S(1)}, f32[24,128]{1,0:T(8,128)S(1)}, f32[8,128]{1,0:T(8,128)S(1)}) custom-call(f32[5,288,128]{2,1,0:T(8,128)S(1)} %get-tuple-element.20.refs_0_, f32[256,128]{1,0:T(8,128)S(1)} %get-tuple-element.21.refs_1_), custom_call_target="tpu_custom_call" | custom-call | tf_op jit(solution)/shard_map/edges/pallas_call | solution.py:548
  11.9 3.8 %collective-permute-start = (f32[24,128]{1,0:T(8,128)S(1)}, f32[24,128]{1,0:T(8,128)S(1)}, u32[]{:S(2)}, u32[]{:S(2)}) collective-permute-start(f32[24,128]{1,0:T(8,128)S(1)} %get-tuple-element.23), channel_id=1, source_target_pairs={{1,0},{2,1},{3,2},{4,3},{5,4},{6,5},{7,6},{8,7},{9,8},{10,9},{11,1... | collective-permute-start | bytes 36872 | tf_op jit(solution)/shard_map/ppermute | solution.py:557
  15.8 1.9 %collective-permute-start.1 = (f32[24,128]{1,0:T(8,128)S(1)}, f32[24,128]{1,0:T(8,128)S(1)}, u32[]{:S(2)}, u32[]{:S(2)}) collective-permute-start(f32[24,128]{1,0:T(8,128)S(1)} %get-tuple-element.24), channel_id=1, source_target_pairs={{0,1},{1,2},{2,3},{3,4},{4,5},{5,6},{6,7},{7,8},{8,9},{9,10},{10,1... | collective-permute-start | bytes 36872 | tf_op jit(solution)/shard_map/ppermute | solution.py:556
  17.7 0.0 collective-permute-done.refs_3_
  17.7 3.7 %collective-permute-done.1.refs_4_ = f32[24,128]{1,0:T(8,128)S(1)} collective-permute-done((f32[24,128]{1,0:T(8,128)S(1)}, f32[24,128]{1,0:T(8,128)S(1)}, u32[]{:S(2)}, u32[]{:S(2)}) %collective-permute-start.1) | collective-permute-done | bytes 12320 | tf_op jit(solution)/shard_map/ppermute | solution.py:556
  21.5 0.0 all-to-all-done
  21.5 1.3 %reduced.1 = (f32[384,128]{1,0:T(8,128)S(1)}, f32[16,32,128]{2,1,0:T(8,128)S(1)}, f32[5,256,128]{2,1,0:T(8,128)S(1)}) custom-call(f32[384,128]{1,0:T(8,128)S(1)} %bitcast.19, f32[5,256,128]{2,1,0:T(8,128)S(1)} %get-tuple-element.19.refs_1_, f32[8,128]{1,0:T(8,128)S(1)} %get-tuple-element.22.refs_2_, f32[24,128]{1,0:T(8,128)S(1)} %collective-permute-done.refs_3_, ...), custom_call_target="tpu_custom_call" | custom-call | tf_op jit(solution)/shard_map/reduced/pallas_call | solution.py:558
  22.7 16.9 %all_to_all.10 = f32[32,1,1536]{2,1,0:T(1,128)S(1)} all-to-all(f32[32,1,1536]{2,1,0:T(1,128)S(1)} %bitcast.21), channel_id=1, replica_groups=mesh['sec'=32,'cross'=16] {'sec'}, dimensions={0} | all-to-all | bytes 393216 | tf_op jit(solution)/shard_map/all_to_all | solution.py:503
  39.6 1.9 %final.1 = f32[5,256,128]{2,1,0:T(8,128)} custom-call(f32[5,256,128]{2,1,0:T(8,128)S(1)} %get-tuple-element.27.refs_0_, f32[384,128]{1,0:T(8,128)S(1)} %bitcast.20, f32[16,32,128]{2,1,0:T(8,128)S(1)} %get-tuple-element.29.refs_2_, f32[16,128]{1,0:T(8,128)S(4)} %get-tuple-element.25.refs_5_.refs_3_, f32[5,5]{1,0:T(8,128)S(4)} %get-tuple-element.30.refs_4_), custom_call_target="tpu_custom_call" | custom-call | tf_op jit(solution)/shard_map/final/pallas_call | solution.py:572
Async XLA Ops:
  3.7 17.7 %all-to-all-start = ((f32[32,1,1536]{2,1,0:T(1,128)}), f32[32,1,1536]{2,1,0:T(1,128)S(1)}, u32[]{:S(2)}, u32[]{:S(2)}) async-start(f32[32,1,1536]{2,1,0:T(1,128)} %bitcast.23), calls=%async_computation | async-start | bytes 393216 | tf_op jit(solution)/shard_map/all_to_all | solution.py:503
  11.9 5.8 %collective-permute-start = (f32[24,128]{1,0:T(8,128)S(1)}, f32[24,128]{1,0:T(8,128)S(1)}, u32[]{:S(2)}, u32[]{:S(2)}) collective-permute-start(f32[24,128]{1,0:T(8,128)S(1)} %get-tuple-element.23), channel_id=1, source_target_pairs={{1,0},{2,1},{3,2},{4,3},{5,4},{6,5},{7,6},{8,7},{9,8},{10,9},{11,1... | collective-permute-start | bytes 36872 | tf_op jit(solution)/shard_map/ppermute | solution.py:557
  15.8 5.7 %collective-permute-start.1 = (f32[24,128]{1,0:T(8,128)S(1)}, f32[24,128]{1,0:T(8,128)S(1)}, u32[]{:S(2)}, u32[]{:S(2)}) collective-permute-start(f32[24,128]{1,0:T(8,128)S(1)} %get-tuple-element.24), channel_id=1, source_target_pairs={{0,1},{1,2},{2,3},{3,4},{4,5},{5,6},{6,7},{7,8},{8,9},{9,10},{10,1... | collective-permute-start | bytes 36872 | tf_op jit(solution)/shard_map/ppermute | solution.py:556
